TPU v7x, 256 devices: a whole 4x4x8 slice. The times are simulated.
256 devices in a mesh: grp: 2 (over z_lo), gy: 8 (over z_hi, core), gz: 16 (over y, x).
Axes of the slice: x: 4, y: 4, z: 8 (z_hi: 4, z_lo: 2; z = z_hi * 2 + z_lo), core: 2. Of those that a mesh axis runs over, the one named last changes fastest.
Arguments:
- field_pairs: float32 [2, 2, 384, 256, 128], P('grp', None, 'gy', 'gz'), may hold values from -6 to 6
- tile_owner: int32 [2, 48, 16, 1], replicated, may hold values from 0 to 511
- electrode_volts: float32 [512], P(('grp', 'gy', 'gz')), may hold values from -6 to 6
Outputs:
- advanced: float32 [2, 2, 384, 256, 128], P('grp', None, 'gy', 'gz')
- electrode_grad: float32 [512], P(('grp', 'gy', 'gz'))
Inputs may be any that keep to these rules, and one draw needn't show every extreme that they name: `tile_owner`: electrode numbers; every electrode owns at least one wall tile.
All inputs are finite; a program needn't handle non-finite values.
Results may differ from a plain program's by a relative error of at most 0.00011.
Values sent between devices are 32-bit elements; how exact they have to be, the bound alone decides.
No kernel may reach another device: no remote copies, remote signals or barrier semaphores. Data moves between devices by JAX's collectives and lax.ppermute only.
A program may use at most 64 MiB of HBM per device.

v0:
```python
import jax
import jax.numpy as jnp
from jax import lax
from jax.sharding import PartitionSpec as P

STEPS = 2
SWEEPS = 2
TILE_Y = 8
TILE_X = 8


self_weight = 0.35
diffusion = 0.1
induction = 0.5
coupling = 0.5


def padded_2(array, sides, width):
    for axis, dim in sides:
        count, length = (lax.axis_size(axis), array.shape[dim])
        up = [(i, (i + 1) % count) for i in range(count - 1)]
        down = [(j, i) for i, j in up]
        last = lax.slice_in_dim(array, length - width, length, axis=dim)
        initial = lax.slice_in_dim(array, 0, width, axis=dim)
        before = lax.ppermute(last, axis, up)
        after = lax.ppermute(initial, axis, down)
        array = jnp.concatenate([before, array, after], axis=dim)
    return array


def passed_along(array, axis, by):
    count = lax.axis_size(axis)
    pairs = [(i, i + by) for i in range(count) if 0 <= i + by < count]
    return lax.ppermute(array, axis, pairs)


def neighbour_sum(padded):
    middle = padded[1:-1, 1:-1]
    total = padded[2:, 1:-1] + padded[:-2, 1:-1] + padded[1:-1, 2:] + padded[1:-1, :-2]
    return total + jnp.roll(middle, 1, 2) + jnp.roll(middle, -1, 2)


def span_diff(padded):
    return padded[1:-1, 2:] - padded[1:-1, :-2]


def faces(field):
    return padded_2(field, (("gy", 0), ("gz", 1)), 1)


def wall_ghost(wall_rows, first_col, count, span_total):
    columns = first_col + jnp.arange(count, dtype=jnp.int32)
    lower = (columns == 0)[None, :, None]
    upper = (columns == span_total - 1)[None, :, None]
    zeros = jnp.zeros((), jnp.float32)
    return jnp.where(lower, wall_rows[0][:, None, :], zeros) + jnp.where(
        upper, wall_rows[1][:, None, :], zeros
    )


def advance(velocity, potential, wall_pad, row_first, col_first, span_total):
    rows = velocity.shape[0]
    cols = velocity.shape[1]
    ghost = wall_ghost(
        lax.dynamic_slice_in_dim(wall_pad, row_first + SWEEPS, rows, 1), col_first, cols, span_total
    )
    states = []
    for step in range(STEPS):
        padded = faces(velocity)
        near_sum = neighbour_sum(padded)
        source = induction * span_diff(padded)
        for sweep in range(SWEEPS):
            potential = (neighbour_sum(faces(potential)) + ghost - source) / 6.0
        velocity = (
            self_weight * velocity + diffusion * near_sum + coupling * span_diff(faces(potential))
        )
        states.append(velocity)
    return (velocity, potential, states)


def retreat(adj_vel, adj_pot, sources, lower_wall, upper_wall):
    zeros = jnp.zeros((), jnp.float32)
    wall_grad = jnp.zeros((2, adj_vel.shape[0], adj_vel.shape[2]), jnp.float32)
    for step in reversed(range(STEPS)):
        adj_vel = adj_vel + sources[step]
        padded = faces(adj_vel)
        earlier = self_weight * adj_vel + diffusion * neighbour_sum(padded)
        spread = adj_pot - coupling * span_diff(padded)
        total = jnp.zeros_like(spread)
        for sweep in range(SWEEPS):
            total = total + spread / 6.0
            spread = neighbour_sum(faces(spread)) / 6.0
        earlier = earlier + induction * span_diff(faces(total))
        wall_grad = wall_grad + jnp.stack(
            [
                jnp.where(lower_wall, total[:, 0, :], zeros),
                jnp.where(upper_wall, total[:, -1, :], zeros),
            ]
        )
        adj_vel = earlier
        adj_pot = spread
    return (adj_vel, adj_pot, wall_grad)


def per_device(field_pairs, tile_owner, electrode_volts):
    is_forward = lax.axis_index("grp") == 0
    rows = field_pairs.shape[2]
    cols = field_pairs.shape[3]
    row_first = lax.axis_index("gy") * rows
    col_first = lax.axis_index("gz") * cols
    span_total = cols * lax.axis_size("gz")
    all_volts = lax.all_gather(electrode_volts, ("grp", "gy", "gz"), axis=0, tiled=True)
    electrodes = all_volts.shape[0]
    labels = tile_owner[..., 0]
    numbers = jnp.arange(electrodes, dtype=jnp.int32)[None, :]
    one_hot = (labels.reshape(-1, 1) == numbers).astype(jnp.float32)
    tile_volts = jnp.dot(one_hot, all_volts, precision=lax.Precision.HIGHEST).reshape(labels.shape)
    wall = jnp.repeat(jnp.repeat(tile_volts, TILE_Y, 1), TILE_X, 2)
    wall_pad = jnp.pad(wall, ((0, 0), (SWEEPS, SWEEPS), (0, 0)))
    own = field_pairs[0]
    velocity, potential, states = advance(
        own[0], own[1], wall_pad, row_first, col_first, span_total
    )
    sources = passed_along(jnp.stack(states), "grp", 1)
    adj_vel, adj_pot, wall_grad = retreat(
        own[0], own[1], sources, col_first == 0, col_first + cols == span_total
    )
    advanced = jnp.where(
        is_forward, jnp.stack([velocity, potential]), jnp.stack([adj_vel, adj_pot])
    )[None]
    tile_grad = wall_grad.reshape(
        2, rows // TILE_Y, TILE_Y, wall_grad.shape[2] // TILE_X, TILE_X
    ).sum(axis=(2, 4))
    local_labels = lax.dynamic_slice_in_dim(labels, row_first // TILE_Y, rows // TILE_Y, 1)
    local_hot = (local_labels.reshape(-1, 1) == numbers).astype(jnp.float32)
    per_electrode = jnp.dot(tile_grad.reshape(1, -1), local_hot, precision=lax.Precision.HIGHEST)[0]
    per_electrode = jnp.where(is_forward, jnp.zeros((), jnp.float32), per_electrode)
    electrode_grad = lax.psum_scatter(
        per_electrode, ("grp", "gy", "gz"), scatter_dimension=0, tiled=True
    )
    return (advanced, electrode_grad)


def solution(mesh):
    placed = (P("grp", None, "gy", "gz", None), P(), P(("grp", "gy", "gz")))
    return jax.shard_map(
        per_device,
        mesh=mesh,
        in_specs=placed,
        out_specs=(P("grp", None, "gy", "gz", None), P(("grp", "gy", "gz"))),
        check_vma=False,
    )
```

profile of v0, /device:TPU:32, one launch (start us, length us, event | category | flops | bytes accessed | tf_op | source)
XLA Modules:
  0.0 462.9 jit_solution(6725813879116356300)
XLA Ops:
  7.0 5.4 %collective-permute-start.5 = (f32[1,16,128]{2,1,0:T(8,128)S(1)}, f32[1,16,128]{2,1,0:T(8,128)S(1)}, u32[]{:S(2)}, u32[]{:S(2)}) collective-permute-start(f32[1,16,128]{2,1,0:T(8,128)S(1)} %get-tuple-element.12), channel_id=1, source_target_pairs={{0,16},{16,32},{32,48},{48,64},{64,80},{80,96},{96,112},{1,17},{17... | collective-permute-start | bytes 24584 | tf_op jit(solution)/shard_map/ppermute | solution.py:25
  14.6 82.0 %all-reduce.1 = f32[512]{0:T(512)S(1)} all-reduce(f32[512]{0:T(512)S(1)} %dynamic-update-slice), channel_id=1, replica_groups=mesh['grp'=2,'gy'=8,'gz'=16] {'grp','gy','gz'}, use_global_device_ids=true, to_apply=%add.1 | all-reduce | flops 512 | bytes 4096
  129.7 5.0 %collective-permute-done.13 = f32[1,16,128]{2,1,0:T(8,128)S(1)} collective-permute-done((f32[1,16,128]{2,1,0:T(8,128)S(1)}, f32[1,16,128]{2,1,0:T(8,128)S(1)}, u32[]{:S(2)}, u32[]{:S(2)}) %collective-permute-start.13) | collective-permute-done | bytes 8224 | tf_op jit(solution)/shard_map/ppermute | solution.py:26
  144.2 5.0 %collective-permute-start.17 = (f32[1,16,128]{2,1,0:T(8,128)S(1)}, f32[1,16,128]{2,1,0:T(8,128)S(1)}, u32[]{:S(2)}, u32[]{:S(2)}) collective-permute-start(f32[1,16,128]{2,1,0:T(8,128)S(1)} %get-tuple-element.98), channel_id=1, source_target_pairs={{0,16},{16,32},{32,48},{48,64},{64,80},{80,96},{96,112},{1,17},{17... | collective-permute-start | bytes 24584 | tf_op jit(solution)/shard_map/ppermute | solution.py:25
  165.6 6.7 %collective-permute-start.23 = (f32[50,1,128]{2,1,0:T(1,128)S(1)}, f32[50,1,128]{2,1,0:T(1,128)S(1)}, u32[]{:S(2)}, u32[]{:S(2)}) collective-permute-start(f32[50,1,128]{2,1,0:T(1,128)S(1)} %get-tuple-element.35), channel_id=1, source_target_pairs={{0,1},{1,2},{2,3},{3,4},{4,5},{5,6},{6,7},{7,8},{8,9},{9,10},{10,1... | collective-permute-start | bytes 76808 | tf_op jit(solution)/shard_map/ppermute | solution.py:25
  174.4 5.1 %collective-permute-start.24 = (f32[1,16,128]{2,1,0:T(8,128)S(1)}, f32[1,16,128]{2,1,0:T(8,128)S(1)}, u32[]{:S(2)}, u32[]{:S(2)}) collective-permute-start(f32[1,16,128]{2,1,0:T(8,128)S(1)} %get-tuple-element.90), channel_id=1, source_target_pairs={{0,16},{16,32},{32,48},{48,64},{64,80},{80,96},{96,112},{1,17},{17... | collective-permute-start | bytes 24584 | tf_op jit(solution)/shard_map/ppermute | solution.py:25
  180.9 5.1 %collective-permute-done.25 = f32[1,16,128]{2,1,0:T(8,128)S(1)} collective-permute-done((f32[1,16,128]{2,1,0:T(8,128)S(1)}, f32[1,16,128]{2,1,0:T(8,128)S(1)}, u32[]{:S(2)}, u32[]{:S(2)}) %collective-permute-start.25) | collective-permute-done | bytes 8224 | tf_op jit(solution)/shard_map/ppermute | solution.py:26
  187.4 7.0 %collective-permute-start.27 = (f32[50,1,128]{2,1,0:T(1,128)S(1)}, f32[50,1,128]{2,1,0:T(1,128)S(1)}, u32[]{:S(2)}, u32[]{:S(2)}) collective-permute-start(f32[50,1,128]{2,1,0:T(1,128)S(1)} %get-tuple-element.33), channel_id=1, source_target_pairs={{0,1},{1,2},{2,3},{3,4},{4,5},{5,6},{6,7},{7,8},{8,9},{9,10},{10,1... | collective-permute-start | bytes 76808 | tf_op jit(solution)/shard_map/ppermute | solution.py:25
  198.7 17.6 %collective-permute-done.28 = f32[2,48,16,128]{3,2,1,0:T(8,128)S(1)} collective-permute-done((f32[2,48,16,128]{3,2,1,0:T(8,128)S(1)}, f32[2,48,16,128]{3,2,1,0:T(8,128)S(1)}, u32[]{:S(2)}, u32[]{:S(2)}) %collective-permute-start.28) | collective-permute-done | bytes 786464 | tf_op jit(solution)/shard_map/ppermute | solution.py:34
  217.7 4.9 %collective-permute-start.30 = (f32[1,16,128]{2,1,0:T(8,128)S(1)}, f32[1,16,128]{2,1,0:T(8,128)S(1)}, u32[]{:S(2)}, u32[]{:S(2)}) collective-permute-start(f32[1,16,128]{2,1,0:T(8,128)S(1)} %get-tuple-element.84), channel_id=1, source_target_pairs={{0,16},{16,32},{32,48},{48,64},{64,80},{80,96},{96,112},{1,17},{17... | collective-permute-start | bytes 24584 | tf_op jit(solution)/shard_map/ppermute | solution.py:25
  224.8 6.7 %collective-permute-start.32 = (f32[50,1,128]{2,1,0:T(1,128)S(1)}, f32[50,1,128]{2,1,0:T(1,128)S(1)}, u32[]{:S(2)}, u32[]{:S(2)}) collective-permute-start(f32[50,1,128]{2,1,0:T(1,128)S(1)} %get-tuple-element.30), channel_id=1, source_target_pairs={{0,1},{1,2},{2,3},{3,4},{4,5},{5,6},{6,7},{7,8},{8,9},{9,10},{10,1... | collective-permute-start | bytes 76808 | tf_op jit(solution)/shard_map/ppermute | solution.py:25
  234.4 8.0 %collective-permute-start.34 = (f32[1,16,128]{2,1,0:T(8,128)S(1)}, f32[1,16,128]{2,1,0:T(8,128)S(1)}, u32[]{:S(2)}, u32[]{:S(2)}) collective-permute-start(f32[1,16,128]{2,1,0:T(8,128)S(1)} %get-tuple-element.78), channel_id=1, source_target_pairs={{0,16},{16,32},{32,48},{48,64},{64,80},{80,96},{96,112},{1,17},{17... | collective-permute-start | bytes 24584 | tf_op jit(solution)/shard_map/ppermute | solution.py:25
  244.5 7.0 %collective-permute-start.36 = (f32[50,1,128]{2,1,0:T(1,128)S(1)}, f32[50,1,128]{2,1,0:T(1,128)S(1)}, u32[]{:S(2)}, u32[]{:S(2)}) collective-permute-start(f32[50,1,128]{2,1,0:T(1,128)S(1)} %get-tuple-element.29), channel_id=1, source_target_pairs={{0,1},{1,2},{2,3},{3,4},{4,5},{5,6},{6,7},{7,8},{8,9},{9,10},{10,1... | collective-permute-start | bytes 76808 | tf_op jit(solution)/shard_map/ppermute | solution.py:25
  255.4 5.0 %collective-permute-start.37 = (f32[1,16,128]{2,1,0:T(8,128)S(1)}, f32[1,16,128]{2,1,0:T(8,128)S(1)}, u32[]{:S(2)}, u32[]{:S(2)}) collective-permute-start(f32[1,16,128]{2,1,0:T(8,128)S(1)} %get-tuple-element.70), channel_id=1, source_target_pairs={{0,16},{16,32},{32,48},{48,64},{64,80},{80,96},{96,112},{1,17},{17... | collective-permute-start | bytes 24584 | tf_op jit(solution)/shard_map/ppermute | solution.py:25
  263.0 7.4 %collective-permute-start.46 = (f32[1,16,128]{2,1,0:T(8,128)S(1)}, f32[1,16,128]{2,1,0:T(8,128)S(1)}, u32[]{:S(2)}, u32[]{:S(2)}) collective-permute-start(f32[1,16,128]{2,1,0:T(8,128)S(1)} %get-tuple-element.76), channel_id=1, source_target_pairs={{0,16},{16,32},{32,48},{48,64},{64,80},{80,96},{96,112},{1,17},{17... | collective-permute-start | bytes 24584 | tf_op jit(solution)/shard_map/ppermute | solution.py:25
  274.0 7.0 %collective-permute-start.40 = (f32[50,1,128]{2,1,0:T(1,128)S(1)}, f32[50,1,128]{2,1,0:T(1,128)S(1)}, u32[]{:S(2)}, u32[]{:S(2)}) collective-permute-start(f32[50,1,128]{2,1,0:T(1,128)S(1)} %get-tuple-element.25), channel_id=1, source_target_pairs={{0,1},{1,2},{2,3},{3,4},{4,5},{5,6},{6,7},{7,8},{8,9},{9,10},{10,1... | collective-permute-start | bytes 76808 | tf_op jit(solution)/shard_map/ppermute | solution.py:25
  282.4 7.2 %collective-permute-start.48 = (f32[50,1,128]{2,1,0:T(1,128)S(1)}, f32[50,1,128]{2,1,0:T(1,128)S(1)}, u32[]{:S(2)}, u32[]{:S(2)}) collective-permute-start(f32[50,1,128]{2,1,0:T(1,128)S(1)} %get-tuple-element.27), channel_id=1, source_target_pairs={{0,1},{1,2},{2,3},{3,4},{4,5},{5,6},{6,7},{7,8},{8,9},{9,10},{10,1... | collective-permute-start | bytes 76808 | tf_op jit(solution)/shard_map/ppermute | solution.py:25
  292.5 5.3 %collective-permute-start.42 = (f32[1,16,128]{2,1,0:T(8,128)S(1)}, f32[1,16,128]{2,1,0:T(8,128)S(1)}, u32[]{:S(2)}, u32[]{:S(2)}) collective-permute-start(f32[1,16,128]{2,1,0:T(8,128)S(1)} %get-tuple-element.64), channel_id=1, source_target_pairs={{0,16},{16,32},{32,48},{48,64},{64,80},{80,96},{96,112},{1,17},{17... | collective-permute-start | bytes 24584 | tf_op jit(solution)/shard_map/ppermute | solution.py:25
  300.2 7.1 %collective-permute-start.44 = (f32[50,1,128]{2,1,0:T(1,128)S(1)}, f32[50,1,128]{2,1,0:T(1,128)S(1)}, u32[]{:S(2)}, u32[]{:S(2)}) collective-permute-start(f32[50,1,128]{2,1,0:T(1,128)S(1)} %get-tuple-element.22), channel_id=1, source_target_pairs={{0,1},{1,2},{2,3},{3,4},{4,5},{5,6},{6,7},{7,8},{8,9},{9,10},{10,1... | collective-permute-start | bytes 76808 | tf_op jit(solution)/shard_map/ppermute | solution.py:25
  310.7 7.6 %collective-permute-start.50 = (f32[1,16,128]{2,1,0:T(8,128)S(1)}, f32[1,16,128]{2,1,0:T(8,128)S(1)}, u32[]{:S(2)}, u32[]{:S(2)}) collective-permute-start(f32[1,16,128]{2,1,0:T(8,128)S(1)} %get-tuple-element.58), channel_id=1, source_target_pairs={{0,16},{16,32},{32,48},{48,64},{64,80},{80,96},{96,112},{1,17},{17... | collective-permute-start | bytes 24584 | tf_op jit(solution)/shard_map/ppermute | solution.py:25
  320.5 7.0 %collective-permute-start.52 = (f32[50,1,128]{2,1,0:T(1,128)S(1)}, f32[50,1,128]{2,1,0:T(1,128)S(1)}, u32[]{:S(2)}, u32[]{:S(2)}) collective-permute-start(f32[50,1,128]{2,1,0:T(1,128)S(1)} %get-tuple-element.21), channel_id=1, source_target_pairs={{0,1},{1,2},{2,3},{3,4},{4,5},{5,6},{6,7},{7,8},{8,9},{9,10},{10,1... | collective-permute-start | bytes 76808 | tf_op jit(solution)/shard_map/ppermute | solution.py:25
  336.2 5.0 %collective-permute-start.53 = (f32[1,16,128]{2,1,0:T(8,128)}, f32[1,16,128]{2,1,0:T(8,128)S(1)}, u32[]{:S(2)}, u32[]{:S(2)}) collective-permute-start(f32[1,16,128]{2,1,0:T(8,128)} %get-tuple-element.50), channel_id=1, source_target_pairs={{0,16},{16,32},{32,48},{48,64},{64,80},{80,96},{96,112},{1,17},{17... | collective-permute-start | bytes 24584 | tf_op jit(solution)/shard_map/ppermute | solution.py:25
  343.9 7.2 %collective-permute-start.58 = (f32[1,16,128]{2,1,0:T(8,128)}, f32[1,16,128]{2,1,0:T(8,128)S(1)}, u32[]{:S(2)}, u32[]{:S(2)}) collective-permute-start(f32[1,16,128]{2,1,0:T(8,128)} %get-tuple-element.56), channel_id=1, source_target_pairs={{0,16},{16,32},{32,48},{48,64},{64,80},{80,96},{96,112},{1,17},{17... | collective-permute-start | bytes 24584 | tf_op jit(solution)/shard_map/ppermute | solution.py:25
  352.0 95.3 %all-reduce.2 = f32[512]{0:T(512)S(1)} all-reduce(f32[512]{0:T(512)S(1)} %broadcast_select_fusion.4), channel_id=2, replica_groups=mesh['grp'=2,'gy'=8,'gz'=16] {'grp','gy','gz'}, use_global_device_ids=true, to_apply=%region_1.2.clone | all-reduce | flops 512 | bytes 4096
  (257 shorter events, 134.6 us)
Async XLA Ops:
  1.4 97.4 %collective-permute-start = (f32[1,16,128]{2,1,0:T(8,128)S(1)}, f32[1,16,128]{2,1,0:T(8,128)S(1)}, u32[]{:S(2)}, u32[]{:S(2)}) collective-permute-start(f32[1,16,128]{2,1,0:T(8,128)S(1)} %get-tuple-element.11), channel_id=1, source_target_pairs={{16,0},{32,16},{48,32},{64,48},{80,64},{96,80},{112,96},{17,1},{33... | collective-permute-start | bytes 24584 | tf_op jit(solution)/shard_map/ppermute | solution.py:26
  2.7 96.1 %collective-permute-start.1 = (f32[1,16,128]{2,1,0:T(8,128)S(1)}, f32[1,16,128]{2,1,0:T(8,128)S(1)}, u32[]{:S(2)}, u32[]{:S(2)}) collective-permute-start(f32[1,16,128]{2,1,0:T(8,128)S(1)} %get-tuple-element.10), channel_id=1, source_target_pairs={{0,16},{16,32},{32,48},{48,64},{64,80},{80,96},{96,112},{1,17},{17... | collective-permute-start | bytes 24584 | tf_op jit(solution)/shard_map/ppermute | solution.py:25
  5.7 99.0 %collective-permute-start.4 = (f32[1,16,128]{2,1,0:T(8,128)S(1)}, f32[1,16,128]{2,1,0:T(8,128)S(1)}, u32[]{:S(2)}, u32[]{:S(2)}) collective-permute-start(f32[1,16,128]{2,1,0:T(8,128)S(1)} %get-tuple-element.13), channel_id=1, source_target_pairs={{16,0},{32,16},{48,32},{64,48},{80,64},{96,80},{112,96},{17,1},{33... | collective-permute-start | bytes 24584 | tf_op jit(solution)/shard_map/ppermute | solution.py:26
  7.0 97.7 %collective-permute-start.5 = (f32[1,16,128]{2,1,0:T(8,128)S(1)}, f32[1,16,128]{2,1,0:T(8,128)S(1)}, u32[]{:S(2)}, u32[]{:S(2)}) collective-permute-start(f32[1,16,128]{2,1,0:T(8,128)S(1)} %get-tuple-element.12), channel_id=1, source_target_pairs={{0,16},{16,32},{32,48},{48,64},{64,80},{80,96},{96,112},{1,17},{17... | collective-permute-start | bytes 24584 | tf_op jit(solution)/shard_map/ppermute | solution.py:25
  98.8 11.9 %collective-permute-start.2 = (f32[50,1,128]{2,1,0:T(1,128)S(1)}, f32[50,1,128]{2,1,0:T(1,128)S(1)}, u32[]{:S(2)}, u32[]{:S(2)}) collective-permute-start(f32[50,1,128]{2,1,0:T(1,128)S(1)} %get-tuple-element.42), channel_id=1, source_target_pairs={{1,0},{2,1},{3,2},{4,3},{5,4},{6,5},{7,6},{8,7},{9,8},{10,9},{11,1... | collective-permute-start | bytes 76808 | tf_op jit(solution)/shard_map/ppermute | solution.py:26
  100.1 10.7 %collective-permute-start.3 = (f32[50,1,128]{2,1,0:T(1,128)S(1)}, f32[50,1,128]{2,1,0:T(1,128)S(1)}, u32[]{:S(2)}, u32[]{:S(2)}) collective-permute-start(f32[50,1,128]{2,1,0:T(1,128)S(1)} %get-tuple-element.43), channel_id=1, source_target_pairs={{0,1},{1,2},{2,3},{3,4},{4,5},{5,6},{6,7},{7,8},{8,9},{9,10},{10,1... | collective-permute-start | bytes 76808 | tf_op jit(solution)/shard_map/ppermute | solution.py:25
  196.4 19.9 %collective-permute-start.28 = (f32[2,48,16,128]{3,2,1,0:T(8,128)S(1)}, f32[2,48,16,128]{3,2,1,0:T(8,128)S(1)}, u32[]{:S(2)}, u32[]{:S(2)}) collective-permute-start(f32[2,48,16,128]{3,2,1,0:T(8,128)S(1)} %pad_maximum_fusion), channel_id=1, source_target_pairs={{0,128},{1,129},{2,130},{3,131},{4,132},{5,133},{6,134},{7,135},{8... | collective-permute-start | bytes 2359304 | tf_op jit(solution)/shard_map/ppermute | solution.py:34
  233.1 9.5 %collective-permute-start.33 = (f32[1,16,128]{2,1,0:T(8,128)S(1)}, f32[1,16,128]{2,1,0:T(8,128)S(1)}, u32[]{:S(2)}, u32[]{:S(2)}) collective-permute-start(f32[1,16,128]{2,1,0:T(8,128)S(1)} %get-tuple-element.79), channel_id=1, source_target_pairs={{16,0},{32,16},{48,32},{64,48},{80,64},{96,80},{112,96},{17,1},{33... | collective-permute-start | bytes 24584 | tf_op jit(solution)/shard_map/ppermute | solution.py:26
  255.4 17.1 %collective-permute-start.37 = (f32[1,16,128]{2,1,0:T(8,128)S(1)}, f32[1,16,128]{2,1,0:T(8,128)S(1)}, u32[]{:S(2)}, u32[]{:S(2)}) collective-permute-start(f32[1,16,128]{2,1,0:T(8,128)S(1)} %get-tuple-element.70), channel_id=1, source_target_pairs={{0,16},{16,32},{32,48},{48,64},{64,80},{80,96},{96,112},{1,17},{17... | collective-permute-start | bytes 24584 | tf_op jit(solution)/shard_map/ppermute | solution.py:25
  260.4 12.1 %collective-permute-start.38 = (f32[1,16,128]{2,1,0:T(8,128)S(1)}, f32[1,16,128]{2,1,0:T(8,128)S(1)}, u32[]{:S(2)}, u32[]{:S(2)}) collective-permute-start(f32[1,16,128]{2,1,0:T(8,128)S(1)} %get-tuple-element.71), channel_id=1, source_target_pairs={{16,0},{32,16},{48,32},{64,48},{80,64},{96,80},{112,96},{17,1},{33... | collective-permute-start | bytes 24584 | tf_op jit(solution)/shard_map/ppermute | solution.py:26
  261.7 19.3 %collective-permute-start.45 = (f32[1,16,128]{2,1,0:T(8,128)S(1)}, f32[1,16,128]{2,1,0:T(8,128)S(1)}, u32[]{:S(2)}, u32[]{:S(2)}) collective-permute-start(f32[1,16,128]{2,1,0:T(8,128)S(1)} %get-tuple-element.77), channel_id=1, source_target_pairs={{16,0},{32,16},{48,32},{64,48},{80,64},{96,80},{112,96},{17,1},{33... | collective-permute-start | bytes 24584 | tf_op jit(solution)/shard_map/ppermute | solution.py:26
  263.0 18.0 %collective-permute-start.46 = (f32[1,16,128]{2,1,0:T(8,128)S(1)}, f32[1,16,128]{2,1,0:T(8,128)S(1)}, u32[]{:S(2)}, u32[]{:S(2)}) collective-permute-start(f32[1,16,128]{2,1,0:T(8,128)S(1)} %get-tuple-element.76), channel_id=1, source_target_pairs={{0,16},{16,32},{32,48},{48,64},{64,80},{80,96},{96,112},{1,17},{17... | collective-permute-start | bytes 24584 | tf_op jit(solution)/shard_map/ppermute | solution.py:25
  272.6 17.0 %collective-permute-start.39 = (f32[50,1,128]{2,1,0:T(1,128)S(1)}, f32[50,1,128]{2,1,0:T(1,128)S(1)}, u32[]{:S(2)}, u32[]{:S(2)}) collective-permute-start(f32[50,1,128]{2,1,0:T(1,128)S(1)} %get-tuple-element.24), channel_id=1, source_target_pairs={{1,0},{2,1},{3,2},{4,3},{5,4},{6,5},{7,6},{8,7},{9,8},{10,9},{11,1... | collective-permute-start | bytes 76808 | tf_op jit(solution)/shard_map/ppermute | solution.py:26
  274.0 15.6 %collective-permute-start.40 = (f32[50,1,128]{2,1,0:T(1,128)S(1)}, f32[50,1,128]{2,1,0:T(1,128)S(1)}, u32[]{:S(2)}, u32[]{:S(2)}) collective-permute-start(f32[50,1,128]{2,1,0:T(1,128)S(1)} %get-tuple-element.25), channel_id=1, source_target_pairs={{0,1},{1,2},{2,3},{3,4},{4,5},{5,6},{6,7},{7,8},{8,9},{9,10},{10,1... | collective-permute-start | bytes 76808 | tf_op jit(solution)/shard_map/ppermute | solution.py:25
  281.1 27.2 %collective-permute-start.47 = (f32[50,1,128]{2,1,0:T(1,128)S(1)}, f32[50,1,128]{2,1,0:T(1,128)S(1)}, u32[]{:S(2)}, u32[]{:S(2)}) collective-permute-start(f32[50,1,128]{2,1,0:T(1,128)S(1)} %get-tuple-element.26), channel_id=1, source_target_pairs={{1,0},{2,1},{3,2},{4,3},{5,4},{6,5},{7,6},{8,7},{9,8},{10,9},{11,1... | collective-permute-start | bytes 76808 | tf_op jit(solution)/shard_map/ppermute | solution.py:26
  282.4 25.9 %collective-permute-start.48 = (f32[50,1,128]{2,1,0:T(1,128)S(1)}, f32[50,1,128]{2,1,0:T(1,128)S(1)}, u32[]{:S(2)}, u32[]{:S(2)}) collective-permute-start(f32[50,1,128]{2,1,0:T(1,128)S(1)} %get-tuple-element.27), channel_id=1, source_target_pairs={{0,1},{1,2},{2,3},{3,4},{4,5},{5,6},{6,7},{7,8},{8,9},{9,10},{10,1... | collective-permute-start | bytes 76808 | tf_op jit(solution)/shard_map/ppermute | solution.py:25
  298.9 9.5 %collective-permute-start.43 = (f32[50,1,128]{2,1,0:T(1,128)S(1)}, f32[50,1,128]{2,1,0:T(1,128)S(1)}, u32[]{:S(2)}, u32[]{:S(2)}) collective-permute-start(f32[50,1,128]{2,1,0:T(1,128)S(1)} %get-tuple-element.23), channel_id=1, source_target_pairs={{1,0},{2,1},{3,2},{4,3},{5,4},{6,5},{7,6},{8,7},{9,8},{10,9},{11,1... | collective-permute-start | bytes 76808 | tf_op jit(solution)/shard_map/ppermute | solution.py:26
  309.4 9.1 %collective-permute-start.49 = (f32[1,16,128]{2,1,0:T(8,128)S(1)}, f32[1,16,128]{2,1,0:T(8,128)S(1)}, u32[]{:S(2)}, u32[]{:S(2)}) collective-permute-start(f32[1,16,128]{2,1,0:T(8,128)S(1)} %get-tuple-element.59), channel_id=1, source_target_pairs={{16,0},{32,16},{48,32},{64,48},{80,64},{96,80},{112,96},{17,1},{33... | collective-permute-start | bytes 24584 | tf_op jit(solution)/shard_map/ppermute | solution.py:26
  336.2 111.6 %collective-permute-start.53 = (f32[1,16,128]{2,1,0:T(8,128)}, f32[1,16,128]{2,1,0:T(8,128)S(1)}, u32[]{:S(2)}, u32[]{:S(2)}) collective-permute-start(f32[1,16,128]{2,1,0:T(8,128)} %get-tuple-element.50), channel_id=1, source_target_pairs={{0,16},{16,32},{32,48},{48,64},{64,80},{80,96},{96,112},{1,17},{17... | collective-permute-start | bytes 24584 | tf_op jit(solution)/shard_map/ppermute | solution.py:25
  341.3 106.6 %collective-permute-start.54 = (f32[1,16,128]{2,1,0:T(8,128)}, f32[1,16,128]{2,1,0:T(8,128)S(1)}, u32[]{:S(2)}, u32[]{:S(2)}) collective-permute-start(f32[1,16,128]{2,1,0:T(8,128)} %get-tuple-element.51), channel_id=1, source_target_pairs={{16,0},{32,16},{48,32},{64,48},{80,64},{96,80},{112,96},{17,1},{33... | collective-permute-start | bytes 24584 | tf_op jit(solution)/shard_map/ppermute | solution.py:26
  342.6 111.2 %collective-permute-start.57 = (f32[1,16,128]{2,1,0:T(8,128)}, f32[1,16,128]{2,1,0:T(8,128)S(1)}, u32[]{:S(2)}, u32[]{:S(2)}) collective-permute-start(f32[1,16,128]{2,1,0:T(8,128)} %get-tuple-element.57), channel_id=1, source_target_pairs={{16,0},{32,16},{48,32},{64,48},{80,64},{96,80},{112,96},{17,1},{33... | collective-permute-start | bytes 24584 | tf_op jit(solution)/shard_map/ppermute | solution.py:26
  343.9 109.9 %collective-permute-start.58 = (f32[1,16,128]{2,1,0:T(8,128)}, f32[1,16,128]{2,1,0:T(8,128)S(1)}, u32[]{:S(2)}, u32[]{:S(2)}) collective-permute-start(f32[1,16,128]{2,1,0:T(8,128)} %get-tuple-element.56), channel_id=1, source_target_pairs={{0,16},{16,32},{32,48},{48,64},{64,80},{80,96},{96,112},{1,17},{17... | collective-permute-start | bytes 24584 | tf_op jit(solution)/shard_map/ppermute | solution.py:25
  447.9 11.8 %collective-permute-start.55 = (f32[50,1,128]{2,1,0:T(1,128)S(1)}, f32[50,1,128]{2,1,0:T(1,128)S(1)}, u32[]{:S(2)}, u32[]{:S(2)}) collective-permute-start(f32[50,1,128]{2,1,0:T(1,128)S(1)} %get-tuple-element.16), channel_id=1, source_target_pairs={{1,0},{2,1},{3,2},{4,3},{5,4},{6,5},{7,6},{8,7},{9,8},{10,9},{11,1... | collective-permute-start | bytes 76808 | tf_op jit(solution)/shard_map/ppermute | solution.py:26
  449.2 10.5 %collective-permute-start.56 = (f32[50,1,128]{2,1,0:T(1,128)S(1)}, f32[50,1,128]{2,1,0:T(1,128)S(1)}, u32[]{:S(2)}, u32[]{:S(2)}) collective-permute-start(f32[50,1,128]{2,1,0:T(1,128)S(1)} %get-tuple-element.17), channel_id=1, source_target_pairs={{0,1},{1,2},{2,3},{3,4},{4,5},{5,6},{6,7},{7,8},{8,9},{9,10},{10,1... | collective-permute-start | bytes 76808 | tf_op jit(solution)/shard_map/ppermute | solution.py:25
  (66 other events, 1010.6 us)
where the time goes:
time: 472 us; the launch traced here: 463 us
  starting transfers between devices  206 us (44%)
  blocking collectives  177 us (38%)
  waiting for transfers between devices  43.2 us (9%)
  local copies, waits for them, and re-layouts  20.1 us (4%)
  other arithmetic  11.3 us (2%)
    unnamed x2, blocking collectives  177 us
    ppermute x30, starting transfers between devices, padded_2(): before = lax.ppermute(last, axis, up)  166 us
    ppermute x30, starting transfers between devices, padded_2(): after = lax.ppermute(initial, axis, down)  38.9 us
    ppermute x1, waiting for transfers between devices, passed_along(): return lax.ppermute(array, axis, pairs)  17.6 us
    ppermute x30, waiting for transfers between devices, padded_2(): before = lax.ppermute(last, axis, up)  15.4 us
    ppermute x30, waiting for transfers between devices, padded_2(): after = lax.ppermute(initial, axis, down)  10.2 us
    slice x24, local copies, waits for them, and re-layouts, neighbour_sum(): return total + jnp.roll(middle, 1, 2) + jnp.roll(middle, -1, 2)  10 us
  transfers between devices with their start and end apart: 61, of which 19 were waited for; matrix products, arithmetic and copies ran while one was open for 4% of the time, Pallas kernels for 0%

commit v1 on v0

v1 whole, which is shorter than its diff:
```python
import jax
import jax.numpy as jnp
from jax import lax
from jax.experimental import pallas as pl
from jax.experimental.pallas import tpu as pltpu
from jax.sharding import PartitionSpec as P

AXES = ("grp", "gy", "gz")
TY = 6
ROWS, COLS, LANES = 48, 16, 128
HY = 8
EXT = ROWS + 2 * HY
ZE = 48
ZO = 16


def rows_loop(first, last, n, body):
    def step(i, carry):
        body(first + i * n)
        return carry
    lax.fori_loop(0, (last - first + 1) // n, step, 0)


def zshift(v):
    z = v.shape[1]
    return pltpu.roll(v, z - 1, 1), pltpu.roll(v, 1, 1)


def around(w):
    c = w[1:-1]
    zp, zm = zshift(c)
    s = (w[:-2] + w[2:]) + (zp + zm)
    s = s + (pltpu.roll(c, 1, 2) + pltpu.roll(c, LANES - 1, 2))
    return c, s, zp - zm


def ld(ref, r, n, z0=0, z1=ZE):
    return ref[pl.ds(r, n), z0:z1, :]


def zero_edges(edge, ref):
    ylo, yhi, zlo, zhi = edge

    @pl.when(ylo)
    def _():
        ref[HY - 1] = jnp.zeros((ZE, LANES), jnp.float32)

    @pl.when(yhi)
    def _():
        ref[HY + ROWS] = jnp.zeros((ZE, LANES), jnp.float32)

    @pl.when(zlo)
    def _():
        ref[:, ZO - 8:ZO, :] = jnp.zeros((EXT, 8, LANES), jnp.float32)

    @pl.when(zhi)
    def _():
        ref[:, ZO + COLS:ZO + COLS + 8, :] = jnp.zeros((EXT, 8, LANES), jnp.float32)


def add_ghost(edge, ref, ghost):
    if ghost is None:
        return
    _, _, zlo, zhi = edge

    @pl.when(zlo)
    def _():
        ref[:, ZO:ZO + 8, :] += ghost[...]

    @pl.when(zhi)
    def _():
        ref[:, ZO + 8:ZO + 16, :] += ghost[...]


N = 2
M0, M1 = 8, 40


def forward(edge, ghost, U, P, SRC, B, Q, U1, A):
    def stage_a(r):
        c, s, d = around(ld(U, r - 1, N + 2))
        src = (0.5 / 6.0) * d
        SRC[pl.ds(r, N)] = src
        B[pl.ds(r, N)] = 0.35 * c + 0.1 * s
        _, s, _ = around(ld(P, r - 1, N + 2))
        Q[pl.ds(r, N)] = s * (1.0 / 6.0) - src
    rows_loop(1, 62, N, stage_a)
    add_ghost(edge, Q, ghost)
    zero_edges(edge, Q)

    def stage_b(r):
        _, s, _ = around(ld(Q, r - 1, N + 2))
        P[pl.ds(r, N)] = s * (1.0 / 6.0) - ld(SRC, r, N)
    rows_loop(2, 61, N, stage_b)
    add_ghost(edge, P, ghost)
    zero_edges(edge, P)

    def stage_c(r):
        zp, zm = zshift(ld(P, r, N))
        U1[pl.ds(r, N)] = ld(B, r, N) + 0.5 * (zp - zm)
    rows_loop(3, 60, N, stage_c)
    zero_edges(edge, U1)

    def stage_d(r):
        c, s, d = around(ld(U1, r - 1, N + 2))
        src = (0.5 / 6.0) * d[:, M0:M1]
        SRC[pl.ds(r, N), M0:M1, :] = src
        B[pl.ds(r, N), M0:M1, :] = 0.35 * c[:, M0:M1] + 0.1 * s[:, M0:M1]
        _, s, _ = around(ld(P, r - 1, N + 2))
        Q[pl.ds(r, N), M0:M1, :] = s[:, M0:M1] * (1.0 / 6.0) - src
    rows_loop(3, 60, N, stage_d)
    add_ghost(edge, Q, ghost)
    zero_edges(edge, Q)

    def stage_e(r):
        _, s, _ = around(ld(Q, r - 1, N + 2, M0, M1))
        P[pl.ds(r, N), M0:M1, :] = s * (1.0 / 6.0) - ld(SRC, r, N, M0, M1)
    rows_loop(4, 59, N, stage_e)
    add_ghost(edge, P, ghost)
    zero_edges(edge, P)

    def stage_f(r):
        zp, zm = zshift(ld(P, r, N, M0, M1))
        A[pl.ds(r, N), M0:M1, :] = ld(B, r, N, M0, M1) + 0.5 * (zp - zm)
    rows_loop(4, 59, N, stage_f)
    zero_edges(edge, A)


def adjoint(edge, A, pot, u1, B, SP, S2, T, A1, S3, T2, out_u, out_p):
    def stage_g(r):
        c, s, d = around(ld(A, r - 1, N + 2, M0, M1))
        B[pl.ds(r, N), M0:M1, :] = 0.35 * c + 0.1 * s
        sp = -0.5 * d
        if pot is not None:
            sp = sp + ld(pot, r, N, M0, M1)
        SP[pl.ds(r, N), M0:M1, :] = sp
    rows_loop(4, 59, N, stage_g)
    zero_edges(edge, SP)

    def stage_h(r):
        c, s, _ = around(ld(SP, r - 1, N + 2, M0, M1))
        s = s * (1.0 / 6.0)
        S2[pl.ds(r, N), M0:M1, :] = s
        T[pl.ds(r, N), M0:M1, :] = (c + s) * (1.0 / 6.0)
    rows_loop(5, 58, N, stage_h)
    zero_edges(edge, S2)
    zero_edges(edge, T)

    def stage_i(r):
        _, s, _ = around(ld(S2, r - 1, N + 2, M0, M1))
        S3[pl.ds(r, N), M0:M1, :] = s * (1.0 / 6.0)
        zp, zm = zshift(ld(T, r, N, M0, M1))
        a = ld(B, r, N, M0, M1) + 0.5 * (zp - zm)
        if u1 is not None:
            a = a + ld(u1, r, N, M0, M1)
        A1[pl.ds(r, N), M0:M1, :] = a
    rows_loop(6, 57, N, stage_i)
    zero_edges(edge, A1)

    def stage_j(r):
        c, s, d = around(ld(A1, r - 1, N + 2, M0, M1))
        B[pl.ds(r, N), M0:M1, :] = 0.35 * c + 0.1 * s
        SP[pl.ds(r, N), M0:M1, :] = ld(S3, r, N, M0, M1) - 0.5 * d
    rows_loop(6, 57, N, stage_j)
    zero_edges(edge, SP)

    def stage_k(r):
        c, s, _ = around(ld(SP, r - 1, N + 2, M0, M1))
        s = s * (1.0 / 6.0)
        S2[pl.ds(r, N), M0:M1, :] = s
        T2[pl.ds(r, N), M0:M1, :] = (c + s) * (1.0 / 6.0)
    rows_loop(7, 56, N, stage_k)
    zero_edges(edge, S2)
    zero_edges(edge, T2)

    c0, c1 = ZO - M0, ZO - M0 + COLS

    def stage_l(r):
        _, s, _ = around(ld(S2, r - 1, N + 2, M0, M1))
        out_p[pl.ds(r - HY, N)] = s[:, c0:c1] * (1.0 / 6.0)
        zp, zm = zshift(ld(T2, r, N, M0, M1))
        out_u[pl.ds(r - HY, N)] = (ld(B, r, N, M0, M1) + 0.5 * (zp - zm))[:, c0:c1]
    rows_loop(8, 55, N, stage_l)


def load_extended(dst, f, own, yd, yu, zd, zu):
    dst[0:HY, ZO:ZO + COLS, :] = yd[f]
    dst[HY:HY + ROWS, ZO:ZO + COLS, :] = own[f]
    dst[HY + ROWS:, ZO:ZO + COLS, :] = yu[f]
    h = EXT // 2
    dst[:, 8:16, :] = zd[f, 0:EXT]
    dst[0:h, 4:8, :] = zd[f, EXT:, 0:4, :]
    dst[h:, 4:8, :] = zd[f, EXT:, 4:8, :]
    dst[:, 0:4, :] = jnp.zeros((EXT, 4, LANES), jnp.float32)
    dst[:, 32:40, :] = zu[f, 0:EXT]
    dst[0:h, 40:44, :] = zu[f, EXT:, 0:4, :]
    dst[h:, 40:44, :] = zu[f, EXT:, 4:8, :]
    dst[:, 44:48, :] = jnp.zeros((EXT, 4, LANES), jnp.float32)


def pack_kernel(own, yd, yu, up, dn):
    h = EXT // 2
    for f in range(2):
        for r0, r1, src in ((0, HY, yd), (HY, HY + ROWS, own), (HY + ROWS, EXT, yu)):
            up[f, r0:r1] = src[f, :, 8:16, :]
            dn[f, r0:r1] = src[f, :, 0:8, :]
        up[f, EXT:EXT + HY, 0:4, :] = yd[f, :, 4:8, :]
        up[f, EXT + HY:, 0:4, :] = own[f, 0:h - HY, 4:8, :]
        up[f, EXT:EXT + h - HY, 4:8, :] = own[f, h - HY:, 4:8, :]
        up[f, EXT + h - HY:, 4:8, :] = yu[f, :, 4:8, :]
        dn[f, EXT:EXT + HY, 0:4, :] = yd[f, :, 8:12, :]
        dn[f, EXT + HY:, 0:4, :] = own[f, 0:h - HY, 8:12, :]
        dn[f, EXT:EXT + h - HY, 4:8, :] = own[f, h - HY:, 8:12, :]
        dn[f, EXT + h - HY:, 4:8, :] = yu[f, :, 8:12, :]


HIGHEST = lax.Precision.HIGHEST


def edges():
    gy, gz = lax.axis_index("gy"), lax.axis_index("gz")
    return (gy == 0, gy == lax.axis_size("gy") - 1, gz == 0, gz == lax.axis_size("gz") - 1)


def iota(shape, dim):
    return lax.broadcasted_iota(jnp.int32, shape, dim)


def tile_volts(volts, labels):
    n = volts.shape[0]
    first = 2 * iota((n, LANES), 0)
    lab = jnp.broadcast_to(labels, (n, LANES))
    zero = jnp.zeros((), jnp.float32)
    hit = jnp.where(lab == first, volts[:, 0:1], zero) + jnp.where(lab == first + 1, volts[:, 1:2], zero)
    return jnp.sum(hit, axis=0, keepdims=True)


def fill_ghost(edge, ghost, volts, labels):
    v = tile_volts(volts, labels)
    lane, row = iota((8, LANES), 1), iota((8, LANES), 0)
    apart = jnp.where((lane >> 4) == row, jnp.broadcast_to(v, (8, LANES)), 0.0)
    spread = ((iota((LANES, LANES), 0) & 15) == (iota((LANES, LANES), 1) >> 3)).astype(jnp.float32)
    wall = jnp.dot(apart, spread, precision=HIGHEST, preferred_element_type=jnp.float32) * (1.0 / 6.0)
    sub = jnp.where(edge[2], 0, 7)
    for ty in range(8):
        tile = jnp.where(row == sub, jnp.broadcast_to(wall[ty:ty + 1], (8, LANES)), 0.0)
        ghost[8 * ty:8 * ty + 8] = jnp.broadcast_to(tile[None], (8, 8, LANES))


def wall_tiles(T, T2, z, held):
    w = T[HY:HY + ROWS, z, :] + T2[HY:HY + ROWS, z, :]
    held[...] = jnp.zeros((8, LANES), jnp.float32)
    held[0:TY] = jnp.sum(w.reshape(TY, 8, LANES), axis=1)
    gather = ((iota((LANES, LANES), 0) >> 3) == (iota((LANES, LANES), 1) & 15)).astype(jnp.float32)
    sums = jnp.dot(held[...], gather, precision=HIGHEST, preferred_element_type=jnp.float32)
    keep = (iota((8, LANES), 1) >> 4) == iota((8, LANES), 0)
    return jnp.sum(jnp.where(keep, sums, 0.0), axis=0, keepdims=True)


def bulk_kernel(own, yd, yu, zd, zu, volts, labels, main, send, wall,
                U, V, SRC, B, Q, U1, A, SP, S2, T, A1, S3, T2, ghost, held):
    edge = edges()
    is_forward = lax.axis_index("grp") == 0
    load_extended(U, 0, own, yd, yu, zd, zu)
    load_extended(V, 1, own, yd, yu, zd, zu)

    @pl.when(jnp.logical_or(edge[2], edge[3]))
    def _():
        fill_ghost(edge, ghost, volts[...], labels[...])

    @pl.when(is_forward)
    def _():
        forward(edge, ghost, U, V, SRC, B, Q, U1, A)
        main[0] = A[HY:HY + ROWS, ZO:ZO + COLS, :]
        main[1] = V[HY:HY + ROWS, ZO:ZO + COLS, :]
        adjoint(edge, A, None, U1, B, SP, S2, T, A1, S3, T2, send.at[0], send.at[1])

    @pl.when(jnp.logical_not(is_forward))
    def _():
        adjoint(edge, U, V, None, B, SP, S2, T, A1, S3, T2, main.at[0], main.at[1])

    wall[...] = jnp.zeros((1, LANES), jnp.float32)

    @pl.when(edge[2])
    def _():
        wall[...] = wall_tiles(T, T2, ZO, held)

    @pl.when(edge[3])
    def _():
        wall[...] = wall_tiles(T, T2, ZO + COLS - 1, held)


def final_kernel(main, extra, sums, labels, out, grad):
    out[0] = main[...] + extra[...]
    me = (lax.axis_index("grp") * lax.axis_size("gy") + lax.axis_index("gy")) * lax.axis_size("gz") + lax.axis_index("gz")
    gz, gy = lax.axis_size("gz"), lax.axis_size("gy")
    total = jnp.zeros((8, LANES), jnp.float32)
    pair = [total, total]
    for s in range(2):
        w = sums[pl.ds(s * (gz - 1), gy, stride=gz), :] + sums[pl.ds(gy * gz + s * (gz - 1), gy, stride=gz), :]
        lab = labels[s]
        for j in range(2):
            pair[j] = pair[j] + jnp.where(lab == 2 * me + j, w, 0.0)
    g = [jnp.sum(p) for p in pair]
    lane = iota((1, 2), 1)
    grad[...] = jnp.where(lane == 0, g[0], g[1])


def vmem(n):
    return [pl.BlockSpec(memory_space=pltpu.VMEM)] * n


def shape(*dims):
    return jax.ShapeDtypeStruct(dims, jnp.float32)


def to_all(row):
    n = lax.axis_size(AXES)
    return lax.all_to_all(jnp.broadcast_to(row, (n, LANES)), AXES, 0, 0, tiled=True)


def shifted(array, axis, by):
    count = lax.axis_size(axis)
    pairs = [(i, i + by) for i in range(count) if 0 <= i + by < count]
    return lax.ppermute(array, axis, pairs)


def per_device(field_pairs, tile_owner, electrode_volts):
    own = field_pairs[0]
    labels = tile_owner[..., 0]
    gy, gz = lax.axis_index("gy"), lax.axis_index("gz")
    big = pltpu.VMEM((EXT, ZE, LANES), jnp.float32)
    roomy = pltpu.CompilerParams(vmem_limit_bytes=40 * 1024 * 1024)

    yd = shifted(own[:, ROWS - HY:], "gy", 1)
    yu = shifted(own[:, :HY], "gy", -1)
    volts = to_all(jnp.pad(electrode_volts, (0, LANES - 2))[None])
    up, dn = pl.pallas_call(
        pack_kernel, out_shape=(shape(2, EXT * 3 // 2, 8, LANES),) * 2,
        in_specs=vmem(3), out_specs=vmem(2),
    )(own, yd, yu)
    zd = shifted(up, "gz", 1)
    zu = shifted(dn, "gz", -1)

    fenced = jnp.pad(labels, ((0, 0), (1, 1), (0, 0)), constant_values=-1)
    side = (gz == lax.axis_size("gz") - 1).astype(jnp.int32)
    near = lax.dynamic_slice(fenced, (side, gy * TY, 0), (1, 8, 16)).reshape(1, LANES)
    block = shape(2, ROWS, COLS, LANES)
    main, send, wall = pl.pallas_call(
        bulk_kernel, out_shape=(block, block, shape(1, LANES)),
        in_specs=vmem(7), out_specs=vmem(3),
        scratch_shapes=[big] * 13 + [pltpu.VMEM((EXT, 8, LANES), jnp.float32), pltpu.VMEM((8, LANES), jnp.float32)],
        compiler_params=roomy,
    )(own, yd, yu, zd, zu, volts, near)

    extra = lax.ppermute(send, "grp", [(0, 1)])
    sums = to_all(wall)
    by_block = jnp.pad(labels.reshape(2, 8, TY * 16), ((0, 0), (0, 0), (0, LANES - TY * 16)), constant_values=-1)
    advanced, grad = pl.pallas_call(
        final_kernel, out_shape=(shape(1, 2, ROWS, COLS, LANES), shape(1, 2)),
        in_specs=vmem(4), out_specs=vmem(2), compiler_params=roomy,
    )(main, extra, sums, by_block)
    return (advanced, grad.reshape(2))


def solution(mesh):
    placed = (P("grp", None, "gy", "gz", None), P(), P(AXES))
    return jax.shard_map(
        per_device, mesh=mesh, in_specs=placed,
        out_specs=(P("grp", None, "gy", "gz", None), P(AXES)), check_vma=False,
    )
```

time: 472 us -> 109 us (0.23)
  the two profiles are of different devices: /device:TPU:32 before, /device:TPU:1 now
where the time goes in v1:
time: 109 us
  starting transfers between devices  37.9 us (35%)
  waiting for transfers between devices  33.5 us (31%)
  Pallas kernels  32.2 us (30%)
  local copies, waits for them, and re-layouts  4.21 us (4%)
    pallas_call x1, Pallas kernels, per_device(): pl.pallas_call(bulk_kernel, out_shape=(block, block, shape(1, LANES)), in...  28.7 us
    all_to_all x2, waiting for transfers between devices, to_all(): lax.all_to_all(jnp.broadcast_to(row, (n, LANES)), AXES, 0, 0, tiled=True)  28.2 us
    all_to_all x2, starting transfers between devices, to_all(): lax.all_to_all(jnp.broadcast_to(row, (n, LANES)), AXES, 0, 0, tiled=True)  23.6 us
    ppermute x4, starting transfers between devices, shifted(): return lax.ppermute(array, axis, pairs)  12.9 us
    ppermute x4, waiting for transfers between devices, shifted(): return lax.ppermute(array, axis, pairs)  5.26 us
    pallas_call x1, Pallas kernels, per_device(): pl.pallas_call(pack_kernel, out_shape=(shape(2, EXT * 3 // 2, 8, LANES),)...  2.51 us
  transfers between devices with their start and end apart: 7, of which 3 were waited for; matrix products, arithmetic and copies ran while one was open for 2% of the time, Pallas kernels for 0%

profile of v1, /device:TPU:1, one launch (start us, length us, event | category | flops | bytes accessed | tf_op | source)
XLA Modules:
  0.0 108.5 jit_solution(10340532369469279085)
XLA Ops:
  0.6 1.0 fusion
  1.6 6.4 %collective-permute-start = (f32[2,8,16,128]{3,2,1,0:T(8,128)S(1)}, f32[2,8,16,128]{3,2,1,0:T(8,128)S(1)}, u32[]{:S(2)}, u32[]{:S(2)}) collective-permute-start(f32[2,8,16,128]{3,2,1,0:T(8,128)S(1)} %get-tuple-element.17), channel_id=1, source_target_pairs={{0,16},{16,32},{32,48},{48,64},{64,80},{80,96},{96,112},{1,17},{17... | collective-permute-start | bytes 393224 | tf_op jit(solution)/shard_map/ppermute | solution.py:325
  8.1 1.9 %collective-permute-start.1 = (f32[2,8,16,128]{3,2,1,0:T(8,128)S(1)}, f32[2,8,16,128]{3,2,1,0:T(8,128)S(1)}, u32[]{:S(2)}, u32[]{:S(2)}) collective-permute-start(f32[2,8,16,128]{3,2,1,0:T(8,128)S(1)} %get-tuple-element.16), channel_id=1, source_target_pairs={{16,0},{32,16},{48,32},{64,48},{80,64},{96,80},{112,96},{17,1},{33... | collective-permute-start | bytes 393224 | tf_op jit(solution)/shard_map/ppermute | solution.py:325
  10.0 5.2 %collective-permute-done.1.yu = f32[2,8,16,128]{3,2,1,0:T(8,128)S(1)} collective-permute-done((f32[2,8,16,128]{3,2,1,0:T(8,128)S(1)}, f32[2,8,16,128]{3,2,1,0:T(8,128)S(1)}, u32[]{:S(2)}, u32[]{:S(2)}) %collective-permute-start.1) | collective-permute-done | bytes 131104 | tf_op jit(solution)/shard_map/ppermute | solution.py:325
  15.3 0.6 copy-done.3
  15.9 2.5 %shard_map.50 = (f32[2,96,8,128]{3,2,1,0:T(8,128)}, f32[2,96,8,128]{3,2,1,0:T(8,128)}) custom-call(f32[2,48,16,128]{3,2,1,0:T(8,128)} %bitcast.11, f32[2,8,16,128]{3,2,1,0:T(8,128)} %copy-done.1, f32[2,8,16,128]{3,2,1,0:T(8,128)} %copy-done.3), custom_call_target="tpu_custom_call" | custom-call | tf_op jit(solution)/shard_map/pallas_call | solution.py:338
  18.4 3.3 %collective-permute-start.2 = (f32[2,96,8,128]{3,2,1,0:T(8,128)}, f32[2,96,8,128]{3,2,1,0:T(8,128)S(1)}, u32[]{:S(2)}, u32[]{:S(2)}) collective-permute-start(f32[2,96,8,128]{3,2,1,0:T(8,128)} %get-tuple-element.9), channel_id=1, source_target_pairs={{0,1},{1,2},{2,3},{3,4},{4,5},{5,6},{6,7},{7,8},{8,9},{9,10},{10,1... | collective-permute-start | bytes 2359304 | tf_op jit(solution)/shard_map/ppermute | solution.py:325
  21.7 1.3 %collective-permute-start.3 = (f32[2,96,8,128]{3,2,1,0:T(8,128)}, f32[2,96,8,128]{3,2,1,0:T(8,128)S(1)}, u32[]{:S(2)}, u32[]{:S(2)}) collective-permute-start(f32[2,96,8,128]{3,2,1,0:T(8,128)} %get-tuple-element.10), channel_id=1, source_target_pairs={{1,0},{2,1},{3,2},{4,3},{5,4},{6,5},{7,6},{8,7},{9,8},{10,9},{11,1... | collective-permute-start | bytes 2359304 | tf_op jit(solution)/shard_map/ppermute | solution.py:325
  23.0 0.7 broadcast_in_dim.4
  23.8 15.0 %all-to-all-start = ((f32[256,1,128]{2,1,0:T(1,128)}), f32[256,1,128]{2,1,0:T(1,128)S(1)}, u32[]{:S(2)}, u32[]{:S(2)}) async-start(f32[256,1,128]{2,1,0:T(1,128)} %broadcast_in_dim.4), calls=%async_computation | async-start | bytes 262144 | tf_op jit(solution)/shard_map/all_to_all | solution.py:319
  38.8 0.0 copy-start.5
  38.8 0.7 copy-done.5
  39.5 0.1 pad_dynamic-slice_fusion
  39.6 0.1 copy.9
  39.6 0.1 reshape.22.labels
  39.7 12.0 %all-to-all-done = f32[256,1,128]{2,1,0:T(1,128)S(1)} async-done(((f32[256,1,128]{2,1,0:T(1,128)}), f32[256,1,128]{2,1,0:T(1,128)S(1)}, u32[]{:S(2)}, u32[]{:S(2)}) %all-to-all-start) | async-done | bytes 131104 | tf_op jit(solution)/shard_map/all_to_all | solution.py:319
  51.7 28.7 %shard_map.51 = (f32[2,48,16,128]{3,2,1,0:T(8,128)S(1)}, f32[2,48,16,128]{3,2,1,0:T(8,128)}, f32[1,128]{1,0:T(1,128)S(1)}) custom-call(f32[2,48,16,128]{3,2,1,0:T(8,128)S(1)} %bitcast.12, f32[2,8,16,128]{3,2,1,0:T(8,128)S(1)} %copy-done.2, f32[2,8,16,128]{3,2,1,0:T(8,128)S(1)} %copy-done.4, f32[2,96,8,128]{3,2,1,0:T(8,128)S(1)} %collective-permute-done.2.zd, ...), custom_call_target="tpu_custom_call" | custom-call | tf_op jit(solution)/shard_map/pallas_call | solution.py:349
  80.4 1.3 %collective-permute-start.4 = (f32[2,48,16,128]{3,2,1,0:T(8,128)}, f32[2,48,16,128]{3,2,1,0:T(8,128)S(1)}, u32[]{:S(2)}, u32[]{:S(2)}) collective-permute-start(f32[2,48,16,128]{3,2,1,0:T(8,128)} %get-tuple-element.12), channel_id=1, source_target_pairs={{0,128},{1,129},{2,130},{3,131},{4,132},{5,133},{6,134},{7,135},{8... | collective-permute-start | bytes 2359304 | tf_op jit(solution)/shard_map/ppermute | solution.py:356
  81.8 0.7 broadcast_in_dim.5
  82.5 8.6 %all-to-all-start.1 = ((f32[256,1,128]{2,1,0:T(1,128)}), f32[256,1,128]{2,1,0:T(1,128)S(1)}, u32[]{:S(2)}, u32[]{:S(2)}) async-start(f32[256,1,128]{2,1,0:T(1,128)} %broadcast_in_dim.5), calls=%async_computation.1 | async-start | bytes 262144 | tf_op jit(solution)/shard_map/all_to_all | solution.py:319
  91.1 0.1 copy.10
  91.2 0.1 reshape_squeeze.3
  91.3 16.3 %all-to-all-done.1 = f32[256,1,128]{2,1,0:T(1,128)S(1)} async-done(((f32[256,1,128]{2,1,0:T(1,128)}), f32[256,1,128]{2,1,0:T(1,128)S(1)}, u32[]{:S(2)}, u32[]{:S(2)}) %all-to-all-start.1) | async-done | bytes 131104 | tf_op jit(solution)/shard_map/all_to_all | solution.py:319
  107.6 1.0 shard_map.52
  (19 shorter events, 0.0 us)
Async XLA Ops:
  1.6 50.1 %copy-start = (f32[1,2,48,16,128]{4,3,2,1,0:T(8,128)S(1)}, f32[1,2,48,16,128]{4,3,2,1,0:T(8,128)}, u32[]{:S(2)}) copy-start(f32[1,2,48,16,128]{4,3,2,1,0:T(8,128)} %param.3) | copy-start | bytes 2359300
  1.6 8.4 %collective-permute-start = (f32[2,8,16,128]{3,2,1,0:T(8,128)S(1)}, f32[2,8,16,128]{3,2,1,0:T(8,128)S(1)}, u32[]{:S(2)}, u32[]{:S(2)}) collective-permute-start(f32[2,8,16,128]{3,2,1,0:T(8,128)S(1)} %get-tuple-element.17), channel_id=1, source_target_pairs={{0,16},{16,32},{32,48},{48,64},{64,80},{80,96},{96,112},{1,17},{17... | collective-permute-start | bytes 393224 | tf_op jit(solution)/shard_map/ppermute | solution.py:325
  8.1 7.2 %collective-permute-start.1 = (f32[2,8,16,128]{3,2,1,0:T(8,128)S(1)}, f32[2,8,16,128]{3,2,1,0:T(8,128)S(1)}, u32[]{:S(2)}, u32[]{:S(2)}) collective-permute-start(f32[2,8,16,128]{3,2,1,0:T(8,128)S(1)} %get-tuple-element.16), channel_id=1, source_target_pairs={{16,0},{32,16},{48,32},{64,48},{80,64},{96,80},{112,96},{17,1},{33... | collective-permute-start | bytes 393224 | tf_op jit(solution)/shard_map/ppermute | solution.py:325
  10.0 5.3 %copy-start.1 = (f32[2,8,16,128]{3,2,1,0:T(8,128)}, f32[2,8,16,128]{3,2,1,0:T(8,128)S(1)}, u32[]{:S(2)}) copy-start(f32[2,8,16,128]{3,2,1,0:T(8,128)S(1)} %collective-permute-done.yd) | copy-start | bytes 393220
  15.3 0.6 copy-start.3
  18.4 4.6 %copy-start.7 = (f32[2]{0:T(128)S(1)}, f32[2]{0:T(128)}, u32[]{:S(2)}) copy-start(f32[2]{0:T(128)} %param.5) | copy-start | bytes 28
  18.4 33.3 %collective-permute-start.2 = (f32[2,96,8,128]{3,2,1,0:T(8,128)}, f32[2,96,8,128]{3,2,1,0:T(8,128)S(1)}, u32[]{:S(2)}, u32[]{:S(2)}) collective-permute-start(f32[2,96,8,128]{3,2,1,0:T(8,128)} %get-tuple-element.9), channel_id=1, source_target_pairs={{0,1},{1,2},{2,3},{3,4},{4,5},{5,6},{6,7},{7,8},{8,9},{9,10},{10,1... | collective-permute-start | bytes 2359304 | tf_op jit(solution)/shard_map/ppermute | solution.py:325
  21.7 30.0 %collective-permute-start.3 = (f32[2,96,8,128]{3,2,1,0:T(8,128)}, f32[2,96,8,128]{3,2,1,0:T(8,128)S(1)}, u32[]{:S(2)}, u32[]{:S(2)}) collective-permute-start(f32[2,96,8,128]{3,2,1,0:T(8,128)} %get-tuple-element.10), channel_id=1, source_target_pairs={{1,0},{2,1},{3,2},{4,3},{5,4},{6,5},{7,6},{8,7},{9,8},{10,9},{11,1... | collective-permute-start | bytes 2359304 | tf_op jit(solution)/shard_map/ppermute | solution.py:325
  23.8 27.9 %copy-start.2 = (f32[2,8,16,128]{3,2,1,0:T(8,128)S(1)}, f32[2,8,16,128]{3,2,1,0:T(8,128)}, u32[]{:S(2)}) copy-start(f32[2,8,16,128]{3,2,1,0:T(8,128)} %copy-done.1) | copy-start | bytes 393220
  23.8 28.0 %copy-start.4 = (f32[2,8,16,128]{3,2,1,0:T(8,128)S(1)}, f32[2,8,16,128]{3,2,1,0:T(8,128)}, u32[]{:S(2)}) copy-start(f32[2,8,16,128]{3,2,1,0:T(8,128)} %copy-done.3) | copy-start | bytes 393220
  23.8 27.9 %all-to-all-start = ((f32[256,1,128]{2,1,0:T(1,128)}), f32[256,1,128]{2,1,0:T(1,128)S(1)}, u32[]{:S(2)}, u32[]{:S(2)}) async-start(f32[256,1,128]{2,1,0:T(1,128)} %broadcast_in_dim.4), calls=%async_computation | async-start | bytes 262144 | tf_op jit(solution)/shard_map/all_to_all | solution.py:319
  38.8 0.7 copy-start.5
  80.4 27.1 %collective-permute-start.4 = (f32[2,48,16,128]{3,2,1,0:T(8,128)}, f32[2,48,16,128]{3,2,1,0:T(8,128)S(1)}, u32[]{:S(2)}, u32[]{:S(2)}) collective-permute-start(f32[2,48,16,128]{3,2,1,0:T(8,128)} %get-tuple-element.12), channel_id=1, source_target_pairs={{0,128},{1,129},{2,130},{3,131},{4,132},{5,133},{6,134},{7,135},{8... | collective-permute-start | bytes 2359304 | tf_op jit(solution)/shard_map/ppermute | solution.py:356
  82.5 8.6 %copy-start.6 = (s32[2,48,16,1]{1,3,2,0:T(1,128)S(1)}, s32[2,48,16,1]{1,3,2,0:T(1,128)}, u32[]{:S(2)}) copy-start(s32[2,48,16,1]{1,3,2,0:T(1,128)} %param.4) | copy-start | bytes 18436
  82.5 25.1 %all-to-all-start.1 = ((f32[256,1,128]{2,1,0:T(1,128)}), f32[256,1,128]{2,1,0:T(1,128)S(1)}, u32[]{:S(2)}, u32[]{:S(2)}) async-start(f32[256,1,128]{2,1,0:T(1,128)} %broadcast_in_dim.5), calls=%async_computation.1 | async-start | bytes 262144 | tf_op jit(solution)/shard_map/all_to_all | solution.py:319

commit v2 on v1

v2 whole, which is shorter than its diff:
```python
import functools

import jax
import jax.numpy as jnp
import numpy as np
from jax import lax
from jax.experimental import pallas as pl
from jax.experimental.pallas import tpu as pltpu
from jax.sharding import PartitionSpec as P

AXES = ("grp", "gy", "gz")
TY = 6
VOLT = TY * 16
ROWS, COLS, LANES = 48, 16, 128
HY = 8
EXT = ROWS + 2 * HY
ZE = 48
ZO = 16


def rows_loop(first, last, body):
    n = (last - first + 1) // 2

    def step(i, carry):
        body(first + i * n, n)
        return carry
    lax.fori_loop(0, 2, step, 0)


def zshift(v, closed):
    z = v.shape[1]
    zp, zm = pltpu.roll(v, z - 1, 1), pltpu.roll(v, 1, 1)
    if closed:
        layer = lax.broadcasted_iota(jnp.int32, v.shape, 1)
        zp = jnp.where(layer == z - 1, 0.0, zp)
        zm = jnp.where(layer == 0, 0.0, zm)
    return zp, zm


def around(w, closed):
    c = w[1:-1]
    zp, zm = zshift(c, closed)
    s = (w[:-2] + w[2:]) + (zp + zm)
    s = s + (pltpu.roll(c, 1, 2) + pltpu.roll(c, LANES - 1, 2))
    return c, s, zp - zm


def zero_edges(edge, ref):
    ylo, yhi, zlo, zhi = edge
    depth = ref.shape[1]

    @pl.when(ylo)
    def _():
        ref[HY - 1] = jnp.zeros((depth, LANES), jnp.float32)

    @pl.when(yhi)
    def _():
        ref[HY + ROWS] = jnp.zeros((depth, LANES), jnp.float32)

    if zlo is None:
        return

    @pl.when(zlo)
    def _():
        ref[:, ZO - 8:ZO, :] = jnp.zeros((EXT, 8, LANES), jnp.float32)

    @pl.when(zhi)
    def _():
        ref[:, ZO + COLS:ZO + COLS + 8, :] = jnp.zeros((EXT, 8, LANES), jnp.float32)


BULK = (0, ZE, 8, 40, ZO, False)
NEAR = (0, COLS, 0, COLS, 0, True)


def forward(edge, ghost, window, U, V, SRC, B, Q, U1, A):
    W0, W1, M0, M1, _, closed = window
    m = slice(M0 - W0, M1 - W0)

    def ld(ref, r, n, z0=M0, z1=M1):
        return ref[pl.ds(r, n), z0:z1, :]

    def finish(ref):
        if ghost is not None:
            ref[...] += ghost[...]
        zero_edges(edge, ref)

    def stage_a(r, n):
        c, s, d = around(ld(U, r - 1, n + 2, W0, W1), closed)
        src = (0.5 / 6.0) * d
        SRC[pl.ds(r, n), W0:W1, :] = src
        B[pl.ds(r, n), W0:W1, :] = 0.35 * c + 0.1 * s
        _, s, _ = around(ld(V, r - 1, n + 2, W0, W1), closed)
        Q[pl.ds(r, n), W0:W1, :] = s * (1.0 / 6.0) - src
    if U is None:
        Q[...] = ghost[...]
        zero_edges(edge, Q)
    else:
        rows_loop(1, 62, stage_a)
        finish(Q)

    def stage_b(r, n):
        _, s, _ = around(ld(Q, r - 1, n + 2, W0, W1), closed)
        s = s * (1.0 / 6.0)
        V[pl.ds(r, n), W0:W1, :] = s if U is None else s - ld(SRC, r, n, W0, W1)
    rows_loop(2, 61, stage_b)
    finish(V)

    def stage_c(r, n):
        zp, zm = zshift(ld(V, r, n, W0, W1), closed)
        u = 0.5 * (zp - zm)
        U1[pl.ds(r, n), W0:W1, :] = u if U is None else u + ld(B, r, n, W0, W1)
    rows_loop(3, 60, stage_c)
    zero_edges(edge, U1)

    def stage_d(r, n):
        c, s, d = around(ld(U1, r - 1, n + 2, W0, W1), closed)
        src = (0.5 / 6.0) * d[:, m]
        SRC[pl.ds(r, n), M0:M1, :] = src
        B[pl.ds(r, n), M0:M1, :] = 0.35 * c[:, m] + 0.1 * s[:, m]
        _, s, _ = around(ld(V, r - 1, n + 2, W0, W1), closed)
        Q[pl.ds(r, n), M0:M1, :] = s[:, m] * (1.0 / 6.0) - src
    rows_loop(3, 60, stage_d)
    finish(Q)

    def stage_e(r, n):
        _, s, _ = around(ld(Q, r - 1, n + 2), closed)
        V[pl.ds(r, n), M0:M1, :] = s * (1.0 / 6.0) - ld(SRC, r, n)
    rows_loop(4, 59, stage_e)
    finish(V)

    def stage_f(r, n):
        zp, zm = zshift(ld(V, r, n), closed)
        A[pl.ds(r, n), M0:M1, :] = ld(B, r, n) + 0.5 * (zp - zm)
    rows_loop(4, 59, stage_f)
    zero_edges(edge, A)


def adjoint(edge, window, A, pot, u1, B, SP, S2, T, A1, S3, T2, give):
    _, _, M0, M1, first, closed = window

    def ld(ref, r, n):
        return ref[pl.ds(r, n), M0:M1, :]

    def stage_g(r, n):
        c, s, d = around(ld(A, r - 1, n + 2), closed)
        B[pl.ds(r, n), M0:M1, :] = 0.35 * c + 0.1 * s
        sp = -0.5 * d
        if pot is not None:
            sp = sp + ld(pot, r, n)
        SP[pl.ds(r, n), M0:M1, :] = sp
    rows_loop(4, 59, stage_g)
    zero_edges(edge, SP)

    def stage_h(r, n):
        c, s, _ = around(ld(SP, r - 1, n + 2), closed)
        s = s * (1.0 / 6.0)
        S2[pl.ds(r, n), M0:M1, :] = s
        T[pl.ds(r, n), M0:M1, :] = (c + s) * (1.0 / 6.0)
    rows_loop(5, 58, stage_h)
    zero_edges(edge, S2)
    zero_edges(edge, T)

    def stage_i(r, n):
        _, s, _ = around(ld(S2, r - 1, n + 2), closed)
        S3[pl.ds(r, n), M0:M1, :] = s * (1.0 / 6.0)
        zp, zm = zshift(ld(T, r, n), closed)
        a = ld(B, r, n) + 0.5 * (zp - zm)
        if u1 is not None:
            a = a + ld(u1, r, n)
        A1[pl.ds(r, n), M0:M1, :] = a
    rows_loop(6, 57, stage_i)
    zero_edges(edge, A1)

    def stage_j(r, n):
        c, s, d = around(ld(A1, r - 1, n + 2), closed)
        B[pl.ds(r, n), M0:M1, :] = 0.35 * c + 0.1 * s
        SP[pl.ds(r, n), M0:M1, :] = ld(S3, r, n) - 0.5 * d
    rows_loop(6, 57, stage_j)
    zero_edges(edge, SP)

    def stage_k(r, n):
        c, s, _ = around(ld(SP, r - 1, n + 2), closed)
        s = s * (1.0 / 6.0)
        S2[pl.ds(r, n), M0:M1, :] = s
        T2[pl.ds(r, n), M0:M1, :] = (c + s) * (1.0 / 6.0)
    rows_loop(7, 56, stage_k)
    zero_edges(edge, S2)
    zero_edges(edge, T2)
    if give is None:
        return
    own = slice(first - M0, first - M0 + COLS)

    def stage_l(r, n):
        _, s, _ = around(ld(S2, r - 1, n + 2), closed)
        zp, zm = zshift(ld(T2, r, n), closed)
        u = ld(B, r, n) + 0.5 * (zp - zm)
        give(pl.ds(r - HY, n), u[:, own], s[:, own] * (1.0 / 6.0))
    rows_loop(8, 55, stage_l)


HALF = ROWS // 2


def load_extended(dst, f, own, yd, yu, zd, zu, cd, cu):
    top = HY + ROWS
    dst[0:HY, ZO:ZO + COLS, :] = yd[f]
    dst[HY:top, ZO:ZO + COLS, :] = own[f]
    dst[top:, ZO:ZO + COLS, :] = yu[f]
    for z, c, near, far in ((zd, cd, 8, 4), (zu, cu, 32, 40)):
        dst[HY:top, near:near + 8, :] = z[f, 0:ROWS]
        dst[HY:HY + HALF, far:far + 4, :] = z[f, ROWS:, 0:4, :]
        dst[HY + HALF:top, far:far + 4, :] = z[f, ROWS:, 4:8, :]
        dst[0:HY, near:near + 8, :] = c[f, 0:HY]
        dst[top:, near:near + 8, :] = c[f, HY:2 * HY]
        dst[0:HY, far:far + 4, :] = c[f, 2 * HY:, 0:4, :]
        dst[top:, far:far + 4, :] = c[f, 2 * HY:, 4:8, :]
    for z in (0, 44):
        dst[:, z:z + 4, :] = jnp.zeros((EXT, 4, LANES), jnp.float32)


def pack_kernel(own, low, high, up, dn):
    low[...] = own[:, 0:HY]
    high[...] = own[:, ROWS - HY:]
    up[:, 0:ROWS] = own[:, :, 8:16, :]
    up[:, ROWS:, 0:4, :] = own[:, 0:HALF, 4:8, :]
    up[:, ROWS:, 4:8, :] = own[:, HALF:, 4:8, :]
    dn[:, 0:ROWS] = own[:, :, 0:8, :]
    dn[:, ROWS:, 0:4, :] = own[:, 0:HALF, 8:12, :]
    dn[:, ROWS:, 4:8, :] = own[:, HALF:, 8:12, :]


def corner_kernel(yd, yu, up, dn):
    up[:, 0:HY] = yd[:, :, 8:16, :]
    up[:, HY:2 * HY] = yu[:, :, 8:16, :]
    up[:, 2 * HY:, 0:4, :] = yd[:, :, 4:8, :]
    up[:, 2 * HY:, 4:8, :] = yu[:, :, 4:8, :]
    dn[:, 0:HY] = yd[:, :, 0:8, :]
    dn[:, HY:2 * HY] = yu[:, :, 0:8, :]
    dn[:, 2 * HY:, 0:4, :] = yd[:, :, 8:12, :]
    dn[:, 2 * HY:, 4:8, :] = yu[:, :, 8:12, :]


HIGHEST = lax.Precision.HIGHEST


def edges():
    gy, gz = lax.axis_index("gy"), lax.axis_index("gz")
    return (gy == 0, gy == lax.axis_size("gy") - 1, gz == 0, gz == lax.axis_size("gz") - 1)


def iota(shape, dim):
    return lax.broadcasted_iota(jnp.int32, shape, dim)


def tile_volts(first, second, labels):
    lab = jnp.broadcast_to(labels, first.shape) - 2 * iota(first.shape, 0)
    hit = jnp.where(lab == 0, first, 0.0) + jnp.where(lab == 1, second, 0.0)
    return jnp.sum(hit, axis=0, keepdims=True)


def fill_ghost(upper, ghost, volts):
    lane, row = iota((8, LANES), 1), iota((8, LANES), 0)
    apart = jnp.where((lane >> 4) == row, jnp.broadcast_to(volts, (8, LANES)), 0.0)
    spread = ((iota((LANES, LANES), 0) & 15) == (iota((LANES, LANES), 1) >> 3)).astype(jnp.float32)
    wall = jnp.dot(apart, spread, precision=HIGHEST, preferred_element_type=jnp.float32) * (1.0 / 6.0)
    layer = iota((COLS, LANES), 0) == jnp.where(upper, COLS - 1, 0)
    for ty in range(8):
        tile = jnp.where(layer, jnp.broadcast_to(wall[ty:ty + 1], (COLS, LANES)), 0.0)
        ghost[8 * ty:8 * ty + 8] = jnp.broadcast_to(tile[None], (8, COLS, LANES))


def wall_tiles(upper, T, T2, held):
    layer = iota((ROWS, COLS, LANES), 1) == jnp.where(upper, COLS - 1, 0)
    w = jnp.sum(jnp.where(layer, T[HY:HY + ROWS] + T2[HY:HY + ROWS], 0.0), axis=1)
    held[...] = jnp.zeros((8, LANES), jnp.float32)
    held[0:TY] = jnp.sum(w.reshape(TY, 8, LANES), axis=1)
    gather = ((iota((LANES, LANES), 0) >> 3) == (iota((LANES, LANES), 1) & 15)).astype(jnp.float32)
    sums = jnp.dot(held[...], gather, precision=HIGHEST, preferred_element_type=jnp.float32)
    keep = (iota((8, LANES), 1) >> 4) == iota((8, LANES), 0)
    return jnp.sum(jnp.where(keep, sums, 0.0), axis=0, keepdims=True)


def wall_kernel(own, yd, yu, volts, row, U, V, SRC, B, Q, U1, A, SP, S2, T, A1, S3, T2, held, sums):
    ylo, yhi, zlo, zhi = edges()
    edge = (ylo, yhi, None, None)
    is_forward = lax.axis_index("grp") == 0
    sums[...] = jnp.zeros((1, LANES), jnp.float32)

    @pl.when(jnp.logical_or(zlo, zhi))
    def _():
        for f, ref in ((0, U), (1, V)):
            ref[0:HY] = yd[f]
            ref[HY:HY + ROWS] = own[f]
            ref[HY + ROWS:] = yu[f]

        @pl.when(is_forward)
        def _():
            forward(edge, None, NEAR, U, V, SRC, B, Q, U1, A)
            adjoint(edge, NEAR, A, None, U1, B, SP, S2, T, A1, S3, T2, None)

        @pl.when(jnp.logical_not(is_forward))
        def _():
            adjoint(edge, NEAR, U, V, None, B, SP, S2, T, A1, S3, T2, None)

        sums[...] = wall_tiles(zhi, T, T2, held)

    lane = iota((1, LANES), 1)
    out = jnp.where(lane == VOLT, volts[0], jnp.where(lane == VOLT + 1, volts[1], sums[...]))
    row[...] = jnp.broadcast_to(out, row.shape)


def bulk_kernel(own, yd, yu, zd, zu, cd, cu, main, send, U, V, SRC, B, Q, U1, A, SP, S2, T, A1, S3, T2):
    edge = edges()
    is_forward = lax.axis_index("grp") == 0
    load_extended(U, 0, own, yd, yu, zd, zu, cd, cu)
    load_extended(V, 1, own, yd, yu, zd, zu, cd, cu)

    def into(ref):
        def give(rows, u, p):
            ref[0, rows] = u
            ref[1, rows] = p
        return give

    @pl.when(is_forward)
    def _():
        forward(edge, None, BULK, U, V, SRC, B, Q, U1, A)
        main[0] = A[HY:HY + ROWS, ZO:ZO + COLS, :]
        main[1] = V[HY:HY + ROWS, ZO:ZO + COLS, :]
        adjoint(edge, BULK, A, None, U1, B, SP, S2, T, A1, S3, T2, into(send))

    @pl.when(jnp.logical_not(is_forward))
    def _():
        adjoint(edge, BULK, U, V, None, B, SP, S2, T, A1, S3, T2, into(main))


def volts_kernel(main, rows, near, labels, response, out, grad, V, SRC, B, Q, U1, A, SP, S2, T, A1, S3, T2, ghost):
    ylo, yhi, zlo, zhi = edges()
    edge = (ylo, yhi, None, None)
    is_forward = lax.axis_index("grp") == 0
    n = rows.shape[0]
    first = jnp.broadcast_to(rows[:, VOLT:VOLT + 1], (n, LANES))
    second = jnp.broadcast_to(rows[:, VOLT + 1:VOLT + 2], (n, LANES))

    @pl.when(jnp.logical_or(zlo, zhi))
    def _():
        fill_ghost(zhi, ghost, tile_volts(first, second, near[...]))
        forward(edge, ghost, NEAR, None, V, SRC, B, Q, U1, A)

        @pl.when(is_forward)
        def _():
            out[0] = main[0] + A[HY:HY + ROWS]
            out[1] = main[1] + V[HY:HY + ROWS]

        @pl.when(jnp.logical_not(is_forward))
        def _():
            def give(at, u, p):
                out[0, at] = main[0, at] + u
                out[1, at] = main[1, at] + p
            adjoint(edge, NEAR, A, None, U1, B, SP, S2, T, A1, S3, T2, give)

    @pl.when(jnp.logical_not(jnp.logical_or(zlo, zhi)))
    def _():
        out[...] = main[...]

    gy, gz = lax.axis_size("gy"), lax.axis_size("gz")
    me = (lax.axis_index("grp") * gy + lax.axis_index("gy")) * gz + lax.axis_index("gz")
    pair = [jnp.zeros((gy, LANES), jnp.float32)] * 2
    block = iota((gy, LANES), 0)
    for s in range(2):
        v = jnp.concatenate([tile_volts(first, second, labels[s, g:g + 1]) for g in range(gy)], axis=0)
        r = jnp.dot(v, response[...], precision=HIGHEST, preferred_element_type=jnp.float32)
        r = [r[:, k * LANES:(k + 1) * LANES] for k in range(5)]
        w = jnp.where(block == 0, r[3], jnp.where(block == gy - 1, r[4], r[0]))
        w = w + jnp.where(block == 0, 0.0, pltpu.roll(r[1], 1, 0))
        w = w + jnp.where(block == gy - 1, 0.0, pltpu.roll(r[2], gy - 1, 0))
        for g in range(2):
            w = w + rows[pl.ds(g * gy * gz + s * (gz - 1), gy, stride=gz), :]
        for j in range(2):
            pair[j] = pair[j] + jnp.where(labels[s] == 2 * me + j, w, 0.0)
    total = [jnp.sum(p) for p in pair]
    grad[...] = jnp.where(iota((1, 2), 1) == 0, total[0], total[1])


def sum_kernel(main, extra, out):
    out[0] = main[...] + extra[...]


def wall_response():
    def near_sum(f):
        g = np.pad(f, ((0, 0), (1, 1), (1, 1), (0, 0)))
        t = g[:, 2:, 1:-1] + g[:, :-2, 1:-1] + g[:, 1:-1, 2:] + g[:, 1:-1, :-2]
        return t + np.roll(f, 1, 3) + np.roll(f, -1, 3)

    def diff(f):
        g = np.pad(f, ((0, 0), (0, 0), (1, 1), (0, 0)))
        return g[:, :, 2:] - g[:, :, :-2]

    def sums(blocks, at):
        ghost = np.zeros((TY, blocks * ROWS, 13, LANES))
        for t in range(TY):
            ghost[t, at * ROWS + 8 * t:at * ROWS + 8 * t + 8, 0, 0:8] = 1.0
        u, p, states = np.zeros_like(ghost), np.zeros_like(ghost), []
        for _ in range(2):
            source = 0.5 * diff(u)
            for _ in range(2):
                p = (near_sum(p) + ghost - source) / 6.0
            u = 0.35 * u + 0.1 * near_sum(u) + 0.5 * diff(p)
            states.append(u)
        a, q, wall = np.zeros_like(ghost), np.zeros_like(ghost), 0.0
        for u in reversed(states):
            a = a + u
            spread, total = q - 0.5 * diff(a), 0.0
            for _ in range(2):
                total = total + spread / 6.0
                spread = near_sum(spread) / 6.0
            a = 0.35 * a + 0.1 * near_sum(a) + 0.5 * diff(total)
            q = spread
            wall = wall + total[:, :, 0]
        return wall.reshape(TY, blocks, TY, 8, 16, 8).sum((3, 5))

    def matrix(got):
        m = np.zeros((LANES, LANES), np.float32)
        for t in range(TY):
            for x in range(16):
                m[t * 16 + x, 0:TY * 16] = np.roll(got[t], x, 1).reshape(-1)
        return m

    middle, low, high = sums(3, 1), sums(2, 0), sums(2, 1)
    return np.concatenate([matrix(middle[:, 1]), matrix(middle[:, 2]), matrix(middle[:, 0]),
                           matrix(low[:, 0]), matrix(high[:, 1])], axis=1)


def vmem(n):
    return [pl.BlockSpec(memory_space=pltpu.VMEM)] * n


def shape(*dims):
    return jax.ShapeDtypeStruct(dims, jnp.float32)


def scratch(count, depth):
    return [pltpu.VMEM((EXT, depth, LANES), jnp.float32)] * count


def shifted(array, axis, by):
    count = lax.axis_size(axis)
    pairs = [(i, i + by) for i in range(count) if 0 <= i + by < count]
    return lax.ppermute(array, axis, pairs)


def per_device(response, field_pairs, tile_owner, electrode_volts):
    own = field_pairs[0]
    labels = tile_owner[..., 0]
    gy, gz = lax.axis_index("gy"), lax.axis_index("gz")
    devices = lax.axis_size(AXES)
    roomy = pltpu.CompilerParams(vmem_limit_bytes=40 * 1024 * 1024)
    middling = pltpu.CompilerParams(vmem_limit_bytes=24 * 1024 * 1024)
    tight = pltpu.CompilerParams(vmem_limit_bytes=8 * 1024 * 1024)
    block = shape(2, ROWS, COLS, LANES)

    low, high, up, dn = pl.pallas_call(
        pack_kernel,
        out_shape=(shape(2, HY, COLS, LANES),) * 2 + (shape(2, ROWS * 3 // 2, 8, LANES),) * 2,
        in_specs=vmem(1), out_specs=vmem(4), compiler_params=tight,
    )(own)
    yd = shifted(high, "gy", 1)
    yu = shifted(low, "gy", -1)
    zd = shifted(up, "gz", 1)
    zu = shifted(dn, "gz", -1)
    up, dn = pl.pallas_call(
        corner_kernel, out_shape=(shape(2, 3 * HY, 8, LANES),) * 2,
        in_specs=vmem(2), out_specs=vmem(2), compiler_params=tight,
    )(yd, yu)
    cd = shifted(up, "gz", 1)
    cu = shifted(dn, "gz", -1)

    row = pl.pallas_call(
        wall_kernel, out_shape=shape(devices, LANES),
        in_specs=vmem(3) + [pl.BlockSpec(memory_space=pltpu.SMEM)], out_specs=vmem(1)[0],
        scratch_shapes=scratch(13, COLS) + [pltpu.VMEM((8, LANES), jnp.float32), pltpu.VMEM((1, LANES), jnp.float32)],
        compiler_params=middling,
    )(own, yd, yu, electrode_volts)
    rows = lax.all_to_all(row, AXES, 0, 0, tiled=True)

    main, send = pl.pallas_call(
        bulk_kernel, out_shape=(block, block), in_specs=vmem(7), out_specs=vmem(2),
        scratch_shapes=scratch(13, ZE), compiler_params=roomy,
    )(own, yd, yu, zd, zu, cd, cu)
    extra = lax.ppermute(send, "grp", [(0, 1)])

    fenced = jnp.pad(labels, ((0, 0), (1, 1), (0, 0)), constant_values=-1)
    side = (gz == lax.axis_size("gz") - 1).astype(jnp.int32)
    near = lax.dynamic_slice(fenced, (side, gy * TY, 0), (1, 8, 16)).reshape(1, LANES)
    by_block = jnp.pad(labels.reshape(2, 8, TY * 16), ((0, 0), (0, 0), (0, LANES - TY * 16)), constant_values=-1)
    main, grad = pl.pallas_call(
        volts_kernel, out_shape=(block, shape(1, 2)), in_specs=vmem(5), out_specs=vmem(2),
        scratch_shapes=scratch(13, COLS), compiler_params=middling,
    )(main, rows, near, by_block, response)
    advanced = pl.pallas_call(
        sum_kernel, out_shape=shape(1, 2, ROWS, COLS, LANES), in_specs=vmem(2), out_specs=vmem(1)[0],
        compiler_params=tight,
    )(main, extra)
    return (advanced, grad.reshape(2))


def solution(mesh):
    response = jnp.asarray(wall_response())
    placed = (P("grp", None, "gy", "gz", None), P(), P(AXES))
    return jax.shard_map(
        functools.partial(per_device, response), mesh=mesh, in_specs=placed,
        out_specs=(P("grp", None, "gy", "gz", None), P(AXES)), check_vma=False,
    )
```

time: 109 us -> 84.7 us (0.78)
  Pallas kernels: 32.2 us -> 21 us
  waiting for transfers between devices: 33.5 us -> 25.8 us
  local copies, waits for them, and re-layouts: 4.21 us -> 1.54 us
  starting transfers between devices: 37.9 us -> 35.3 us
    all_to_all x2 -> x1, waiting for transfers between devices: 28.2 us -> 15.4 us  [per_device(): rows = lax.all_to_all(row, AXES, 0, 0, tiled=True)]
    pallas_call x3 -> x6, Pallas kernels: 32.2 us -> 21 us  [the longest x1 9.91 us: per_device(): pl.pallas_call(bulk_kernel, out_shape=(block, block), in_specs=vmem(7), o...]
    all_to_all x2 -> x1, starting transfers between devices: 23.6 us -> 15.3 us  [per_device(): rows = lax.all_to_all(row, AXES, 0, 0, tiled=True)]
    ppermute x4 -> x6, starting transfers between devices: 12.9 us -> 18.6 us  [shifted(): return lax.ppermute(array, axis, pairs)]
    ppermute x4 -> x6, waiting for transfers between devices: 5.26 us -> 10.4 us  [shifted(): return lax.ppermute(array, axis, pairs)]
    broadcast_in_dim x2 -> x0, local copies, waits for them, and re-layouts: 1.44 us -> none  [to_all(): jnp.broadcast_to(row, (n, LANES))]
  transfers between devices with their start and end apart: 7 -> 8, of which waited for: 3 -> 4; matrix products, arithmetic and copies ran while one was open for 2% -> 0% of each run, Pallas kernels for 0% -> 12%
where the time goes in v2:
time: 84.7 us; the launch traced here: 84.4 us
  starting transfers between devices  35.3 us (42%)
  waiting for transfers between devices  25.8 us (30%)
  Pallas kernels  21 us (25%)
  local copies, waits for them, and re-layouts  1.54 us (2%)
    ppermute x6, starting transfers between devices, shifted(): return lax.ppermute(array, axis, pairs)  18.6 us
    all_to_all x1, waiting for transfers between devices, per_device(): rows = lax.all_to_all(row, AXES, 0, 0, tiled=True)  15.4 us
    all_to_all x1, starting transfers between devices, per_device(): rows = lax.all_to_all(row, AXES, 0, 0, tiled=True)  15.3 us
    ppermute x6, waiting for transfers between devices, shifted(): return lax.ppermute(array, axis, pairs)  10.4 us
    pallas_call x1, Pallas kernels, per_device(): pl.pallas_call(bulk_kernel, out_shape=(block, block), in_specs=vmem(7), o...  9.91 us
    pallas_call x1, Pallas kernels, per_device(): pl.pallas_call(wall_kernel, out_shape=shape(devices, LANES), in_specs=vme...  6.03 us
    pallas_call x1, Pallas kernels, per_device(): pl.pallas_call(volts_kernel, out_shape=(block, shape(1, 2)), in_specs=vme...  3.94 us
  transfers between devices with their start and end apart: 8, of which 4 were waited for; matrix products, arithmetic and copies ran while one was open for 0% of the time, Pallas kernels for 12%

profile of v2, /device:TPU:1, one launch (start us, length us, event | category | flops | bytes accessed | tf_op | source)
XLA Modules:
  0.0 84.4 jit_solution(10728505579411643739)
XLA Ops:
  0.6 1.1 %copy-done = f32[1,2,48,16,128]{4,3,2,1,0:T(8,128)S(1)} copy-done((f32[1,2,48,16,128]{4,3,2,1,0:T(8,128)S(1)}, f32[1,2,48,16,128]{4,3,2,1,0:T(8,128)}, u32[]{:S(2)}) %copy-start) | copy-done | bytes 786456
  1.8 0.1 shard_map.59
  1.9 4.1 %collective-permute-start.2 = (f32[2,72,8,128]{3,2,1,0:T(8,128)S(1)}, f32[2,72,8,128]{3,2,1,0:T(8,128)S(1)}, u32[]{:S(2)}, u32[]{:S(2)}) collective-permute-start(f32[2,72,8,128]{3,2,1,0:T(8,128)S(1)} %get-tuple-element.14), channel_id=1, source_target_pairs={{0,1},{1,2},{2,3},{3,4},{4,5},{5,6},{6,7},{7,8},{8,9},{9,10},{10,1... | collective-permute-start | bytes 1769480 | tf_op jit(solution)/shard_map/ppermute | solution.py:449
  6.0 1.3 %collective-permute-start.3 = (f32[2,72,8,128]{3,2,1,0:T(8,128)S(1)}, f32[2,72,8,128]{3,2,1,0:T(8,128)S(1)}, u32[]{:S(2)}, u32[]{:S(2)}) collective-permute-start(f32[2,72,8,128]{3,2,1,0:T(8,128)S(1)} %get-tuple-element.15), channel_id=1, source_target_pairs={{1,0},{2,1},{3,2},{4,3},{5,4},{6,5},{7,6},{8,7},{9,8},{10,9},{11,1... | collective-permute-start | bytes 1769480 | tf_op jit(solution)/shard_map/ppermute | solution.py:449
  7.3 5.7 %collective-permute-start = (f32[2,8,16,128]{3,2,1,0:T(8,128)S(1)}, f32[2,8,16,128]{3,2,1,0:T(8,128)S(1)}, u32[]{:S(2)}, u32[]{:S(2)}) collective-permute-start(f32[2,8,16,128]{3,2,1,0:T(8,128)S(1)} %get-tuple-element.12), channel_id=1, source_target_pairs={{0,16},{16,32},{32,48},{48,64},{64,80},{80,96},{96,112},{1,17},{17... | collective-permute-start | bytes 393224 | tf_op jit(solution)/shard_map/ppermute | solution.py:449
  13.1 1.9 %collective-permute-start.1 = (f32[2,8,16,128]{3,2,1,0:T(8,128)S(1)}, f32[2,8,16,128]{3,2,1,0:T(8,128)S(1)}, u32[]{:S(2)}, u32[]{:S(2)}) collective-permute-start(f32[2,8,16,128]{3,2,1,0:T(8,128)S(1)} %get-tuple-element.13), channel_id=1, source_target_pairs={{16,0},{32,16},{48,32},{64,48},{80,64},{96,80},{112,96},{17,1},{33... | collective-permute-start | bytes 393224 | tf_op jit(solution)/shard_map/ppermute | solution.py:449
  15.0 5.3 %collective-permute-done.1.yu = f32[2,8,16,128]{3,2,1,0:T(8,128)S(1)} collective-permute-done((f32[2,8,16,128]{3,2,1,0:T(8,128)S(1)}, f32[2,8,16,128]{3,2,1,0:T(8,128)S(1)}, u32[]{:S(2)}, u32[]{:S(2)}) %collective-permute-start.1) | collective-permute-done | bytes 131104 | tf_op jit(solution)/shard_map/ppermute | solution.py:449
  20.3 4.3 %collective-permute-start.4 = (f32[2,24,8,128]{3,2,1,0:T(8,128)S(1)}, f32[2,24,8,128]{3,2,1,0:T(8,128)S(1)}, u32[]{:S(2)}, u32[]{:S(2)}) collective-permute-start(f32[2,24,8,128]{3,2,1,0:T(8,128)S(1)} %get-tuple-element.16), channel_id=1, source_target_pairs={{0,1},{1,2},{2,3},{3,4},{4,5},{5,6},{6,7},{7,8},{8,9},{9,10},{10,1... | collective-permute-start | bytes 589832 | tf_op jit(solution)/shard_map/ppermute | solution.py:449
  24.6 1.3 %collective-permute-start.5 = (f32[2,24,8,128]{3,2,1,0:T(8,128)S(1)}, f32[2,24,8,128]{3,2,1,0:T(8,128)S(1)}, u32[]{:S(2)}, u32[]{:S(2)}) collective-permute-start(f32[2,24,8,128]{3,2,1,0:T(8,128)S(1)} %get-tuple-element.17), channel_id=1, source_target_pairs={{1,0},{2,1},{3,2},{4,3},{5,4},{6,5},{7,6},{8,7},{9,8},{10,9},{11,1... | collective-permute-start | bytes 589832 | tf_op jit(solution)/shard_map/ppermute | solution.py:449
  25.9 1.3 %collective-permute-done.4.cd = f32[2,24,8,128]{3,2,1,0:T(8,128)S(1)} collective-permute-done((f32[2,24,8,128]{3,2,1,0:T(8,128)S(1)}, f32[2,24,8,128]{3,2,1,0:T(8,128)S(1)}, u32[]{:S(2)}, u32[]{:S(2)}) %collective-permute-start.4) | collective-permute-done | bytes 196640 | tf_op jit(solution)/shard_map/ppermute | solution.py:449
  27.2 3.8 %collective-permute-done.5.cu = f32[2,24,8,128]{3,2,1,0:T(8,128)S(1)} collective-permute-done((f32[2,24,8,128]{3,2,1,0:T(8,128)S(1)}, f32[2,24,8,128]{3,2,1,0:T(8,128)S(1)}, u32[]{:S(2)}, u32[]{:S(2)}) %collective-permute-start.5) | collective-permute-done | bytes 196640 | tf_op jit(solution)/shard_map/ppermute | solution.py:449
  31.0 9.9 %shard_map.61 = (f32[2,48,16,128]{3,2,1,0:T(8,128)S(1)}, f32[2,48,16,128]{3,2,1,0:T(8,128)S(1)}) custom-call(f32[2,48,16,128]{3,2,1,0:T(8,128)S(1)} %bitcast.12, f32[2,8,16,128]{3,2,1,0:T(8,128)S(1)} %collective-permute-done.yd, f32[2,8,16,128]{3,2,1,0:T(8,128)S(1)} %collective-permute-done.1.yu, f32[2,72,8,128]{3,2,1,0:T(8,128)S(1)} %collective-permute-done.2.zd, ...), custom_call_target="tpu_custom_call" | custom-call | tf_op jit(solution)/shard_map/pallas_call | solution.py:486
  40.9 0.0 copy-start.3
  41.0 1.3 %collective-permute-start.6 = (f32[2,48,16,128]{3,2,1,0:T(8,128)S(1)}, f32[2,48,16,128]{3,2,1,0:T(8,128)S(1)}, u32[]{:S(2)}, u32[]{:S(2)}) collective-permute-start(f32[2,48,16,128]{3,2,1,0:T(8,128)S(1)} %get-tuple-element.20), channel_id=1, source_target_pairs={{0,128},{1,129},{2,130},{3,131},{4,132},{5,133},{6,134},{7,135},{8... | collective-permute-start | bytes 2359304 | tf_op jit(solution)/shard_map/ppermute | solution.py:490
  42.3 6.0 %shard_map.62 = f32[256,128]{1,0:T(8,128)} custom-call(f32[2,48,16,128]{3,2,1,0:T(8,128)S(1)} %bitcast.13, f32[2,8,16,128]{3,2,1,0:T(8,128)S(1)} %collective-permute-done.yd, f32[2,8,16,128]{3,2,1,0:T(8,128)S(1)} %collective-permute-done.1.yu, f32[2]{0:T(128)S(1)} %copy-done.3), custom_call_target="tpu_custom_call" | custom-call | tf_op jit(solution)/shard_map/pallas_call | solution.py:478
  48.3 15.3 %all-to-all-start = ((f32[256,1,128]{2,1,0:T(1,128)}), f32[256,1,128]{2,1,0:T(1,128)S(1)}, u32[]{:S(2)}, u32[]{:S(2)}) async-start(f32[256,1,128]{2,1,0:T(1,128)} %bitcast.2), calls=%async_computation | async-start | bytes 262144 | tf_op jit(solution)/shard_map/all_to_all | solution.py:484
  63.7 0.1 copy.12
  63.7 0.1 pad_dynamic-slice_fusion
  63.8 0.1 copy.11
  63.9 0.1 reshape.12.near
  64.0 0.1 reshape_squeeze.3
  64.1 15.4 %all-to-all-done = f32[256,1,128]{2,1,0:T(1,128)S(1)} async-done(((f32[256,1,128]{2,1,0:T(1,128)}), f32[256,1,128]{2,1,0:T(1,128)S(1)}, u32[]{:S(2)}, u32[]{:S(2)}) %all-to-all-start) | async-done | bytes 131104 | tf_op jit(solution)/shard_map/all_to_all | solution.py:484
  79.5 3.9 %shard_map.63 = (f32[2,48,16,128]{3,2,1,0:T(8,128)S(1)}, f32[1,2]{1,0:T(1,128)}) custom-call(f32[2,48,16,128]{3,2,1,0:T(8,128)S(1)} %get-tuple-element.18.main, f32[256,128]{1,0:T(8,128)S(1)} %bitcast.14, s32[1,128]{1,0:T(1,128)S(1)} %reshape.12.near, s32[2,8,128]{2,1,0:T(8,128)S(1)} %pad.9.labels, f32[128,640]{1,0:T(8,128)S(1)} %copy-done.2), custom_call_target="tpu_custom_call" | custom-call | tf_op jit(solution)/shard_map/pallas_call | solution.py:496
  83.4 1.0 %shard_map.64 = f32[1,2,48,16,128]{4,3,2,1,0:T(8,128)} custom-call(f32[2,48,16,128]{3,2,1,0:T(8,128)S(1)} %get-tuple-element.19.main, f32[2,48,16,128]{3,2,1,0:T(8,128)S(1)} %collective-permute-done.6.extra), custom_call_target="tpu_custom_call" | custom-call | tf_op jit(solution)/shard_map/pallas_call | solution.py:500
  (14 shorter events, 0.1 us)
Async XLA Ops:
  0.6 1.1 %copy-start = (f32[1,2,48,16,128]{4,3,2,1,0:T(8,128)S(1)}, f32[1,2,48,16,128]{4,3,2,1,0:T(8,128)}, u32[]{:S(2)}) copy-start(f32[1,2,48,16,128]{4,3,2,1,0:T(8,128)} %param.4) | copy-start | bytes 2359300
  1.8 29.3 %copy-start.1 = (f32[1,2,48,16,128]{4,3,2,1,0:T(8,128)S(1)}, f32[1,2,48,16,128]{4,3,2,1,0:T(8,128)}, u32[]{:S(2)}) copy-start(f32[1,2,48,16,128]{4,3,2,1,0:T(8,128)} %param.4) | copy-start | bytes 2359300
  1.9 29.1 %collective-permute-start.2 = (f32[2,72,8,128]{3,2,1,0:T(8,128)S(1)}, f32[2,72,8,128]{3,2,1,0:T(8,128)S(1)}, u32[]{:S(2)}, u32[]{:S(2)}) collective-permute-start(f32[2,72,8,128]{3,2,1,0:T(8,128)S(1)} %get-tuple-element.14), channel_id=1, source_target_pairs={{0,1},{1,2},{2,3},{3,4},{4,5},{5,6},{6,7},{7,8},{8,9},{9,10},{10,1... | collective-permute-start | bytes 1769480 | tf_op jit(solution)/shard_map/ppermute | solution.py:449
  6.0 25.0 %collective-permute-start.3 = (f32[2,72,8,128]{3,2,1,0:T(8,128)S(1)}, f32[2,72,8,128]{3,2,1,0:T(8,128)S(1)}, u32[]{:S(2)}, u32[]{:S(2)}) collective-permute-start(f32[2,72,8,128]{3,2,1,0:T(8,128)S(1)} %get-tuple-element.15), channel_id=1, source_target_pairs={{1,0},{2,1},{3,2},{4,3},{5,4},{6,5},{7,6},{8,7},{9,8},{10,9},{11,1... | collective-permute-start | bytes 1769480 | tf_op jit(solution)/shard_map/ppermute | solution.py:449
  7.3 7.7 %collective-permute-start = (f32[2,8,16,128]{3,2,1,0:T(8,128)S(1)}, f32[2,8,16,128]{3,2,1,0:T(8,128)S(1)}, u32[]{:S(2)}, u32[]{:S(2)}) collective-permute-start(f32[2,8,16,128]{3,2,1,0:T(8,128)S(1)} %get-tuple-element.12), channel_id=1, source_target_pairs={{0,16},{16,32},{32,48},{48,64},{64,80},{80,96},{96,112},{1,17},{17... | collective-permute-start | bytes 393224 | tf_op jit(solution)/shard_map/ppermute | solution.py:449
  13.1 7.2 %collective-permute-start.1 = (f32[2,8,16,128]{3,2,1,0:T(8,128)S(1)}, f32[2,8,16,128]{3,2,1,0:T(8,128)S(1)}, u32[]{:S(2)}, u32[]{:S(2)}) collective-permute-start(f32[2,8,16,128]{3,2,1,0:T(8,128)S(1)} %get-tuple-element.13), channel_id=1, source_target_pairs={{16,0},{32,16},{48,32},{64,48},{80,64},{96,80},{112,96},{17,1},{33... | collective-permute-start | bytes 393224 | tf_op jit(solution)/shard_map/ppermute | solution.py:449
  20.3 6.9 %collective-permute-start.4 = (f32[2,24,8,128]{3,2,1,0:T(8,128)S(1)}, f32[2,24,8,128]{3,2,1,0:T(8,128)S(1)}, u32[]{:S(2)}, u32[]{:S(2)}) collective-permute-start(f32[2,24,8,128]{3,2,1,0:T(8,128)S(1)} %get-tuple-element.16), channel_id=1, source_target_pairs={{0,1},{1,2},{2,3},{3,4},{4,5},{5,6},{6,7},{7,8},{8,9},{9,10},{10,1... | collective-permute-start | bytes 589832 | tf_op jit(solution)/shard_map/ppermute | solution.py:449
  24.6 6.4 %collective-permute-start.5 = (f32[2,24,8,128]{3,2,1,0:T(8,128)S(1)}, f32[2,24,8,128]{3,2,1,0:T(8,128)S(1)}, u32[]{:S(2)}, u32[]{:S(2)}) collective-permute-start(f32[2,24,8,128]{3,2,1,0:T(8,128)S(1)} %get-tuple-element.17), channel_id=1, source_target_pairs={{1,0},{2,1},{3,2},{4,3},{5,4},{6,5},{7,6},{8,7},{9,8},{10,9},{11,1... | collective-permute-start | bytes 589832 | tf_op jit(solution)/shard_map/ppermute | solution.py:449
  40.9 1.4 %copy-start.3 = (f32[2]{0:T(128)S(1)}, f32[2]{0:T(128)}, u32[]{:S(2)}) copy-start(f32[2]{0:T(128)} %volts.1) | copy-start | bytes 28
  41.0 42.5 %collective-permute-start.6 = (f32[2,48,16,128]{3,2,1,0:T(8,128)S(1)}, f32[2,48,16,128]{3,2,1,0:T(8,128)S(1)}, u32[]{:S(2)}, u32[]{:S(2)}) collective-permute-start(f32[2,48,16,128]{3,2,1,0:T(8,128)S(1)} %get-tuple-element.20), channel_id=1, source_target_pairs={{0,128},{1,129},{2,130},{3,131},{4,132},{5,133},{6,134},{7,135},{8... | collective-permute-start | bytes 2359304 | tf_op jit(solution)/shard_map/ppermute | solution.py:490
  42.3 21.3 %copy-start.4 = (s32[2,48,16,1]{1,3,2,0:T(1,128)S(1)}, s32[2,48,16,1]{1,3,2,0:T(1,128)}, u32[]{:S(2)}) copy-start(s32[2,48,16,1]{1,3,2,0:T(1,128)} %param.5) | copy-start | bytes 18436
  48.3 31.1 %copy-start.2 = (f32[128,640]{1,0:T(8,128)S(1)}, f32[128,640]{1,0:T(8,128)}, u32[]{:S(2)}) copy-start(f32[128,640]{1,0:T(8,128)} %constant.23.clone.response) | copy-start | bytes 983044
  48.3 31.1 %all-to-all-start = ((f32[256,1,128]{2,1,0:T(1,128)}), f32[256,1,128]{2,1,0:T(1,128)S(1)}, u32[]{:S(2)}, u32[]{:S(2)}) async-start(f32[256,1,128]{2,1,0:T(1,128)} %bitcast.2), calls=%async_computation | async-start | bytes 262144 | tf_op jit(solution)/shard_map/all_to_all | solution.py:484

commit v3 on v2

--- a/solution.py
+++ b/solution.py
@@ -199,46 +199,48 @@
     rows_loop(8, 55, stage_l)
 
 
-HALF = ROWS // 2
-
-
-def load_extended(dst, f, own, yd, yu, zd, zu, cd, cu):
+HALF = EXT // 2
+
+
+def load_extended(dst, f, own, yd, yu, zd, zu):
     top = HY + ROWS
     dst[0:HY, ZO:ZO + COLS, :] = yd[f]
     dst[HY:top, ZO:ZO + COLS, :] = own[f]
     dst[top:, ZO:ZO + COLS, :] = yu[f]
-    for z, c, near, far in ((zd, cd, 8, 4), (zu, cu, 32, 40)):
-        dst[HY:top, near:near + 8, :] = z[f, 0:ROWS]
-        dst[HY:HY + HALF, far:far + 4, :] = z[f, ROWS:, 0:4, :]
-        dst[HY + HALF:top, far:far + 4, :] = z[f, ROWS:, 4:8, :]
-        dst[0:HY, near:near + 8, :] = c[f, 0:HY]
-        dst[top:, near:near + 8, :] = c[f, HY:2 * HY]
-        dst[0:HY, far:far + 4, :] = c[f, 2 * HY:, 0:4, :]
-        dst[top:, far:far + 4, :] = c[f, 2 * HY:, 4:8, :]
+    for z, near, far in ((zd, 8, 4), (zu, 32, 40)):
+        dst[:, near:near + 8, :] = z[f, 0:EXT]
+        dst[0:HALF, far:far + 4, :] = z[f, EXT:, 0:4, :]
+        dst[HALF:, far:far + 4, :] = z[f, EXT:, 4:8, :]
     for z in (0, 44):
         dst[:, z:z + 4, :] = jnp.zeros((EXT, 4, LANES), jnp.float32)
 
 
-def pack_kernel(own, low, high, up, dn):
-    low[...] = own[:, 0:HY]
-    high[...] = own[:, ROWS - HY:]
-    up[:, 0:ROWS] = own[:, :, 8:16, :]
-    up[:, ROWS:, 0:4, :] = own[:, 0:HALF, 4:8, :]
-    up[:, ROWS:, 4:8, :] = own[:, HALF:, 4:8, :]
-    dn[:, 0:ROWS] = own[:, :, 0:8, :]
-    dn[:, ROWS:, 0:4, :] = own[:, 0:HALF, 8:12, :]
-    dn[:, ROWS:, 4:8, :] = own[:, HALF:, 8:12, :]
-
-
-def corner_kernel(yd, yu, up, dn):
-    up[:, 0:HY] = yd[:, :, 8:16, :]
-    up[:, HY:2 * HY] = yu[:, :, 8:16, :]
-    up[:, 2 * HY:, 0:4, :] = yd[:, :, 4:8, :]
-    up[:, 2 * HY:, 4:8, :] = yu[:, :, 4:8, :]
-    dn[:, 0:HY] = yd[:, :, 0:8, :]
-    dn[:, HY:2 * HY] = yu[:, :, 0:8, :]
-    dn[:, 2 * HY:, 0:4, :] = yd[:, :, 8:12, :]
-    dn[:, 2 * HY:, 4:8, :] = yu[:, :, 8:12, :]
+def is_even(axis):
+    return lax.rem(lax.axis_index(axis), 2) == 0
+
+
+def pack_kernel(own, far, near, yd, yu, z_near, z_far):
+    even = is_even("gy")
+    yd[...] = jnp.where(even, far[...], near[...])
+    yu[...] = jnp.where(even, near[...], far[...])
+
+    def pack(dst, whole, part):
+        for r0, r1, src in ((0, HY, yd), (HY, HY + ROWS, own), (HY + ROWS, EXT, yu)):
+            dst[:, r0:r1] = src[:, :, whole:whole + 8, :]
+        dst[:, EXT:EXT + HY, 0:4, :] = yd[:, :, part:part + 4, :]
+        dst[:, EXT + HY:, 0:4, :] = own[:, 0:HALF - HY, part:part + 4, :]
+        dst[:, EXT:EXT + HALF - HY, 4:8, :] = own[:, HALF - HY:, part:part + 4, :]
+        dst[:, EXT + HALF - HY:, 4:8, :] = yu[:, :, part:part + 4, :]
+
+    @pl.when(is_even("gz"))
+    def _():
+        pack(z_near, 8, 4)
+        pack(z_far, 0, 8)
+
+    @pl.when(jnp.logical_not(is_even("gz")))
+    def _():
+        pack(z_near, 0, 8)
+        pack(z_far, 8, 4)
 
 
 HIGHEST = lax.Precision.HIGHEST
@@ -310,11 +312,18 @@
     row[...] = jnp.broadcast_to(out, row.shape)
 
 
-def bulk_kernel(own, yd, yu, zd, zu, cd, cu, main, send, U, V, SRC, B, Q, U1, A, SP, S2, T, A1, S3, T2):
+def bulk_kernel(own, yd, yu, far, near, main, send, U, V, SRC, B, Q, U1, A, SP, S2, T, A1, S3, T2):
     edge = edges()
     is_forward = lax.axis_index("grp") == 0
-    load_extended(U, 0, own, yd, yu, zd, zu, cd, cu)
-    load_extended(V, 1, own, yd, yu, zd, zu, cd, cu)
+    @pl.when(is_even("gz"))
+    def _():
+        load_extended(U, 0, own, yd, yu, far, near)
+        load_extended(V, 1, own, yd, yu, far, near)
+
+    @pl.when(jnp.logical_not(is_even("gz")))
+    def _():
+        load_extended(U, 0, own, yd, yu, near, far)
+        load_extended(V, 1, own, yd, yu, near, far)
 
     def into(ref):
         def give(rows, u, p):
@@ -443,9 +452,10 @@
     return [pltpu.VMEM((EXT, depth, LANES), jnp.float32)] * count
 
 
-def shifted(array, axis, by):
-    count = lax.axis_size(axis)
-    pairs = [(i, i + by) for i in range(count) if 0 <= i + by < count]
+def swapped(array, axis, first):
+    pairs = []
+    for i in range(first, lax.axis_size(axis) - 1, 2):
+        pairs += [(i, i + 1), (i + 1, i)]
     return lax.ppermute(array, axis, pairs)
 
 
@@ -459,44 +469,44 @@
     tight = pltpu.CompilerParams(vmem_limit_bytes=8 * 1024 * 1024)
     block = shape(2, ROWS, COLS, LANES)
 
-    low, high, up, dn = pl.pallas_call(
-        pack_kernel,
-        out_shape=(shape(2, HY, COLS, LANES),) * 2 + (shape(2, ROWS * 3 // 2, 8, LANES),) * 2,
-        in_specs=vmem(1), out_specs=vmem(4), compiler_params=tight,
-    )(own)
-    yd = shifted(high, "gy", 1)
-    yu = shifted(low, "gy", -1)
-    zd = shifted(up, "gz", 1)
-    zu = shifted(dn, "gz", -1)
-    up, dn = pl.pallas_call(
-        corner_kernel, out_shape=(shape(2, 3 * HY, 8, LANES),) * 2,
-        in_specs=vmem(2), out_specs=vmem(2), compiler_params=tight,
-    )(yd, yu)
-    cd = shifted(up, "gz", 1)
-    cu = shifted(dn, "gz", -1)
-
+    even = is_even("gy")
+    low, high = own[:, :HY], own[:, ROWS - HY:]
+    far = swapped(jnp.where(even, low, high), "gy", 1)
+    near = swapped(jnp.where(even, high, low), "gy", 0)
+    rows_of, strip = shape(2, HY, COLS, LANES), shape(2, EXT * 3 // 2, 8, LANES)
+    yd, yu, z_near, z_far = pl.pallas_call(
+        pack_kernel, out_shape=(rows_of, rows_of, strip, strip),
+        in_specs=vmem(3), out_specs=vmem(4), compiler_params=tight,
+    )(own, far, near)
+    far = swapped(z_far, "gz", 1)
+    near = swapped(z_near, "gz", 0)
+
+    mine, _ = lax.optimization_barrier((own, z_far))
     row = pl.pallas_call(
         wall_kernel, out_shape=shape(devices, LANES),
         in_specs=vmem(3) + [pl.BlockSpec(memory_space=pltpu.SMEM)], out_specs=vmem(1)[0],
         scratch_shapes=scratch(13, COLS) + [pltpu.VMEM((8, LANES), jnp.float32), pltpu.VMEM((1, LANES), jnp.float32)],
         compiler_params=middling,
-    )(own, yd, yu, electrode_volts)
+    )(mine, yd, yu, electrode_volts)
     rows = lax.all_to_all(row, AXES, 0, 0, tiled=True)
 
+    mine, _ = lax.optimization_barrier((own, row))
     main, send = pl.pallas_call(
-        bulk_kernel, out_shape=(block, block), in_specs=vmem(7), out_specs=vmem(2),
+        bulk_kernel, out_shape=(block, block), in_specs=vmem(5), out_specs=vmem(2),
         scratch_shapes=scratch(13, ZE), compiler_params=roomy,
-    )(own, yd, yu, zd, zu, cd, cu)
+        cost_estimate=pl.CostEstimate(flops=10 ** 8, bytes_accessed=36 * 10 ** 6, transcendentals=0),
+    )(mine, yd, yu, far, near)
+    send, rows = lax.optimization_barrier((send, rows))
     extra = lax.ppermute(send, "grp", [(0, 1)])
 
     fenced = jnp.pad(labels, ((0, 0), (1, 1), (0, 0)), constant_values=-1)
     side = (gz == lax.axis_size("gz") - 1).astype(jnp.int32)
-    near = lax.dynamic_slice(fenced, (side, gy * TY, 0), (1, 8, 16)).reshape(1, LANES)
+    by_wall = lax.dynamic_slice(fenced, (side, gy * TY, 0), (1, 8, 16)).reshape(1, LANES)
     by_block = jnp.pad(labels.reshape(2, 8, TY * 16), ((0, 0), (0, 0), (0, LANES - TY * 16)), constant_values=-1)
     main, grad = pl.pallas_call(
         volts_kernel, out_shape=(block, shape(1, 2)), in_specs=vmem(5), out_specs=vmem(2),
         scratch_shapes=scratch(13, COLS), compiler_params=middling,
-    )(main, rows, near, by_block, response)
+    )(main, rows, by_wall, by_block, response)
     advanced = pl.pallas_call(
         sum_kernel, out_shape=shape(1, 2, ROWS, COLS, LANES), in_specs=vmem(2), out_specs=vmem(1)[0],
         compiler_params=tight,

time: 84.7 us -> 72.4 us (0.85)
  the two profiles are of different devices: /device:TPU:1 before, /device:TPU:32 now
where the time goes in v3:
time: 72.4 us; the launch traced here: 72.1 us
  starting transfers between devices  29.3 us (40%)
  waiting for transfers between devices  20.5 us (28%)
  Pallas kernels  16.6 us (23%)
  local copies, waits for them, and re-layouts  4.03 us (6%)
  other arithmetic  1 us (1%)
  between operations  0.75 us (1%)
    all_to_all x1, starting transfers between devices, per_device(): rows = lax.all_to_all(row, AXES, 0, 0, tiled=True)  17.6 us
    ppermute x1, waiting for transfers between devices, per_device(): extra = lax.ppermute(send, 'grp', [(0, 1)])  12.6 us
    ppermute x4, starting transfers between devices, swapped(): return lax.ppermute(array, axis, pairs)  10.3 us
    all_to_all x1, waiting for transfers between devices, per_device(): rows = lax.all_to_all(row, AXES, 0, 0, tiled=True)  6.87 us
    pallas_call x1, Pallas kernels, per_device(): pl.pallas_call(volts_kernel, out_shape=(block, shape(1, 2)), in_specs=vme...  6.26 us
    pallas_call x1, Pallas kernels, per_device(): pl.pallas_call(bulk_kernel, out_shape=(block, block), in_specs=vmem(5), o...  4.48 us
    unnamed x13, local copies, waits for them, and re-layouts  3.71 us
    pallas_call x1, Pallas kernels, per_device(): pl.pallas_call(wall_kernel, out_shape=shape(devices, LANES), in_specs=vme...  3.52 us
  transfers between devices with their start and end apart: 6, of which 3 were waited for; matrix products, arithmetic and copies ran while one was open for 1% of the time, Pallas kernels for 20%

profile of v3, /device:TPU:32, one launch (start us, length us, event | category | flops | bytes accessed | tf_op | source)
XLA Modules:
  0.0 72.1 jit_solution(8108865109015019387)
XLA Ops:
  0.6 1.0 %slice_select_fusion = (f32[2,8,16,128]{3,2,1,0:T(8,128)S(1)}, f32[2,8,16,128]{3,2,1,0:T(8,128)S(1)}) fusion(f32[2,48,16,128]{3,2,1,0:T(8,128)} %bitcast.11, pred[]{:T(512)S(6)} %eq.6), kind=kLoop, calls=%fused_computation | loop fusion | flops 65536 | bytes 524289 | tf_op jit(solution)/shard_map/jit(_where)/select_n | solution.py:475
  1.6 0.7 collective-permute-start
  2.3 4.7 %collective-permute-start.1 = (f32[2,8,16,128]{3,2,1,0:T(8,128)S(1)}, f32[2,8,16,128]{3,2,1,0:T(8,128)S(1)}, u32[]{:S(2)}, u32[]{:S(2)}) collective-permute-start(f32[2,8,16,128]{3,2,1,0:T(8,128)S(1)} %get-tuple-element.26), channel_id=1, source_target_pairs={{0,16},{16,0},{32,48},{48,32},{64,80},{80,64},{96,112},{112,96},{1... | collective-permute-start | bytes 393224 | tf_op jit(solution)/shard_map/ppermute | solution.py:459
  7.0 1.0 %collective-permute-done.1.near = f32[2,8,16,128]{3,2,1,0:T(8,128)S(1)} collective-permute-done((f32[2,8,16,128]{3,2,1,0:T(8,128)S(1)}, f32[2,8,16,128]{3,2,1,0:T(8,128)S(1)}, u32[]{:S(2)}, u32[]{:S(2)}) %collective-permute-start.1) | collective-permute-done | bytes 131104 | tf_op jit(solution)/shard_map/ppermute | solution.py:459
  8.0 1.1 %copy-done = f32[1,2,48,16,128]{4,3,2,1,0:T(8,128)S(1)} copy-done((f32[1,2,48,16,128]{4,3,2,1,0:T(8,128)S(1)}, f32[1,2,48,16,128]{4,3,2,1,0:T(8,128)}, u32[]{:S(2)}) %copy-start) | copy-done | bytes 786456
  9.2 1.3 %shard_map.59 = (f32[2,8,16,128]{3,2,1,0:T(8,128)S(1)}, f32[2,8,16,128]{3,2,1,0:T(8,128)S(1)}, f32[2,96,8,128]{3,2,1,0:T(8,128)}, f32[2,96,8,128]{3,2,1,0:T(8,128)}) custom-call(f32[2,48,16,128]{3,2,1,0:T(8,128)S(1)} %bitcast.12, f32[2,8,16,128]{3,2,1,0:T(8,128)S(1)} %collective-permute-done.far, f32[2,8,16,128]{3,2,1,0:T(8,128)S(1)} %collective-permute-done.1.near), custom_call_target="tpu_custom_call" | custom-call | tf_op jit(solution)/shard_map/pallas_call | solution.py:477
  10.5 0.7 collective-permute-start.2
  11.2 4.3 %collective-permute-start.3 = (f32[2,96,8,128]{3,2,1,0:T(8,128)}, f32[2,96,8,128]{3,2,1,0:T(8,128)S(1)}, u32[]{:S(2)}, u32[]{:S(2)}) collective-permute-start(f32[2,96,8,128]{3,2,1,0:T(8,128)} %get-tuple-element.19), channel_id=1, source_target_pairs={{0,1},{1,0},{2,3},{3,2},{4,5},{5,4},{6,7},{7,6},{8,9},{9,8},{10,11... | collective-permute-start | bytes 2359304 | tf_op jit(solution)/shard_map/ppermute | solution.py:459
  15.5 0.7 copy-done.3
  16.1 3.5 %shard_map.60 = f32[256,128]{1,0:T(8,128)} custom-call(f32[2,48,16,128]{3,2,1,0:T(8,128)S(1)} %bitcast.13, f32[2,8,16,128]{3,2,1,0:T(8,128)S(1)} %get-tuple-element.16.yd, f32[2,8,16,128]{3,2,1,0:T(8,128)S(1)} %get-tuple-element.17.yu, f32[2]{0:T(128)S(1)} %copy-done.3), custom_call_target="tpu_custom_call" | custom-call | tf_op jit(solution)/shard_map/pallas_call | solution.py:485
  19.7 17.6 %all-to-all-start = ((f32[256,1,128]{2,1,0:T(1,128)}), f32[256,1,128]{2,1,0:T(1,128)S(1)}, u32[]{:S(2)}, u32[]{:S(2)}) async-start(f32[256,1,128]{2,1,0:T(1,128)} %bitcast.2), calls=%async_computation | async-start | bytes 262144 | tf_op jit(solution)/shard_map/all_to_all | solution.py:491
  37.3 4.5 %shard_map.61 = (f32[2,48,16,128]{3,2,1,0:T(8,128)S(1)}, f32[2,48,16,128]{3,2,1,0:T(8,128)S(1)}) custom-call(f32[2,48,16,128]{3,2,1,0:T(8,128)S(1)} %bitcast.14, f32[2,8,16,128]{3,2,1,0:T(8,128)S(1)} %get-tuple-element.16.yd, f32[2,8,16,128]{3,2,1,0:T(8,128)S(1)} %get-tuple-element.17.yu, f32[2,96,8,128]{3,2,1,0:T(8,128)S(1)} %collective-permute-done.2.far, ...), custom_call_target="tpu_custom_call" | custom-call | flops 100000000 | bytes 36000000 | tf_op jit(solution)/shard_map/pallas_call | solution.py:494
  41.8 0.9 %copy-done.4 = f32[2,48,16,128]{3,2,1,0:T(8,128)} copy-done((f32[2,48,16,128]{3,2,1,0:T(8,128)}, f32[2,48,16,128]{3,2,1,0:T(8,128)S(1)}, u32[]{:S(2)}) %copy-start.4) | copy-done | bytes 786456
  42.7 6.9 %all-to-all-done = f32[256,1,128]{2,1,0:T(1,128)S(1)} async-done(((f32[256,1,128]{2,1,0:T(1,128)}), f32[256,1,128]{2,1,0:T(1,128)S(1)}, u32[]{:S(2)}, u32[]{:S(2)}) %all-to-all-start) | async-done | bytes 131104 | tf_op jit(solution)/shard_map/all_to_all | solution.py:491
  49.6 1.3 %collective-permute-start.4 = (f32[2,48,16,128]{3,2,1,0:T(8,128)}, f32[2,48,16,128]{3,2,1,0:T(8,128)S(1)}, u32[]{:S(2)}, u32[]{:S(2)}) collective-permute-start(f32[2,48,16,128]{3,2,1,0:T(8,128)} %copy-done.4), channel_id=1, source_target_pairs={{0,128},{1,129},{2,130},{3,131},{4,132},{5,133},{6,134},{7,135},{8... | collective-permute-start | bytes 2359304 | tf_op jit(solution)/shard_map/ppermute | solution.py:500
  50.9 0.1 copy.12
  50.9 0.1 pad_dynamic-slice_fusion
  51.0 0.1 copy.11
  51.1 0.1 reshape.12.near
  51.2 0.1 reshape_squeeze.3
  51.3 1.0 %copy-done.2 = f32[128,640]{1,0:T(8,128)S(1)} copy-done((f32[128,640]{1,0:T(8,128)S(1)}, f32[128,640]{1,0:T(8,128)}, u32[]{:S(2)}) %copy-start.2) | copy-done | bytes 327704
  52.2 6.3 %shard_map.62 = (f32[2,48,16,128]{3,2,1,0:T(8,128)S(1)}, f32[1,2]{1,0:T(1,128)}) custom-call(f32[2,48,16,128]{3,2,1,0:T(8,128)S(1)} %get-tuple-element.20.main, f32[256,128]{1,0:T(8,128)S(1)} %bitcast.15, s32[1,128]{1,0:T(1,128)S(1)} %reshape.12.near, s32[2,8,128]{2,1,0:T(8,128)S(1)} %pad.9.labels, f32[128,640]{1,0:T(8,128)S(1)} %copy-done.2), custom_call_target="tpu_custom_call" | custom-call | tf_op jit(solution)/shard_map/pallas_call | solution.py:506
  58.5 12.6 %collective-permute-done.4.extra = f32[2,48,16,128]{3,2,1,0:T(8,128)S(1)} collective-permute-done((f32[2,48,16,128]{3,2,1,0:T(8,128)}, f32[2,48,16,128]{3,2,1,0:T(8,128)S(1)}, u32[]{:S(2)}, u32[]{:S(2)}) %collective-permute-start.4) | collective-permute-done | bytes 786464 | tf_op jit(solution)/shard_map/ppermute | solution.py:500
  71.1 1.0 %shard_map.63 = f32[1,2,48,16,128]{4,3,2,1,0:T(8,128)} custom-call(f32[2,48,16,128]{3,2,1,0:T(8,128)S(1)} %get-tuple-element.23.main, f32[2,48,16,128]{3,2,1,0:T(8,128)S(1)} %collective-permute-done.4.extra), custom_call_target="tpu_custom_call" | custom-call | tf_op jit(solution)/shard_map/pallas_call | solution.py:510
  (12 shorter events, 0.0 us)
Async XLA Ops:
  1.6 5.4 %collective-permute-start = (f32[2,8,16,128]{3,2,1,0:T(8,128)S(1)}, f32[2,8,16,128]{3,2,1,0:T(8,128)S(1)}, u32[]{:S(2)}, u32[]{:S(2)}) collective-permute-start(f32[2,8,16,128]{3,2,1,0:T(8,128)S(1)} %get-tuple-element.27), channel_id=1, source_target_pairs={{16,32},{32,16},{48,64},{64,48},{80,96},{96,80},{17,33},{33,17},{4... | collective-permute-start | bytes 393224 | tf_op jit(solution)/shard_map/ppermute | solution.py:459
  2.3 5.7 %collective-permute-start.1 = (f32[2,8,16,128]{3,2,1,0:T(8,128)S(1)}, f32[2,8,16,128]{3,2,1,0:T(8,128)S(1)}, u32[]{:S(2)}, u32[]{:S(2)}) collective-permute-start(f32[2,8,16,128]{3,2,1,0:T(8,128)S(1)} %get-tuple-element.26), channel_id=1, source_target_pairs={{0,16},{16,0},{32,48},{48,32},{64,80},{80,64},{96,112},{112,96},{1... | collective-permute-start | bytes 393224 | tf_op jit(solution)/shard_map/ppermute | solution.py:459
  8.0 1.1 %copy-start = (f32[1,2,48,16,128]{4,3,2,1,0:T(8,128)S(1)}, f32[1,2,48,16,128]{4,3,2,1,0:T(8,128)}, u32[]{:S(2)}) copy-start(f32[1,2,48,16,128]{4,3,2,1,0:T(8,128)} %param.4) | copy-start | bytes 2359300
  9.1 6.3 %copy-start.1 = (f32[1,2,48,16,128]{4,3,2,1,0:T(8,128)S(1)}, f32[1,2,48,16,128]{4,3,2,1,0:T(8,128)}, u32[]{:S(2)}) copy-start(f32[1,2,48,16,128]{4,3,2,1,0:T(8,128)} %param.4) | copy-start | bytes 2359300
  10.5 26.8 %collective-permute-start.2 = (f32[2,96,8,128]{3,2,1,0:T(8,128)}, f32[2,96,8,128]{3,2,1,0:T(8,128)S(1)}, u32[]{:S(2)}, u32[]{:S(2)}) collective-permute-start(f32[2,96,8,128]{3,2,1,0:T(8,128)} %get-tuple-element.14), channel_id=1, source_target_pairs={{1,2},{2,1},{3,4},{4,3},{5,6},{6,5},{7,8},{8,7},{9,10},{10,9},{11,... | collective-permute-start | bytes 2359304 | tf_op jit(solution)/shard_map/ppermute | solution.py:459
  11.2 26.1 %collective-permute-start.3 = (f32[2,96,8,128]{3,2,1,0:T(8,128)}, f32[2,96,8,128]{3,2,1,0:T(8,128)S(1)}, u32[]{:S(2)}, u32[]{:S(2)}) collective-permute-start(f32[2,96,8,128]{3,2,1,0:T(8,128)} %get-tuple-element.19), channel_id=1, source_target_pairs={{0,1},{1,0},{2,3},{3,2},{4,5},{5,4},{6,7},{7,6},{8,9},{9,8},{10,11... | collective-permute-start | bytes 2359304 | tf_op jit(solution)/shard_map/ppermute | solution.py:459
  15.5 0.7 copy-start.3
  19.7 29.9 %all-to-all-start = ((f32[256,1,128]{2,1,0:T(1,128)}), f32[256,1,128]{2,1,0:T(1,128)S(1)}, u32[]{:S(2)}, u32[]{:S(2)}) async-start(f32[256,1,128]{2,1,0:T(1,128)} %bitcast.2), calls=%async_computation | async-start | bytes 262144 | tf_op jit(solution)/shard_map/all_to_all | solution.py:491
  41.8 0.9 %copy-start.4 = (f32[2,48,16,128]{3,2,1,0:T(8,128)}, f32[2,48,16,128]{3,2,1,0:T(8,128)S(1)}, u32[]{:S(2)}) copy-start(f32[2,48,16,128]{3,2,1,0:T(8,128)S(1)} %get-tuple-element.24) | copy-start | bytes 2359300
  42.7 8.2 %copy-start.5 = (s32[2,48,16,1]{1,3,2,0:T(1,128)S(1)}, s32[2,48,16,1]{1,3,2,0:T(1,128)}, u32[]{:S(2)}) copy-start(s32[2,48,16,1]{1,3,2,0:T(1,128)} %param.5) | copy-start | bytes 18436
  49.6 21.6 %collective-permute-start.4 = (f32[2,48,16,128]{3,2,1,0:T(8,128)}, f32[2,48,16,128]{3,2,1,0:T(8,128)S(1)}, u32[]{:S(2)}, u32[]{:S(2)}) collective-permute-start(f32[2,48,16,128]{3,2,1,0:T(8,128)} %copy-done.4), channel_id=1, source_target_pairs={{0,128},{1,129},{2,130},{3,131},{4,132},{5,133},{6,134},{7,135},{8... | collective-permute-start | bytes 2359304 | tf_op jit(solution)/shard_map/ppermute | solution.py:500
  51.3 1.0 %copy-start.2 = (f32[128,640]{1,0:T(8,128)S(1)}, f32[128,640]{1,0:T(8,128)}, u32[]{:S(2)}) copy-start(f32[128,640]{1,0:T(8,128)} %constant.26.clone.response) | copy-start | bytes 983044

commit v4 on v3

v4 whole, which is shorter than its diff:
```python
import functools

import jax
import jax.numpy as jnp
import numpy as np
from jax import lax
from jax.experimental import pallas as pl
from jax.experimental.pallas import tpu as pltpu
from jax.sharding import PartitionSpec as P

AXES = ("grp", "gy", "gz")
TY = 6
VOLT = TY * 16
ROWS, COLS, LANES = 48, 16, 128
HY, HZ = 8, 12
EXT = ROWS + 2 * HY
HALF = EXT // 2
PART = ROWS // 2
SIXTH = 1.0 / 6.0

BULK = ((12, 40), (8, 32), (4, 24))
NEAR = ((0, COLS),) * 3
LOWER = ((0, COLS), (0, 8), (0, 8))
UPPER = ((0, COLS), (-8, 8), (-8, 8))


def piece(outer, inner):
    start = outer[0] - inner[0]
    return slice(start, start + inner[1])


def rows_loop(first, last, body, pieces):
    n = (last - first + 1) // pieces
    for i in range(pieces):
        body(first + i * n, n)


def zshift(v, closed):
    z = v.shape[1]
    zp, zm = pltpu.roll(v, z - 1, 1), pltpu.roll(v, 1, 1)
    if closed:
        layer = lax.broadcasted_iota(jnp.int32, v.shape, 1)
        zp = jnp.where(layer == z - 1, 0.0, zp)
        zm = jnp.where(layer == 0, 0.0, zm)
    return zp, zm


def around(w, closed):
    c = w[1:-1]
    zp, zm = zshift(c, closed)
    s = (w[:-2] + w[2:]) + (zp + zm)
    s = s + (pltpu.roll(c, 1, 2) + pltpu.roll(c, LANES - 1, 2))
    return c, s, zp - zm


def zero_edges(edge, ref, at):
    ylo, yhi, zlo, zhi = edge
    rows, layers, _ = ref.shape

    def clear(when, index):
        if when is not None:
            @pl.when(when)
            def _():
                part = ref.at[index]
                part[...] = jnp.zeros(part.shape, jnp.float32)
    clear(ylo, pl.ds(HY - 1, 1))
    clear(yhi, pl.ds(rows - HY, 1))
    clear(zlo, (slice(None), pl.ds(at - 1, 1)))
    clear(zhi, (slice(None), pl.ds(at + COLS, 1)))


def early_scratch(rows, window):
    return [pltpu.VMEM((rows, window[0][1], LANES), jnp.float32)] * 6


def mid_scratch(rows, window):
    return [pltpu.VMEM((rows, window[1][1], LANES), jnp.float32)] * 7


def late_scratch(rows, window):
    return [pltpu.VMEM((rows, window[2][1], LANES), jnp.float32)] * 8


def scratch(rows, window):
    return early_scratch(rows, window) + mid_scratch(rows, window) + late_scratch(rows, window)


def forward(edge, ghost, window, pieces, early, mid):
    U, V, SRC, B, Q, U1 = early
    SRC2, B2, Q2, P2, A = mid[:5]
    top = U1.shape[0] - 1
    closed = window[0][0] == 0
    m = piece(window[0], window[1])
    first, second = window[0][0], window[1][0]

    def finish(ref, at):
        if ghost is not None:
            ref[...] += ghost[...]
        zero_edges(edge, ref, at)

    def stage_a(r, n):
        c, s, d = around(U[pl.ds(r - 1, n + 2)], closed)
        src = (0.5 / 6.0) * d
        SRC[pl.ds(r, n)] = src
        B[pl.ds(r, n)] = 0.35 * c + 0.1 * s
        _, s, _ = around(V[pl.ds(r - 1, n + 2)], closed)
        Q[pl.ds(r, n)] = s * SIXTH - src
    if ghost is not None:
        Q[...] = ghost[...]
        zero_edges(edge, Q, first)
    else:
        rows_loop(1, top - 1, stage_a, pieces)
        finish(Q, first)

    def stage_b(r, n):
        _, s, _ = around(Q[pl.ds(r - 1, n + 2)], closed)
        s = s * SIXTH
        V[pl.ds(r, n)] = s if ghost is not None else s - SRC[pl.ds(r, n)]
    rows_loop(2, top - 2, stage_b, pieces)
    finish(V, first)

    def stage_c(r, n):
        zp, zm = zshift(V[pl.ds(r, n)], closed)
        u = 0.5 * (zp - zm)
        U1[pl.ds(r, n)] = u if ghost is not None else u + B[pl.ds(r, n)]
    rows_loop(3, top - 3, stage_c, pieces)
    zero_edges(edge, U1, first)

    def stage_d(r, n):
        c, s, d = around(U1[pl.ds(r - 1, n + 2)], closed)
        src = (0.5 / 6.0) * d[:, m]
        SRC2[pl.ds(r, n)] = src
        B2[pl.ds(r, n)] = 0.35 * c[:, m] + 0.1 * s[:, m]
        _, s, _ = around(V[pl.ds(r - 1, n + 2)], closed)
        Q2[pl.ds(r, n)] = s[:, m] * SIXTH - src
    rows_loop(3, top - 3, stage_d, pieces)
    finish(Q2, second)

    def stage_e(r, n):
        _, s, _ = around(Q2[pl.ds(r - 1, n + 2)], closed)
        P2[pl.ds(r, n)] = s * SIXTH - SRC2[pl.ds(r, n)]
    rows_loop(4, top - 4, stage_e, pieces)
    finish(P2, second)

    def stage_f(r, n):
        zp, zm = zshift(P2[pl.ds(r, n)], closed)
        A[pl.ds(r, n)] = B2[pl.ds(r, n)] + 0.5 * (zp - zm)
    rows_loop(4, top - 4, stage_f, pieces)
    zero_edges(edge, A, second)


def adjoint(edge, window, pieces, a2, pot, u1, mid, late, give):
    BM, SP = mid[5:7]
    S2, T, B, A1, S3, SP2, S4, T2 = late
    top = SP.shape[0] - 1
    closed = window[0][0] == 0
    second, third = window[1][0], window[2][0]
    m = piece(window[1], window[2])

    def take(source, inner, r, n):
        ref, place = source
        return ref[pl.ds(r, n), piece(place, inner), :]

    def stage_g(r, n):
        c, s, d = around(take(a2, window[1], r - 1, n + 2), closed)
        BM[pl.ds(r, n)] = 0.35 * c + 0.1 * s
        sp = -0.5 * d
        if pot is not None:
            sp = sp + take(pot, window[1], r, n)
        SP[pl.ds(r, n)] = sp
    rows_loop(4, top - 4, stage_g, pieces)
    zero_edges(edge, SP, second)

    def stage_h(r, n):
        c, s, _ = around(SP[pl.ds(r - 1, n + 2)], closed)
        c, s = c[:, m], s[:, m] * SIXTH
        S2[pl.ds(r, n)] = s
        T[pl.ds(r, n)] = (c + s) * SIXTH
    rows_loop(5, top - 5, stage_h, pieces)
    zero_edges(edge, S2, third)
    zero_edges(edge, T, third)

    def stage_i(r, n):
        _, s, _ = around(S2[pl.ds(r - 1, n + 2)], closed)
        S3[pl.ds(r, n)] = s * SIXTH
        zp, zm = zshift(T[pl.ds(r, n)], closed)
        a = BM[pl.ds(r, n), m, :] + 0.5 * (zp - zm)
        if u1 is not None:
            a = a + take(u1, window[2], r, n)
        A1[pl.ds(r, n)] = a
    rows_loop(6, top - 6, stage_i, pieces)
    zero_edges(edge, A1, third)

    def stage_j(r, n):
        if give is None:
            zp, zm = zshift(A1[pl.ds(r, n)], closed)
            d = zp - zm
        else:
            c, s, d = around(A1[pl.ds(r - 1, n + 2)], closed)
            B[pl.ds(r, n)] = 0.35 * c + 0.1 * s
        SP2[pl.ds(r, n)] = S3[pl.ds(r, n)] - 0.5 * d
    rows_loop(6, top - 6, stage_j, pieces)
    zero_edges(edge, SP2, third)

    def stage_k(r, n):
        c, s, _ = around(SP2[pl.ds(r - 1, n + 2)], closed)
        s = s * SIXTH
        S4[pl.ds(r, n)] = s
        T2[pl.ds(r, n)] = (c + s) * SIXTH
    rows_loop(7, top - 7, stage_k, pieces)
    zero_edges(edge, S4, third)
    zero_edges(edge, T2, third)
    if give is None:
        return
    own = slice(third, third + COLS)

    def stage_l(r, n):
        _, s, _ = around(S4[pl.ds(r - 1, n + 2)], closed)
        zp, zm = zshift(T2[pl.ds(r, n)], closed)
        u = B[pl.ds(r, n)] + 0.5 * (zp - zm)
        give(r - HY, n, u[:, own], s[:, own] * SIXTH)
    rows_loop(8, top - 8, stage_l, pieces)


def load_extended(dst, f, part, own, yd, yu, zd, zu):
    block = slice(HZ, HZ + COLS)
    n = PART + 2 * HY
    if part == 0:
        dst[0:HY, block, :] = yd[f]
        dst[HY:n, block, :] = own[f, 0:n - HY]
    else:
        dst[0:n - HY, block, :] = own[f, ROWS - n + HY:]
        dst[n - HY:n, block, :] = yu[f]
    r = part * PART
    for z, near, far in ((zd, 4, 0), (zu, HZ + COLS, HZ + COLS + 8)):
        dst[:, near:near + 8, :] = z[f, r:r + n]
        dst[0:HALF - r, far:far + 4, :] = z[f, EXT + r:EXT + HALF, 0:4, :]
        dst[HALF - r:n, far:far + 4, :] = z[f, EXT:EXT + r + n - HALF, 4:8, :]


def is_even(axis):
    return lax.rem(lax.axis_index(axis), 2) == 0


def strips_kernel(own, far, near):
    even = is_even("gy")
    low, high = own[:, 0:HY], own[:, ROWS - HY:]
    far[...] = jnp.where(even, low, high)
    near[...] = jnp.where(even, high, low)


def pack_kernel(own, far, near, yd, yu, z_near, z_far):
    even = is_even("gy")
    yd[...] = jnp.where(even, far[...], near[...])
    yu[...] = jnp.where(even, near[...], far[...])

    def pack(dst, whole, part):
        for r0, r1, src in ((0, HY, yd), (HY, HY + ROWS, own), (HY + ROWS, EXT, yu)):
            dst[:, r0:r1] = src[:, :, whole:whole + 8, :]
        dst[:, EXT:EXT + HY, 0:4, :] = yd[:, :, part:part + 4, :]
        dst[:, EXT + HY:, 0:4, :] = own[:, 0:HALF - HY, part:part + 4, :]
        dst[:, EXT:EXT + HALF - HY, 4:8, :] = own[:, HALF - HY:, part:part + 4, :]
        dst[:, EXT + HALF - HY:, 4:8, :] = yu[:, :, part:part + 4, :]

    @pl.when(is_even("gz"))
    def _():
        pack(z_near, 8, 4)
        pack(z_far, 0, 8)

    @pl.when(jnp.logical_not(is_even("gz")))
    def _():
        pack(z_near, 0, 8)
        pack(z_far, 8, 4)


HIGHEST = lax.Precision.HIGHEST


def edges():
    gy, gz = lax.axis_index("gy"), lax.axis_index("gz")
    return (gy == 0, gy == lax.axis_size("gy") - 1, gz == 0, gz == lax.axis_size("gz") - 1)


def iota(shape, dim):
    return lax.broadcasted_iota(jnp.int32, shape, dim)


def tile_volts(first, second, labels):
    lab = jnp.broadcast_to(labels, first.shape) - 2 * iota(first.shape, 0)
    hit = jnp.where(lab == 0, first, 0.0) + jnp.where(lab == 1, second, 0.0)
    return jnp.sum(hit, axis=0, keepdims=True)


def fill_ghost(upper, ghost, volts):
    lane, row = iota((8, LANES), 1), iota((8, LANES), 0)
    apart = jnp.where((lane >> 4) == row, jnp.broadcast_to(volts, (8, LANES)), 0.0)
    spread = ((iota((LANES, LANES), 0) & 15) == (iota((LANES, LANES), 1) >> 3)).astype(jnp.float32)
    wall = jnp.dot(apart, spread, precision=HIGHEST, preferred_element_type=jnp.float32) * (1.0 / 6.0)
    layer = iota((COLS, LANES), 0) == jnp.where(upper, COLS - 1, 0)
    for ty in range(8):
        tile = jnp.where(layer, jnp.broadcast_to(wall[ty:ty + 1], (COLS, LANES)), 0.0)
        ghost[8 * ty:8 * ty + 8] = jnp.broadcast_to(tile[None], (8, COLS, LANES))


def wall_tiles(layer, T, T2, held):
    at = slice(HY, HY + ROWS)
    w = T[at, layer, :] + T2[at, layer, :]
    held[...] = jnp.zeros((8, LANES), jnp.float32)
    held[0:TY] = jnp.sum(w.reshape(TY, 8, LANES), axis=1)
    gather = ((iota((LANES, LANES), 0) >> 3) == (iota((LANES, LANES), 1) & 15)).astype(jnp.float32)
    sums = jnp.dot(held[...], gather, precision=HIGHEST, preferred_element_type=jnp.float32)
    keep = (iota((8, LANES), 1) >> 4) == iota((8, LANES), 0)
    return jnp.sum(jnp.where(keep, sums, 0.0), axis=0, keepdims=True)


def split(refs):
    return refs[:6], refs[6:13], refs[13:21]


def wall_kernel(own, yd, yu, volts, row, *refs):
    early, mid, late = split(refs)
    held, sums = refs[21:]
    ylo, yhi, zlo, zhi = edges()
    edge = (ylo, yhi, None, None)
    is_forward = lax.axis_index("grp") == 0
    sums[...] = jnp.zeros((1, LANES), jnp.float32)

    @pl.when(jnp.logical_or(zlo, zhi))
    def _():
        for f in range(2):
            early[f][0:HY] = yd[f]
            early[f][HY:HY + ROWS] = own[f]
            early[f][HY + ROWS:] = yu[f]

    def side(window, layer):
        @pl.when(is_forward)
        def _():
            forward(edge, None, window, 2, early, mid)
            adjoint(edge, window, 2, (mid[4], window[1]), None, (early[5], window[0]), mid, late, None)

        @pl.when(jnp.logical_not(is_forward))
        def _():
            adjoint(edge, window, 2, (early[0], window[0]), (early[1], window[0]), None, mid, late, None)

        sums[...] = wall_tiles(layer, late[1], late[7], held)

    @pl.when(zlo)
    def _():
        side(LOWER, 0)

    @pl.when(zhi)
    def _():
        side(UPPER, 7)

    lane = iota((1, LANES), 1)
    out = jnp.where(lane == VOLT, volts[0], jnp.where(lane == VOLT + 1, volts[1], sums[...]))
    row[...] = jnp.broadcast_to(out, row.shape)


def bulk_kernel(part, own, yd, yu, far, near, main, send, *refs):
    early, mid, late = split(refs)
    ylo, yhi, zlo, zhi = edges()
    edge = (ylo, None, zlo, zhi) if part == 0 else (None, yhi, zlo, zhi)
    is_forward = lax.axis_index("grp") == 0

    @pl.when(is_even("gz"))
    def _():
        for f in range(2):
            load_extended(early[f], f, part, own, yd, yu, far, near)

    @pl.when(jnp.logical_not(is_even("gz")))
    def _():
        for f in range(2):
            load_extended(early[f], f, part, own, yd, yu, near, far)

    def into(ref):
        def give(r, n, u, p):
            ref[0, pl.ds(r, n)] = u
            ref[1, pl.ds(r, n)] = p
        return give

    @pl.when(is_forward)
    def _():
        forward(edge, None, BULK, 1, early, mid)
        at = (slice(HY, HY + PART), slice(BULK[1][0], BULK[1][0] + COLS))
        main[0] = mid[4][at]
        main[1] = mid[3][at]
        adjoint(edge, BULK, 1, (mid[4], BULK[1]), None, (early[5], BULK[0]), mid, late, into(send))

    @pl.when(jnp.logical_not(is_forward))
    def _():
        adjoint(edge, BULK, 1, (early[0], BULK[0]), (early[1], BULK[0]), None, mid, late, into(main))


def volts_kernel(lower, upper, rows, near, labels, response, out, grad, *refs):
    early, mid, late = split(refs)
    ghost = refs[21]
    ylo, yhi, zlo, zhi = edges()
    edge = (ylo, yhi, None, None)
    is_forward = lax.axis_index("grp") == 0
    n = rows.shape[0]
    first = jnp.broadcast_to(rows[:, VOLT:VOLT + 1], (n, LANES))
    second = jnp.broadcast_to(rows[:, VOLT + 1:VOLT + 2], (n, LANES))
    out[:, 0:PART] = lower[...]
    out[:, PART:] = upper[...]

    @pl.when(jnp.logical_or(zlo, zhi))
    def _():
        fill_ghost(zhi, ghost, tile_volts(first, second, near[...]))
        forward(edge, ghost, NEAR, 2, early, mid)

        @pl.when(is_forward)
        def _():
            out[0] += mid[4][HY:HY + ROWS]
            out[1] += mid[3][HY:HY + ROWS]

        @pl.when(jnp.logical_not(is_forward))
        def _():
            def give(r, n, u, p):
                out[0, pl.ds(r, n)] += u
                out[1, pl.ds(r, n)] += p
            adjoint(edge, NEAR, 2, (mid[4], NEAR[1]), None, (early[5], NEAR[0]), mid, late, give)

    gy, gz = lax.axis_size("gy"), lax.axis_size("gz")
    me = (lax.axis_index("grp") * gy + lax.axis_index("gy")) * gz + lax.axis_index("gz")
    pair = [jnp.zeros((gy, LANES), jnp.float32)] * 2
    block = iota((gy, LANES), 0)
    for s in range(2):
        v = jnp.concatenate([tile_volts(first, second, labels[s, g:g + 1]) for g in range(gy)], axis=0)
        r = jnp.dot(v, response[...], precision=HIGHEST, preferred_element_type=jnp.float32)
        r = [r[:, k * LANES:(k + 1) * LANES] for k in range(5)]
        w = jnp.where(block == 0, r[3], jnp.where(block == gy - 1, r[4], r[0]))
        w = w + jnp.where(block == 0, 0.0, pltpu.roll(r[1], 1, 0))
        w = w + jnp.where(block == gy - 1, 0.0, pltpu.roll(r[2], gy - 1, 0))
        for g in range(2):
            w = w + rows[pl.ds(g * gy * gz + s * (gz - 1), gy, stride=gz), :]
        for j in range(2):
            pair[j] = pair[j] + jnp.where(labels[s] == 2 * me + j, w, 0.0)
    total = [jnp.sum(p) for p in pair]
    grad[...] = jnp.where(iota((1, 2), 1) == 0, total[0], total[1])


def sum_kernel(main, lower, upper, out):
    out[0, :, 0:PART] = main[:, 0:PART] + lower[...]
    out[0, :, PART:] = main[:, PART:] + upper[...]


def wall_response():
    def near_sum(f):
        g = np.pad(f, ((0, 0), (1, 1), (1, 1), (0, 0)))
        t = g[:, 2:, 1:-1] + g[:, :-2, 1:-1] + g[:, 1:-1, 2:] + g[:, 1:-1, :-2]
        return t + np.roll(f, 1, 3) + np.roll(f, -1, 3)

    def diff(f):
        g = np.pad(f, ((0, 0), (0, 0), (1, 1), (0, 0)))
        return g[:, :, 2:] - g[:, :, :-2]

    def sums(blocks, at):
        ghost = np.zeros((TY, blocks * ROWS, 13, LANES))
        for t in range(TY):
            ghost[t, at * ROWS + 8 * t:at * ROWS + 8 * t + 8, 0, 0:8] = 1.0
        u, p, states = np.zeros_like(ghost), np.zeros_like(ghost), []
        for _ in range(2):
            source = 0.5 * diff(u)
            for _ in range(2):
                p = (near_sum(p) + ghost - source) / 6.0
            u = 0.35 * u + 0.1 * near_sum(u) + 0.5 * diff(p)
            states.append(u)
        a, q, wall = np.zeros_like(ghost), np.zeros_like(ghost), 0.0
        for u in reversed(states):
            a = a + u
            spread, total = q - 0.5 * diff(a), 0.0
            for _ in range(2):
                total = total + spread / 6.0
                spread = near_sum(spread) / 6.0
            a = 0.35 * a + 0.1 * near_sum(a) + 0.5 * diff(total)
            q = spread
            wall = wall + total[:, :, 0]
        return wall.reshape(TY, blocks, TY, 8, 16, 8).sum((3, 5))

    def matrix(got):
        m = np.zeros((LANES, LANES), np.float32)
        for t in range(TY):
            for x in range(16):
                m[t * 16 + x, 0:TY * 16] = np.roll(got[t], x, 1).reshape(-1)
        return m

    middle, low, high = sums(3, 1), sums(2, 0), sums(2, 1)
    return np.concatenate([matrix(middle[:, 1]), matrix(middle[:, 2]), matrix(middle[:, 0]),
                           matrix(low[:, 0]), matrix(high[:, 1])], axis=1)


def vmem(n):
    return [pl.BlockSpec(memory_space=pltpu.VMEM)] * n


def shape(*dims):
    return jax.ShapeDtypeStruct(dims, jnp.float32)


def swapped(array, axis, first):
    pairs = []
    for i in range(first, lax.axis_size(axis) - 1, 2):
        pairs += [(i, i + 1), (i + 1, i)]
    return lax.ppermute(array, axis, pairs)


def per_device(response, field_pairs, tile_owner, electrode_volts):
    own = field_pairs[0]
    labels = tile_owner[..., 0]
    gy, gz = lax.axis_index("gy"), lax.axis_index("gz")
    devices = lax.axis_size(AXES)
    half = shape(2, PART, COLS, LANES)
    strip, slab = shape(2, HY, COLS, LANES), shape(2, EXT * 3 // 2, 8, LANES)

    def limit(mib):
        return pltpu.CompilerParams(vmem_limit_bytes=mib * 1024 * 1024)

    far, near = pl.pallas_call(
        strips_kernel, out_shape=(strip, strip), in_specs=vmem(1), out_specs=vmem(2), compiler_params=limit(4),
    )(own)
    far = swapped(far, "gy", 1)
    near = swapped(near, "gy", 0)
    yd, yu, z_near, z_far = pl.pallas_call(
        pack_kernel, out_shape=(strip, strip, slab, slab), in_specs=vmem(3), out_specs=vmem(4), compiler_params=limit(8),
    )(own, far, near)
    far = swapped(z_far, "gz", 1)
    near = swapped(z_near, "gz", 0)

    mine, _ = lax.optimization_barrier((own, z_far))
    row = pl.pallas_call(
        wall_kernel, out_shape=shape(devices, LANES),
        in_specs=vmem(3) + [pl.BlockSpec(memory_space=pltpu.SMEM)], out_specs=vmem(1)[0],
        scratch_shapes=scratch(EXT, LOWER) + [pltpu.VMEM((8, LANES), jnp.float32), pltpu.VMEM((1, LANES), jnp.float32)],
        compiler_params=limit(12),
    )(mine, yd, yu, electrode_volts)
    rows = lax.all_to_all(row, AXES, 0, 0, tiled=True)

    mine, _ = lax.optimization_barrier((own, row))
    def bulk(part, block, load):
        return pl.pallas_call(
            functools.partial(bulk_kernel, part), out_shape=(half, half), in_specs=vmem(5), out_specs=vmem(2),
            scratch_shapes=scratch(PART + 2 * HY, BULK), compiler_params=limit(20),
            cost_estimate=pl.CostEstimate(flops=10 ** 8, bytes_accessed=load * 10 ** 6, transcendentals=0),
        )(block, yd, yu, far, near)

    main0, send = bulk(0, mine, 36)
    lower = lax.ppermute(send, "grp", [(0, 1)])
    mine, _ = lax.optimization_barrier((own, send))
    main1, send = bulk(1, mine, 9)
    send, rows = lax.optimization_barrier((send, rows))
    upper = lax.ppermute(send, "grp", [(0, 1)])

    fenced = jnp.pad(labels, ((0, 0), (1, 1), (0, 0)), constant_values=-1)
    side = (gz == lax.axis_size("gz") - 1).astype(jnp.int32)
    by_wall = lax.dynamic_slice(fenced, (side, gy * TY, 0), (1, 8, 16)).reshape(1, LANES)
    by_block = jnp.pad(labels.reshape(2, 8, TY * 16), ((0, 0), (0, 0), (0, LANES - TY * 16)), constant_values=-1)
    total, grad = pl.pallas_call(
        volts_kernel, out_shape=(shape(2, ROWS, COLS, LANES), shape(1, 2)), in_specs=vmem(6), out_specs=vmem(2),
        scratch_shapes=scratch(EXT, NEAR) + [pltpu.VMEM((EXT, COLS, LANES), jnp.float32)], compiler_params=limit(16),
    )(main0, main1, rows, by_wall, by_block, response)
    advanced = pl.pallas_call(
        sum_kernel, out_shape=shape(1, 2, ROWS, COLS, LANES), in_specs=vmem(3), out_specs=vmem(1)[0],
        compiler_params=limit(8),
    )(total, lower, upper)
    return (advanced, grad.reshape(2))


def solution(mesh):
    response = jnp.asarray(wall_response())
    placed = (P("grp", None, "gy", "gz", None), P(), P(AXES))
    return jax.shard_map(
        functools.partial(per_device, response), mesh=mesh, in_specs=placed,
        out_specs=(P("grp", None, "gy", "gz", None), P(AXES)), check_vma=False,
    )
```

time: 72.4 us -> 63.2 us (0.87)
  the two profiles are of different devices: /device:TPU:32 before, /device:TPU:120 now
where the time goes in v4:
time: 63.2 us; the launch traced here: 62.8 us
  starting transfers between devices  29 us (46%)
  waiting for transfers between devices  17.2 us (27%)
  Pallas kernels  10.2 us (16%)
  local copies, waits for them, and re-layouts  5.63 us (9%)
  between operations  0.75 us (1%)
    all_to_all x1, starting transfers between devices, per_device(): rows = lax.all_to_all(row, AXES, 0, 0, tiled=True)  15.5 us
    ppermute x4, starting transfers between devices, swapped(): return lax.ppermute(array, axis, pairs)  10.8 us
    ppermute x1, waiting for transfers between devices, per_device(): upper = lax.ppermute(send, 'grp', [(0, 1)])  8.15 us
    ppermute x4, waiting for transfers between devices, swapped(): return lax.ppermute(array, axis, pairs)  5.43 us
    unnamed x17, local copies, waits for them, and re-layouts  5.32 us
    pallas_call x2, Pallas kernels, bulk(): pl.pallas_call(functools.partial(bulk_kernel, part), out_shape=(half, hal...  5.16 us
    ppermute x1, waiting for transfers between devices, per_device(): lower = lax.ppermute(send, 'grp', [(0, 1)])  3.63 us
    pallas_call x1, Pallas kernels, per_device(): pl.pallas_call(volts_kernel, out_shape=(shape(2, ROWS, COLS, LANES), shap...  1.71 us
  transfers between devices with their start and end apart: 7, of which 5 were waited for; matrix products, arithmetic and copies ran while one was open for 1% of the time, Pallas kernels for 13%

profile of v4, /device:TPU:120, one launch (start us, length us, event | category | flops | bytes accessed | tf_op | source)
XLA Modules:
  0.0 62.8 jit_solution(1150098757838969337)
XLA Ops:
  0.6 1.1 %copy-done = f32[1,2,48,16,128]{4,3,2,1,0:T(8,128)S(1)} copy-done((f32[1,2,48,16,128]{4,3,2,1,0:T(8,128)S(1)}, f32[1,2,48,16,128]{4,3,2,1,0:T(8,128)}, u32[]{:S(2)}) %copy-start) | copy-done | bytes 786456
  1.8 2.1 %collective-permute-start = (f32[2,8,16,128]{3,2,1,0:T(8,128)S(1)}, f32[2,8,16,128]{3,2,1,0:T(8,128)S(1)}, u32[]{:S(2)}, u32[]{:S(2)}) collective-permute-start(f32[2,8,16,128]{3,2,1,0:T(8,128)S(1)} %get-tuple-element.19), channel_id=1, source_target_pairs={{16,32},{32,16},{48,64},{64,48},{80,96},{96,80},{17,33},{33,17},{4... | collective-permute-start | bytes 393224 | tf_op jit(solution)/shard_map/ppermute | solution.py:505
  3.9 3.8 %collective-permute-start.1 = (f32[2,8,16,128]{3,2,1,0:T(8,128)S(1)}, f32[2,8,16,128]{3,2,1,0:T(8,128)S(1)}, u32[]{:S(2)}, u32[]{:S(2)}) collective-permute-start(f32[2,8,16,128]{3,2,1,0:T(8,128)S(1)} %get-tuple-element.20), channel_id=1, source_target_pairs={{0,16},{16,0},{32,48},{48,32},{64,80},{80,64},{96,112},{112,96},{1... | collective-permute-start | bytes 393224 | tf_op jit(solution)/shard_map/ppermute | solution.py:505
  7.6 2.5 %collective-permute-done.far = f32[2,8,16,128]{3,2,1,0:T(8,128)S(1)} collective-permute-done((f32[2,8,16,128]{3,2,1,0:T(8,128)S(1)}, f32[2,8,16,128]{3,2,1,0:T(8,128)S(1)}, u32[]{:S(2)}, u32[]{:S(2)}) %collective-permute-start) | collective-permute-done | bytes 131104 | tf_op jit(solution)/shard_map/ppermute | solution.py:505
  10.1 1.1 %shard_map.60 = (f32[2,8,16,128]{3,2,1,0:T(8,128)S(1)}, f32[2,8,16,128]{3,2,1,0:T(8,128)S(1)}, f32[2,96,8,128]{3,2,1,0:T(8,128)S(1)}, f32[2,96,8,128]{3,2,1,0:T(8,128)}) custom-call(f32[2,48,16,128]{3,2,1,0:T(8,128)S(1)} %bitcast.12, f32[2,8,16,128]{3,2,1,0:T(8,128)S(1)} %collective-permute-done.far, f32[2,8,16,128]{3,2,1,0:T(8,128)S(1)} %collective-permute-done.1.near), custom_call_target="tpu_custom_call" | custom-call | tf_op jit(solution)/shard_map/pallas_call | solution.py:524
  11.2 4.8 %collective-permute-start.2 = (f32[2,96,8,128]{3,2,1,0:T(8,128)}, f32[2,96,8,128]{3,2,1,0:T(8,128)S(1)}, u32[]{:S(2)}, u32[]{:S(2)}) collective-permute-start(f32[2,96,8,128]{3,2,1,0:T(8,128)} %get-tuple-element.21), channel_id=1, source_target_pairs={{1,2},{2,1},{3,4},{4,3},{5,6},{6,5},{7,8},{8,7},{9,10},{10,9},{11,... | collective-permute-start | bytes 2359304 | tf_op jit(solution)/shard_map/ppermute | solution.py:505
  16.1 0.1 collective-permute-start.3
  16.2 0.7 %copy-done.5 = f32[2]{0:T(128)S(1)} copy-done((f32[2]{0:T(128)S(1)}, f32[2]{0:T(128)}, u32[]{:S(2)}) %copy-start.5) | copy-done | bytes 32
  16.9 1.2 %shard_map.61 = f32[256,128]{1,0:T(8,128)} custom-call(f32[2,48,16,128]{3,2,1,0:T(8,128)S(1)} %bitcast.13, f32[2,8,16,128]{3,2,1,0:T(8,128)S(1)} %get-tuple-element.23.yd, f32[2,8,16,128]{3,2,1,0:T(8,128)S(1)} %get-tuple-element.24.yu, f32[2]{0:T(128)S(1)} %copy-done.5), custom_call_target="tpu_custom_call" | custom-call | tf_op jit(solution)/shard_map/pallas_call | solution.py:531
  18.1 15.5 %all-to-all-start = ((f32[256,1,128]{2,1,0:T(1,128)}), f32[256,1,128]{2,1,0:T(1,128)S(1)}, u32[]{:S(2)}, u32[]{:S(2)}) async-start(f32[256,1,128]{2,1,0:T(1,128)} %bitcast.2), calls=%async_computation | async-start | bytes 262144 | tf_op jit(solution)/shard_map/all_to_all | solution.py:537
  33.6 2.1 %collective-permute-done.2.far = f32[2,96,8,128]{3,2,1,0:T(8,128)S(1)} collective-permute-done((f32[2,96,8,128]{3,2,1,0:T(8,128)}, f32[2,96,8,128]{3,2,1,0:T(8,128)S(1)}, u32[]{:S(2)}, u32[]{:S(2)}) %collective-permute-start.2) | collective-permute-done | bytes 786464 | tf_op jit(solution)/shard_map/ppermute | solution.py:505
  35.7 0.8 %collective-permute-done.3.near = f32[2,96,8,128]{3,2,1,0:T(8,128)S(1)} collective-permute-done((f32[2,96,8,128]{3,2,1,0:T(8,128)S(1)}, f32[2,96,8,128]{3,2,1,0:T(8,128)S(1)}, u32[]{:S(2)}, u32[]{:S(2)}) %collective-permute-start.3) | collective-permute-done | bytes 786464 | tf_op jit(solution)/shard_map/ppermute | solution.py:505
  36.5 3.0 %shard_map.62 = (f32[2,24,16,128]{3,2,1,0:T(8,128)S(1)}, f32[2,24,16,128]{3,2,1,0:T(8,128)}) custom-call(f32[2,48,16,128]{3,2,1,0:T(8,128)S(1)} %bitcast.14, f32[2,8,16,128]{3,2,1,0:T(8,128)S(1)} %get-tuple-element.23.yd, f32[2,8,16,128]{3,2,1,0:T(8,128)S(1)} %get-tuple-element.24.yu, f32[2,96,8,128]{3,2,1,0:T(8,128)S(1)} %collective-permute-done.2.far, ...), custom_call_target="tpu_custom_call" | custom-call | flops 100000000 | bytes 36000000 | tf_op jit(solution)/shard_map/pallas_call | solution.py:541
  39.6 1.3 %collective-permute-start.4 = (f32[2,24,16,128]{3,2,1,0:T(8,128)}, f32[2,24,16,128]{3,2,1,0:T(8,128)S(1)}, u32[]{:S(2)}, u32[]{:S(2)}) collective-permute-start(f32[2,24,16,128]{3,2,1,0:T(8,128)} %get-tuple-element.28), channel_id=1, source_target_pairs={{0,128},{1,129},{2,130},{3,131},{4,132},{5,133},{6,134},{7,135},{8... | collective-permute-start | bytes 1179656 | tf_op jit(solution)/shard_map/ppermute | solution.py:548
  40.9 2.1 %shard_map.63 = (f32[2,24,16,128]{3,2,1,0:T(8,128)S(1)}, f32[2,24,16,128]{3,2,1,0:T(8,128)S(1)}) custom-call(f32[2,48,16,128]{3,2,1,0:T(8,128)S(1)} %bitcast.15, f32[2,8,16,128]{3,2,1,0:T(8,128)S(1)} %get-tuple-element.23.yd, f32[2,8,16,128]{3,2,1,0:T(8,128)S(1)} %get-tuple-element.24.yu, f32[2,96,8,128]{3,2,1,0:T(8,128)S(1)} %collective-permute-done.2.far, ...), custom_call_target="tpu_custom_call" | custom-call | flops 100000000 | bytes 9000000 | tf_op jit(solution)/shard_map/pallas_call | solution.py:541
  43.0 0.7 %copy-done.2 = f32[2,24,16,128]{3,2,1,0:T(8,128)} copy-done((f32[2,24,16,128]{3,2,1,0:T(8,128)}, f32[2,24,16,128]{3,2,1,0:T(8,128)S(1)}, u32[]{:S(2)}) %copy-start.2) | copy-done | bytes 393240
  43.7 0.7 %copy-done.6 = f32[2,24,16,128]{3,2,1,0:T(8,128)} copy-done((f32[2,24,16,128]{3,2,1,0:T(8,128)}, f32[2,24,16,128]{3,2,1,0:T(8,128)S(1)}, u32[]{:S(2)}) %copy-start.6) | copy-done | bytes 393240
  44.5 1.4 %collective-permute-start.5 = (f32[2,24,16,128]{3,2,1,0:T(8,128)}, f32[2,24,16,128]{3,2,1,0:T(8,128)S(1)}, u32[]{:S(2)}, u32[]{:S(2)}) collective-permute-start(f32[2,24,16,128]{3,2,1,0:T(8,128)} %copy-done.6), channel_id=1, source_target_pairs={{0,128},{1,129},{2,130},{3,131},{4,132},{5,133},{6,134},{7,135},{8... | collective-permute-start | bytes 1179656 | tf_op jit(solution)/shard_map/ppermute | solution.py:552
  46.3 1.0 %copy-done.3 = f32[2,24,16,128]{3,2,1,0:T(8,128)S(1)} copy-done((f32[2,24,16,128]{3,2,1,0:T(8,128)S(1)}, f32[2,24,16,128]{3,2,1,0:T(8,128)}, u32[]{:S(2)}) %copy-start.3) | copy-done | bytes 393240
  47.3 1.0 %copy-done.4 = f32[128,640]{1,0:T(8,128)S(1)} copy-done((f32[128,640]{1,0:T(8,128)S(1)}, f32[128,640]{1,0:T(8,128)}, u32[]{:S(2)}) %copy-start.4) | copy-done | bytes 327704
  48.3 1.7 %shard_map.64 = (f32[2,48,16,128]{3,2,1,0:T(8,128)S(1)}, f32[1,2]{1,0:T(1,128)}) custom-call(f32[2,24,16,128]{3,2,1,0:T(8,128)S(1)} %get-tuple-element.27.lower, f32[2,24,16,128]{3,2,1,0:T(8,128)S(1)} %copy-done.3, f32[256,128]{1,0:T(8,128)S(1)} %bitcast.16, s32[1,128]{1,0:T(1,128)S(1)} %reshape.12.near, s32[2,8,128]{2,1,0:T(8,128)S(1)} %pad.9.labels, ...), custom_call_target="tpu_custom_call" | custom-call | tf_op jit(solution)/shard_map/pallas_call | solution.py:558
  50.0 3.6 %collective-permute-done.4.lower = f32[2,24,16,128]{3,2,1,0:T(8,128)S(1)} collective-permute-done((f32[2,24,16,128]{3,2,1,0:T(8,128)}, f32[2,24,16,128]{3,2,1,0:T(8,128)S(1)}, u32[]{:S(2)}, u32[]{:S(2)}) %collective-permute-start.4) | collective-permute-done | bytes 393248 | tf_op jit(solution)/shard_map/ppermute | solution.py:548
  53.7 8.1 %collective-permute-done.5.upper = f32[2,24,16,128]{3,2,1,0:T(8,128)S(1)} collective-permute-done((f32[2,24,16,128]{3,2,1,0:T(8,128)}, f32[2,24,16,128]{3,2,1,0:T(8,128)S(1)}, u32[]{:S(2)}, u32[]{:S(2)}) %collective-permute-start.5) | collective-permute-done | bytes 393248 | tf_op jit(solution)/shard_map/ppermute | solution.py:552
  61.8 1.0 %shard_map.65 = f32[1,2,48,16,128]{4,3,2,1,0:T(8,128)} custom-call(f32[2,48,16,128]{3,2,1,0:T(8,128)S(1)} %get-tuple-element.33.main, f32[2,24,16,128]{3,2,1,0:T(8,128)S(1)} %collective-permute-done.4.lower, f32[2,24,16,128]{3,2,1,0:T(8,128)S(1)} %collective-permute-done.5.upper), custom_call_target="tpu_custom_call" | custom-call | tf_op jit(solution)/shard_map/pallas_call | solution.py:562
  (19 shorter events, 0.4 us)
Async XLA Ops:
  0.6 1.1 %copy-start = (f32[1,2,48,16,128]{4,3,2,1,0:T(8,128)S(1)}, f32[1,2,48,16,128]{4,3,2,1,0:T(8,128)}, u32[]{:S(2)}) copy-start(f32[1,2,48,16,128]{4,3,2,1,0:T(8,128)} %param.4) | copy-start | bytes 2359300
  1.8 8.4 %copy-start.1 = (f32[1,2,48,16,128]{4,3,2,1,0:T(8,128)S(1)}, f32[1,2,48,16,128]{4,3,2,1,0:T(8,128)}, u32[]{:S(2)}) copy-start(f32[1,2,48,16,128]{4,3,2,1,0:T(8,128)} %param.4) | copy-start | bytes 2359300
  1.8 8.3 %collective-permute-start = (f32[2,8,16,128]{3,2,1,0:T(8,128)S(1)}, f32[2,8,16,128]{3,2,1,0:T(8,128)S(1)}, u32[]{:S(2)}, u32[]{:S(2)}) collective-permute-start(f32[2,8,16,128]{3,2,1,0:T(8,128)S(1)} %get-tuple-element.19), channel_id=1, source_target_pairs={{16,32},{32,16},{48,64},{64,48},{80,96},{96,80},{17,33},{33,17},{4... | collective-permute-start | bytes 393224 | tf_op jit(solution)/shard_map/ppermute | solution.py:505
  3.9 6.3 %collective-permute-start.1 = (f32[2,8,16,128]{3,2,1,0:T(8,128)S(1)}, f32[2,8,16,128]{3,2,1,0:T(8,128)S(1)}, u32[]{:S(2)}, u32[]{:S(2)}) collective-permute-start(f32[2,8,16,128]{3,2,1,0:T(8,128)S(1)} %get-tuple-element.20), channel_id=1, source_target_pairs={{0,16},{16,0},{32,48},{48,32},{64,80},{80,64},{96,112},{112,96},{1... | collective-permute-start | bytes 393224 | tf_op jit(solution)/shard_map/ppermute | solution.py:505
  11.2 24.5 %collective-permute-start.2 = (f32[2,96,8,128]{3,2,1,0:T(8,128)}, f32[2,96,8,128]{3,2,1,0:T(8,128)S(1)}, u32[]{:S(2)}, u32[]{:S(2)}) collective-permute-start(f32[2,96,8,128]{3,2,1,0:T(8,128)} %get-tuple-element.21), channel_id=1, source_target_pairs={{1,2},{2,1},{3,4},{4,3},{5,6},{6,5},{7,8},{8,7},{9,10},{10,9},{11,... | collective-permute-start | bytes 2359304 | tf_op jit(solution)/shard_map/ppermute | solution.py:505
  16.1 20.5 %collective-permute-start.3 = (f32[2,96,8,128]{3,2,1,0:T(8,128)S(1)}, f32[2,96,8,128]{3,2,1,0:T(8,128)S(1)}, u32[]{:S(2)}, u32[]{:S(2)}) collective-permute-start(f32[2,96,8,128]{3,2,1,0:T(8,128)S(1)} %get-tuple-element.26), channel_id=1, source_target_pairs={{0,1},{1,0},{2,3},{3,2},{4,5},{5,4},{6,7},{7,6},{8,9},{9,8},{10,11... | collective-permute-start | bytes 2359304 | tf_op jit(solution)/shard_map/ppermute | solution.py:505
  16.2 0.7 %copy-start.5 = (f32[2]{0:T(128)S(1)}, f32[2]{0:T(128)}, u32[]{:S(2)}) copy-start(f32[2]{0:T(128)} %volts.1) | copy-start | bytes 28
  18.1 26.4 %all-to-all-start = ((f32[256,1,128]{2,1,0:T(1,128)}), f32[256,1,128]{2,1,0:T(1,128)S(1)}, u32[]{:S(2)}, u32[]{:S(2)}) async-start(f32[256,1,128]{2,1,0:T(1,128)} %bitcast.2), calls=%async_computation | async-start | bytes 262144 | tf_op jit(solution)/shard_map/all_to_all | solution.py:537
  39.6 14.1 %collective-permute-start.4 = (f32[2,24,16,128]{3,2,1,0:T(8,128)}, f32[2,24,16,128]{3,2,1,0:T(8,128)S(1)}, u32[]{:S(2)}, u32[]{:S(2)}) collective-permute-start(f32[2,24,16,128]{3,2,1,0:T(8,128)} %get-tuple-element.28), channel_id=1, source_target_pairs={{0,128},{1,129},{2,130},{3,131},{4,132},{5,133},{6,134},{7,135},{8... | collective-permute-start | bytes 1179656 | tf_op jit(solution)/shard_map/ppermute | solution.py:548
  43.0 0.8 %copy-start.2 = (f32[2,24,16,128]{3,2,1,0:T(8,128)}, f32[2,24,16,128]{3,2,1,0:T(8,128)S(1)}, u32[]{:S(2)}) copy-start(f32[2,24,16,128]{3,2,1,0:T(8,128)S(1)} %get-tuple-element.30.upper) | copy-start | bytes 1179652
  43.7 0.7 %copy-start.6 = (f32[2,24,16,128]{3,2,1,0:T(8,128)}, f32[2,24,16,128]{3,2,1,0:T(8,128)S(1)}, u32[]{:S(2)}) copy-start(f32[2,24,16,128]{3,2,1,0:T(8,128)S(1)} %get-tuple-element.34) | copy-start | bytes 1179652
  44.5 1.4 %copy-start.7 = (s32[2,48,16,1]{1,3,2,0:T(1,128)S(1)}, s32[2,48,16,1]{1,3,2,0:T(1,128)}, u32[]{:S(2)}) copy-start(s32[2,48,16,1]{1,3,2,0:T(1,128)} %param.5) | copy-start | bytes 18436
  44.5 17.3 %collective-permute-start.5 = (f32[2,24,16,128]{3,2,1,0:T(8,128)}, f32[2,24,16,128]{3,2,1,0:T(8,128)S(1)}, u32[]{:S(2)}, u32[]{:S(2)}) collective-permute-start(f32[2,24,16,128]{3,2,1,0:T(8,128)} %copy-done.6), channel_id=1, source_target_pairs={{0,128},{1,129},{2,130},{3,131},{4,132},{5,133},{6,134},{7,135},{8... | collective-permute-start | bytes 1179656 | tf_op jit(solution)/shard_map/ppermute | solution.py:552
  46.3 1.0 %copy-start.3 = (f32[2,24,16,128]{3,2,1,0:T(8,128)S(1)}, f32[2,24,16,128]{3,2,1,0:T(8,128)}, u32[]{:S(2)}) copy-start(f32[2,24,16,128]{3,2,1,0:T(8,128)} %copy-done.2) | copy-start | bytes 1179652
  47.3 1.0 %copy-start.4 = (f32[128,640]{1,0:T(8,128)S(1)}, f32[128,640]{1,0:T(8,128)}, u32[]{:S(2)}) copy-start(f32[128,640]{1,0:T(8,128)} %constant.23.clone.response) | copy-start | bytes 983044

commit v5 on v4

--- a/solution.py
+++ b/solution.py
@@ -14,9 +14,12 @@
 ROWS, COLS, LANES = 48, 16, 128
 HY, HZ = 8, 12
 EXT = ROWS + 2 * HY
-HALF = EXT // 2
-PART = ROWS // 2
+RIM = 4
+HALF = EXT // 2 - RIM
+PARTS = 2
+PART = ROWS // PARTS
 SIXTH = 1.0 / 6.0
+SHARE, PIECES = 0.34, 3
 
 BULK = ((12, 40), (8, 32), (4, 24))
 NEAR = ((0, COLS),) * 3
@@ -45,12 +48,29 @@
     return zp, zm
 
 
+def beside(c):
+    n, z, _ = c.shape
+    k = int(n * SHARE)
+    row = lax.broadcasted_iota(jnp.int32, (LANES, LANES), 0)
+    lane = lax.broadcasted_iota(jnp.int32, (LANES, LANES), 1)
+    apart = (row - lane) & (LANES - 1)
+    ring = jnp.where((apart == 1) | (apart == LANES - 1), 1.0, 0.0).astype(jnp.bfloat16)
+    rest, total = c[:k].reshape(k * z, LANES), None
+    for i in range(PIECES):
+        part = rest.astype(jnp.bfloat16)
+        got = jnp.dot(part, ring, preferred_element_type=jnp.float32)
+        total = got if total is None else total + got
+        if i < PIECES - 1:
+            rest = rest - part.astype(jnp.float32)
+    rolled = pltpu.roll(c[k:], 1, 2) + pltpu.roll(c[k:], LANES - 1, 2)
+    return jnp.concatenate([total.reshape(k, z, LANES), rolled], axis=0)
+
+
 def around(w, closed):
     c = w[1:-1]
     zp, zm = zshift(c, closed)
     s = (w[:-2] + w[2:]) + (zp + zm)
-    s = s + (pltpu.roll(c, 1, 2) + pltpu.roll(c, LANES - 1, 2))
-    return c, s, zp - zm
+    return c, s + beside(c), zp - zm
 
 
 def zero_edges(edge, ref, at):
@@ -222,20 +242,26 @@
     rows_loop(8, top - 8, stage_l, pieces)
 
 
-def load_extended(dst, f, part, own, yd, yu, zd, zu):
-    block = slice(HZ, HZ + COLS)
-    n = PART + 2 * HY
-    if part == 0:
-        dst[0:HY, block, :] = yd[f]
-        dst[HY:n, block, :] = own[f, 0:n - HY]
-    else:
-        dst[0:n - HY, block, :] = own[f, ROWS - n + HY:]
-        dst[n - HY:n, block, :] = yu[f]
-    r = part * PART
-    for z, near, far in ((zd, 4, 0), (zu, HZ + COLS, HZ + COLS + 8)):
-        dst[:, near:near + 8, :] = z[f, r:r + n]
-        dst[0:HALF - r, far:far + 4, :] = z[f, EXT + r:EXT + HALF, 0:4, :]
-        dst[HALF - r:n, far:far + 4, :] = z[f, EXT:EXT + r + n - HALF, 4:8, :]
+def load_extended(dst, f, part, own, yd, yu, below, above):
+    first, end = part * PART, part * PART + PART + 2 * HY
+    top = HY + ROWS
+
+    def rows(src_first, src_end, src, offset, layers, to_layer):
+        r0, r1 = max(first, src_first), min(end, src_end)
+        if r0 < r1:
+            at = slice(offset + r0 - src_first, offset + r1 - src_first)
+            dst[r0 - first:r1 - first, to_layer:to_layer + layers.stop - layers.start, :] = src[f, at, layers, :]
+
+    block, tile = slice(0, COLS), slice(0, 8)
+    rows(0, HY, yd, 0, block, HZ)
+    rows(HY, top, own, 0, block, HZ)
+    rows(top, EXT, yu, 0, block, HZ)
+    for (z, rest), near, far in ((below, 4, 0), (above, HZ + COLS, HZ + COLS + 8)):
+        rows(HY, top, z, 0, tile, near)
+        rows(0, HY, rest, 0, tile, near)
+        rows(top, EXT, rest, HY, tile, near)
+        for k in range(2):
+            rows(RIM + k * HALF, RIM + (k + 1) * HALF, rest, 2 * HY, slice(4 * k, 4 * k + 4), far)
 
 
 def is_even(axis):
@@ -249,18 +275,26 @@
     near[...] = jnp.where(even, high, low)
 
 
+def tiles_kernel(own, near, far):
+    even = is_even("gz")
+    low, high = own[:, :, 0:8, :], own[:, :, 8:16, :]
+    near[...] = jnp.where(even, high, low)
+    far[...] = jnp.where(even, low, high)
+
+
 def pack_kernel(own, far, near, yd, yu, z_near, z_far):
     even = is_even("gy")
     yd[...] = jnp.where(even, far[...], near[...])
     yu[...] = jnp.where(even, near[...], far[...])
 
     def pack(dst, whole, part):
-        for r0, r1, src in ((0, HY, yd), (HY, HY + ROWS, own), (HY + ROWS, EXT, yu)):
-            dst[:, r0:r1] = src[:, :, whole:whole + 8, :]
-        dst[:, EXT:EXT + HY, 0:4, :] = yd[:, :, part:part + 4, :]
-        dst[:, EXT + HY:, 0:4, :] = own[:, 0:HALF - HY, part:part + 4, :]
-        dst[:, EXT:EXT + HALF - HY, 4:8, :] = own[:, HALF - HY:, part:part + 4, :]
-        dst[:, EXT + HALF - HY:, 4:8, :] = yu[:, :, part:part + 4, :]
+        dst[:, 0:HY] = yd[:, :, whole:whole + 8, :]
+        dst[:, HY:2 * HY] = yu[:, :, whole:whole + 8, :]
+        at, edge = 2 * HY, HY - RIM
+        dst[:, at:at + edge, 0:4, :] = yd[:, RIM:, part:part + 4, :]
+        dst[:, at + edge:, 0:4, :] = own[:, 0:HALF - edge, part:part + 4, :]
+        dst[:, at:at + HALF - edge, 4:8, :] = own[:, HALF - edge:, part:part + 4, :]
+        dst[:, at + HALF - edge:, 4:8, :] = yu[:, 0:edge, part:part + 4, :]
 
     @pl.when(is_even("gz"))
     def _():
@@ -335,12 +369,12 @@
     def side(window, layer):
         @pl.when(is_forward)
         def _():
-            forward(edge, None, window, 2, early, mid)
-            adjoint(edge, window, 2, (mid[4], window[1]), None, (early[5], window[0]), mid, late, None)
+            forward(edge, None, window, 1, early, mid)
+            adjoint(edge, window, 1, (mid[4], window[1]), None, (early[5], window[0]), mid, late, None)
 
         @pl.when(jnp.logical_not(is_forward))
         def _():
-            adjoint(edge, window, 2, (early[0], window[0]), (early[1], window[0]), None, mid, late, None)
+            adjoint(edge, window, 1, (early[0], window[0]), (early[1], window[0]), None, mid, late, None)
 
         sums[...] = wall_tiles(layer, late[1], late[7], held)
 
@@ -352,15 +386,14 @@
     def _():
         side(UPPER, 7)
 
-    lane = iota((1, LANES), 1)
-    out = jnp.where(lane == VOLT, volts[0], jnp.where(lane == VOLT + 1, volts[1], sums[...]))
-    row[...] = jnp.broadcast_to(out, row.shape)
-
-
-def bulk_kernel(part, own, yd, yu, far, near, main, send, *refs):
+    row[...] = jnp.broadcast_to(sums[...] + volts[...], row.shape)
+
+
+def bulk_kernel(part, own, yd, yu, z_far, z_near, far, near, main, send, *refs):
+    far, near = (z_far, far), (z_near, near)
     early, mid, late = split(refs)
     ylo, yhi, zlo, zhi = edges()
-    edge = (ylo, None, zlo, zhi) if part == 0 else (None, yhi, zlo, zhi)
+    edge = (ylo if part == 0 else None, yhi if part == PARTS - 1 else None, zlo, zhi)
     is_forward = lax.axis_index("grp") == 0
 
     @pl.when(is_even("gz"))
@@ -392,17 +425,19 @@
         adjoint(edge, BULK, 1, (early[0], BULK[0]), (early[1], BULK[0]), None, mid, late, into(main))
 
 
-def volts_kernel(lower, upper, rows, near, labels, response, out, grad, *refs):
-    early, mid, late = split(refs)
-    ghost = refs[21]
+def volts_kernel(*refs):
+    parts, refs = refs[:PARTS], refs[PARTS:]
+    rows, near, labels, response, out, grad = refs[:6]
+    early, mid, late = split(refs[6:])
+    ghost = refs[27]
     ylo, yhi, zlo, zhi = edges()
     edge = (ylo, yhi, None, None)
     is_forward = lax.axis_index("grp") == 0
     n = rows.shape[0]
     first = jnp.broadcast_to(rows[:, VOLT:VOLT + 1], (n, LANES))
     second = jnp.broadcast_to(rows[:, VOLT + 1:VOLT + 2], (n, LANES))
-    out[:, 0:PART] = lower[...]
-    out[:, PART:] = upper[...]
+    for i, part in enumerate(parts):
+        out[:, i * PART:(i + 1) * PART] = part[...]
 
     @pl.when(jnp.logical_or(zlo, zhi))
     def _():
@@ -440,9 +475,11 @@
     grad[...] = jnp.where(iota((1, 2), 1) == 0, total[0], total[1])
 
 
-def sum_kernel(main, lower, upper, out):
-    out[0, :, 0:PART] = main[:, 0:PART] + lower[...]
-    out[0, :, PART:] = main[:, PART:] + upper[...]
+def sum_kernel(main, *refs):
+    out = refs[PARTS]
+    for i in range(PARTS):
+        at = slice(i * PART, (i + 1) * PART)
+        out[0, :, at] = main[:, at] + refs[i][...]
 
 
 def wall_response():
@@ -498,6 +535,10 @@
     return jax.ShapeDtypeStruct(dims, jnp.float32)
 
 
+def kept(*dims):
+    return pltpu.VMEM(dims, jnp.float32)
+
+
 def swapped(array, axis, first):
     pairs = []
     for i in range(first, lax.axis_size(axis) - 1, 2):
@@ -510,8 +551,9 @@
     labels = tile_owner[..., 0]
     gy, gz = lax.axis_index("gy"), lax.axis_index("gz")
     devices = lax.axis_size(AXES)
-    half = shape(2, PART, COLS, LANES)
-    strip, slab = shape(2, HY, COLS, LANES), shape(2, EXT * 3 // 2, 8, LANES)
+    half = kept(2, PART, COLS, LANES)
+    strip, tiles = kept(2, HY, COLS, LANES), kept(2, ROWS, 8, LANES)
+    slab = kept(2, 2 * HY + HALF, 8, LANES)
 
     def limit(mib):
         return pltpu.CompilerParams(vmem_limit_bytes=mib * 1024 * 1024)
@@ -521,48 +563,57 @@
     )(own)
     far = swapped(far, "gy", 1)
     near = swapped(near, "gy", 0)
-    yd, yu, z_near, z_far = pl.pallas_call(
+    mine, near = lax.optimization_barrier((own, near))
+    z_near, z_far = pl.pallas_call(
+        tiles_kernel, out_shape=(tiles, tiles), in_specs=vmem(1), out_specs=vmem(2), compiler_params=limit(8),
+    )(mine)
+    z_far = swapped(z_far, "gz", 1)
+    z_near = swapped(z_near, "gz", 0)
+    yd, yu, near, far = pl.pallas_call(
         pack_kernel, out_shape=(strip, strip, slab, slab), in_specs=vmem(3), out_specs=vmem(4), compiler_params=limit(8),
     )(own, far, near)
-    far = swapped(z_far, "gz", 1)
-    near = swapped(z_near, "gz", 0)
-
-    mine, _ = lax.optimization_barrier((own, z_far))
+    mine, _ = lax.optimization_barrier((own, far))
+    far = swapped(far, "gz", 1)
+    near = swapped(near, "gz", 0)
+
+    volts = jnp.pad(electrode_volts, (VOLT, LANES - VOLT - 2))[None]
     row = pl.pallas_call(
-        wall_kernel, out_shape=shape(devices, LANES),
-        in_specs=vmem(3) + [pl.BlockSpec(memory_space=pltpu.SMEM)], out_specs=vmem(1)[0],
+        wall_kernel, out_shape=kept(devices, LANES),
+        in_specs=vmem(4), out_specs=vmem(1)[0],
         scratch_shapes=scratch(EXT, LOWER) + [pltpu.VMEM((8, LANES), jnp.float32), pltpu.VMEM((1, LANES), jnp.float32)],
         compiler_params=limit(12),
-    )(mine, yd, yu, electrode_volts)
+    )(mine, yd, yu, volts)
     rows = lax.all_to_all(row, AXES, 0, 0, tiled=True)
 
     mine, _ = lax.optimization_barrier((own, row))
     def bulk(part, block, load):
         return pl.pallas_call(
-            functools.partial(bulk_kernel, part), out_shape=(half, half), in_specs=vmem(5), out_specs=vmem(2),
+            functools.partial(bulk_kernel, part), out_shape=(half, half), in_specs=vmem(7), out_specs=vmem(2),
             scratch_shapes=scratch(PART + 2 * HY, BULK), compiler_params=limit(20),
             cost_estimate=pl.CostEstimate(flops=10 ** 8, bytes_accessed=load * 10 ** 6, transcendentals=0),
-        )(block, yd, yu, far, near)
-
-    main0, send = bulk(0, mine, 36)
-    lower = lax.ppermute(send, "grp", [(0, 1)])
-    mine, _ = lax.optimization_barrier((own, send))
-    main1, send = bulk(1, mine, 9)
-    send, rows = lax.optimization_barrier((send, rows))
-    upper = lax.ppermute(send, "grp", [(0, 1)])
+        )(block, yd, yu, z_far, z_near, far, near)
+
+    mains, extras = [], []
+    for part in range(PARTS):
+        main, send = bulk(part, mine, 36 if part == 0 else 9)
+        mains.append(main)
+        mine, _ = lax.optimization_barrier((own, send))
+        if part == PARTS - 1:
+            send, rows = lax.optimization_barrier((send, rows))
+        extras.append(lax.ppermute(send, "grp", [(0, 1)]))
 
     fenced = jnp.pad(labels, ((0, 0), (1, 1), (0, 0)), constant_values=-1)
     side = (gz == lax.axis_size("gz") - 1).astype(jnp.int32)
     by_wall = lax.dynamic_slice(fenced, (side, gy * TY, 0), (1, 8, 16)).reshape(1, LANES)
     by_block = jnp.pad(labels.reshape(2, 8, TY * 16), ((0, 0), (0, 0), (0, LANES - TY * 16)), constant_values=-1)
     total, grad = pl.pallas_call(
-        volts_kernel, out_shape=(shape(2, ROWS, COLS, LANES), shape(1, 2)), in_specs=vmem(6), out_specs=vmem(2),
+        volts_kernel, out_shape=(kept(2, ROWS, COLS, LANES), shape(1, 2)), in_specs=vmem(PARTS + 4), out_specs=vmem(2),
         scratch_shapes=scratch(EXT, NEAR) + [pltpu.VMEM((EXT, COLS, LANES), jnp.float32)], compiler_params=limit(16),
-    )(main0, main1, rows, by_wall, by_block, response)
+    )(*mains, rows, by_wall, by_block, response)
     advanced = pl.pallas_call(
-        sum_kernel, out_shape=shape(1, 2, ROWS, COLS, LANES), in_specs=vmem(3), out_specs=vmem(1)[0],
+        sum_kernel, out_shape=shape(1, 2, ROWS, COLS, LANES), in_specs=vmem(PARTS + 1), out_specs=vmem(1)[0],
         compiler_params=limit(8),
-    )(total, lower, upper)
+    )(total, *extras)
     return (advanced, grad.reshape(2))
 
 

time: 63.2 us -> 60.6 us (0.959)
  the two profiles are of different devices: /device:TPU:120 before, /device:TPU:32 now
where the time goes in v5:
time: 60.6 us; the launch traced here: 60 us
  starting transfers between devices  30.6 us (50%)
  Pallas kernels  14.4 us (24%)
  waiting for transfers between devices  9.14 us (15%)
  local copies, waits for them, and re-layouts  5.05 us (8%)
  between operations  0.8 us (1%)
    all_to_all x1, starting transfers between devices, per_device(): rows = lax.all_to_all(row, AXES, 0, 0, tiled=True)  17.3 us
    ppermute x6, starting transfers between devices, swapped(): return lax.ppermute(array, axis, pairs)  10.7 us
    pallas_call x1, Pallas kernels, per_device(): pl.pallas_call(volts_kernel, out_shape=(kept(2, ROWS, COLS, LANES), shape...  5.47 us
    pallas_call x2, Pallas kernels, bulk(): pl.pallas_call(functools.partial(bulk_kernel, part), out_shape=(half, hal...  4.93 us
    unnamed x17, local copies, waits for them, and re-layouts  4.66 us
    all_to_all x1, waiting for transfers between devices, per_device(): rows = lax.all_to_all(row, AXES, 0, 0, tiled=True)  4.48 us
    ppermute x2, waiting for transfers between devices, per_device(): extras.append(lax.ppermute(send, 'grp', [(0, 1)]))  4.12 us
    ppermute x2, starting transfers between devices, per_device(): extras.append(lax.ppermute(send, 'grp', [(0, 1)]))  2.56 us
  transfers between devices with their start and end apart: 9, of which 3 were waited for; matrix products, arithmetic and copies ran while one was open for 1% of the time, Pallas kernels for 22%

profile of v5, /device:TPU:32, one launch (start us, length us, event | category | flops | bytes accessed | tf_op | source)
XLA Modules:
  0.0 60.0 jit_solution(6295496477881118286)
XLA Ops:
  0.6 1.1 %copy-done = f32[1,2,48,16,128]{4,3,2,1,0:T(8,128)S(1)} copy-done((f32[1,2,48,16,128]{4,3,2,1,0:T(8,128)S(1)}, f32[1,2,48,16,128]{4,3,2,1,0:T(8,128)}, u32[]{:S(2)}) %copy-start) | copy-done | bytes 786456
  1.8 0.1 collective-permute-start.1
  1.9 0.8 %collective-permute-start = (f32[2,8,16,128]{3,2,1,0:T(8,128)S(1)}, f32[2,8,16,128]{3,2,1,0:T(8,128)S(1)}, u32[]{:S(2)}, u32[]{:S(2)}) collective-permute-start(f32[2,8,16,128]{3,2,1,0:T(8,128)S(1)} %get-tuple-element.23), channel_id=1, source_target_pairs={{16,32},{32,16},{48,64},{64,48},{80,96},{96,80},{17,33},{33,17},{4... | collective-permute-start | bytes 393224 | tf_op jit(solution)/shard_map/ppermute | solution.py:546
  2.7 0.5 collective-permute-done.1.near
  3.3 0.7 %collective-permute-start.2 = (f32[2,48,8,128]{3,2,1,0:T(8,128)S(1)}, f32[2,48,8,128]{3,2,1,0:T(8,128)S(1)}, u32[]{:S(2)}, u32[]{:S(2)}) collective-permute-start(f32[2,48,8,128]{3,2,1,0:T(8,128)S(1)} %get-tuple-element.32), channel_id=1, source_target_pairs={{1,2},{2,1},{3,4},{4,3},{5,6},{6,5},{7,8},{8,7},{9,10},{10,9},{11,... | collective-permute-start | bytes 1179656 | tf_op jit(solution)/shard_map/ppermute | solution.py:546
  4.0 4.3 %collective-permute-start.3 = (f32[2,48,8,128]{3,2,1,0:T(8,128)S(1)}, f32[2,48,8,128]{3,2,1,0:T(8,128)S(1)}, u32[]{:S(2)}, u32[]{:S(2)}) collective-permute-start(f32[2,48,8,128]{3,2,1,0:T(8,128)S(1)} %get-tuple-element.33), channel_id=1, source_target_pairs={{0,1},{1,0},{2,3},{3,2},{4,5},{5,4},{6,7},{7,6},{8,9},{9,8},{10,11... | collective-permute-start | bytes 1179656 | tf_op jit(solution)/shard_map/ppermute | solution.py:546
  8.3 1.0 %shard_map.60 = (f32[2,8,16,128]{3,2,1,0:T(8,128)S(1)}, f32[2,8,16,128]{3,2,1,0:T(8,128)S(1)}, f32[2,44,8,128]{3,2,1,0:T(8,128)}, f32[2,44,8,128]{3,2,1,0:T(8,128)}) custom-call(f32[2,48,16,128]{3,2,1,0:T(8,128)S(1)} %bitcast.15, f32[2,8,16,128]{3,2,1,0:T(8,128)S(1)} %collective-permute-done.far, f32[2,8,16,128]{3,2,1,0:T(8,128)S(1)} %collective-permute-done.1.near), custom_call_target="tpu_custom_call" | custom-call | tf_op jit(solution)/shard_map/pallas_call | solution.py:572
  9.3 0.8 %collective-permute-start.4 = (f32[2,44,8,128]{3,2,1,0:T(8,128)}, f32[2,44,8,128]{3,2,1,0:T(8,128)S(1)}, u32[]{:S(2)}, u32[]{:S(2)}) collective-permute-start(f32[2,44,8,128]{3,2,1,0:T(8,128)} %get-tuple-element.26), channel_id=1, source_target_pairs={{1,2},{2,1},{3,4},{4,3},{5,6},{6,5},{7,8},{8,7},{9,10},{10,9},{11,... | collective-permute-start | bytes 1081352 | tf_op jit(solution)/shard_map/ppermute | solution.py:546
  10.1 4.0 %collective-permute-start.5 = (f32[2,44,8,128]{3,2,1,0:T(8,128)}, f32[2,44,8,128]{3,2,1,0:T(8,128)S(1)}, u32[]{:S(2)}, u32[]{:S(2)}) collective-permute-start(f32[2,44,8,128]{3,2,1,0:T(8,128)} %get-tuple-element.34), channel_id=1, source_target_pairs={{0,1},{1,0},{2,3},{3,2},{4,5},{5,4},{6,7},{7,6},{8,9},{9,8},{10,11... | collective-permute-start | bytes 1081352 | tf_op jit(solution)/shard_map/ppermute | solution.py:546
  14.2 1.9 %shard_map.61 = f32[256,128]{1,0:T(8,128)} custom-call(f32[2,48,16,128]{3,2,1,0:T(8,128)S(1)} %bitcast.16, f32[2,8,16,128]{3,2,1,0:T(8,128)S(1)} %get-tuple-element.28.yd, f32[2,8,16,128]{3,2,1,0:T(8,128)S(1)} %get-tuple-element.29.yu, f32[1,128]{1,0:T(1,128)S(1)} %pad_bitcast_fusion.volts), custom_call_target="tpu_custom_call" | custom-call | tf_op jit(solution)/shard_map/pallas_call | solution.py:580
  16.1 17.3 %all-to-all-start = ((f32[256,1,128]{2,1,0:T(1,128)}), f32[256,1,128]{2,1,0:T(1,128)S(1)}, u32[]{:S(2)}, u32[]{:S(2)}) async-start(f32[256,1,128]{2,1,0:T(1,128)} %bitcast.3), calls=%async_computation | async-start | bytes 262144 | tf_op jit(solution)/shard_map/all_to_all | solution.py:586
  33.5 3.0 %shard_map.63 = (f32[2,24,16,128]{3,2,1,0:T(8,128)S(1)}, f32[2,24,16,128]{3,2,1,0:T(8,128)}) custom-call(f32[2,48,16,128]{3,2,1,0:T(8,128)S(1)} %bitcast.17, f32[2,8,16,128]{3,2,1,0:T(8,128)S(1)} %get-tuple-element.28.yd, f32[2,8,16,128]{3,2,1,0:T(8,128)S(1)} %get-tuple-element.29.yu, f32[2,48,8,128]{3,2,1,0:T(8,128)S(1)} %collective-permute-done.2.z_far, ...), custom_call_target="tpu_custom_call" | custom-call | flops 100000000 | bytes 36000000 | tf_op jit(solution)/shard_map/pallas_call | solution.py:590
  36.4 1.3 %collective-permute-start.6 = (f32[2,24,16,128]{3,2,1,0:T(8,128)}, f32[2,24,16,128]{3,2,1,0:T(8,128)S(1)}, u32[]{:S(2)}, u32[]{:S(2)}) collective-permute-start(f32[2,24,16,128]{3,2,1,0:T(8,128)} %get-tuple-element.36), channel_id=1, source_target_pairs={{0,128},{1,129},{2,130},{3,131},{4,132},{5,133},{6,134},{7,135},{8... | collective-permute-start | bytes 1179656 | tf_op jit(solution)/shard_map/ppermute | solution.py:603
  37.7 2.0 %shard_map.64 = (f32[2,24,16,128]{3,2,1,0:T(8,128)S(1)}, f32[2,24,16,128]{3,2,1,0:T(8,128)S(1)}) custom-call(f32[2,48,16,128]{3,2,1,0:T(8,128)S(1)} %bitcast.18, f32[2,8,16,128]{3,2,1,0:T(8,128)S(1)} %get-tuple-element.28.yd, f32[2,8,16,128]{3,2,1,0:T(8,128)S(1)} %get-tuple-element.29.yu, f32[2,48,8,128]{3,2,1,0:T(8,128)S(1)} %collective-permute-done.2.z_far, ...), custom_call_target="tpu_custom_call" | custom-call | flops 100000000 | bytes 9000000 | tf_op jit(solution)/shard_map/pallas_call | solution.py:590
  39.7 0.7 %copy-done.2 = f32[2,24,16,128]{3,2,1,0:T(8,128)} copy-done((f32[2,24,16,128]{3,2,1,0:T(8,128)}, f32[2,24,16,128]{3,2,1,0:T(8,128)S(1)}, u32[]{:S(2)}) %copy-start.2) | copy-done | bytes 393240
  40.5 0.7 %copy-done.5 = f32[2,24,16,128]{3,2,1,0:T(8,128)} copy-done((f32[2,24,16,128]{3,2,1,0:T(8,128)}, f32[2,24,16,128]{3,2,1,0:T(8,128)S(1)}, u32[]{:S(2)}) %copy-start.5) | copy-done | bytes 393240
  41.2 4.5 %all-to-all-done = f32[256,1,128]{2,1,0:T(1,128)S(1)} async-done(((f32[256,1,128]{2,1,0:T(1,128)}), f32[256,1,128]{2,1,0:T(1,128)S(1)}, u32[]{:S(2)}, u32[]{:S(2)}) %all-to-all-start) | async-done | bytes 131104 | tf_op jit(solution)/shard_map/all_to_all | solution.py:586
  45.7 1.3 %collective-permute-start.7 = (f32[2,24,16,128]{3,2,1,0:T(8,128)}, f32[2,24,16,128]{3,2,1,0:T(8,128)S(1)}, u32[]{:S(2)}, u32[]{:S(2)}) collective-permute-start(f32[2,24,16,128]{3,2,1,0:T(8,128)} %copy-done.5), channel_id=1, source_target_pairs={{0,128},{1,129},{2,130},{3,131},{4,132},{5,133},{6,134},{7,135},{8... | collective-permute-start | bytes 1179656 | tf_op jit(solution)/shard_map/ppermute | solution.py:603
  47.2 0.1 reshape.12.refs_3_
  47.4 1.0 %copy-done.3 = f32[2,24,16,128]{3,2,1,0:T(8,128)S(1)} copy-done((f32[2,24,16,128]{3,2,1,0:T(8,128)S(1)}, f32[2,24,16,128]{3,2,1,0:T(8,128)}, u32[]{:S(2)}) %copy-start.3) | copy-done | bytes 393240
  48.4 1.0 %copy-done.4 = f32[128,640]{1,0:T(8,128)S(1)} copy-done((f32[128,640]{1,0:T(8,128)S(1)}, f32[128,640]{1,0:T(8,128)}, u32[]{:S(2)}) %copy-start.4) | copy-done | bytes 327704
  49.4 5.5 %shard_map.65 = (f32[2,48,16,128]{3,2,1,0:T(8,128)S(1)}, f32[1,2]{1,0:T(1,128)}) custom-call(f32[2,24,16,128]{3,2,1,0:T(8,128)S(1)} %get-tuple-element.35.refs_0_, f32[2,24,16,128]{3,2,1,0:T(8,128)S(1)} %copy-done.3, f32[256,128]{1,0:T(8,128)S(1)} %bitcast.19, s32[1,128]{1,0:T(1,128)S(1)} %reshape.12.refs_3_, s32[2,8,128]{2,1,0:T(8,128)S(1)} %pad.14.refs_4_, ...), custom_call_target="tpu_custom_call" | custom-call | tf_op jit(solution)/shard_map/pallas_call | solution.py:609
  54.9 4.1 %collective-permute-done.7.refs_1_ = f32[2,24,16,128]{3,2,1,0:T(8,128)S(1)} collective-permute-done((f32[2,24,16,128]{3,2,1,0:T(8,128)}, f32[2,24,16,128]{3,2,1,0:T(8,128)S(1)}, u32[]{:S(2)}, u32[]{:S(2)}) %collective-permute-start.7) | collective-permute-done | bytes 393248 | tf_op jit(solution)/shard_map/ppermute | solution.py:603
  59.0 1.0 %shard_map.66 = f32[1,2,48,16,128]{4,3,2,1,0:T(8,128)} custom-call(f32[2,48,16,128]{3,2,1,0:T(8,128)S(1)} %get-tuple-element.41.main, f32[2,24,16,128]{3,2,1,0:T(8,128)S(1)} %collective-permute-done.6.refs_0_, f32[2,24,16,128]{3,2,1,0:T(8,128)S(1)} %collective-permute-done.7.refs_1_), custom_call_target="tpu_custom_call" | custom-call | tf_op jit(solution)/shard_map/pallas_call | solution.py:613
  (25 shorter events, 0.5 us)
Async XLA Ops:
  0.6 1.1 %copy-start = (f32[1,2,48,16,128]{4,3,2,1,0:T(8,128)S(1)}, f32[1,2,48,16,128]{4,3,2,1,0:T(8,128)}, u32[]{:S(2)}) copy-start(f32[1,2,48,16,128]{4,3,2,1,0:T(8,128)} %param.4) | copy-start | bytes 2359300
  1.8 1.5 %copy-start.1 = (f32[1,2,48,16,128]{4,3,2,1,0:T(8,128)S(1)}, f32[1,2,48,16,128]{4,3,2,1,0:T(8,128)}, u32[]{:S(2)}) copy-start(f32[1,2,48,16,128]{4,3,2,1,0:T(8,128)} %param.4) | copy-start | bytes 2359300
  1.8 1.4 %collective-permute-start.1 = (f32[2,8,16,128]{3,2,1,0:T(8,128)S(1)}, f32[2,8,16,128]{3,2,1,0:T(8,128)S(1)}, u32[]{:S(2)}, u32[]{:S(2)}) collective-permute-start(f32[2,8,16,128]{3,2,1,0:T(8,128)S(1)} %get-tuple-element.24), channel_id=1, source_target_pairs={{0,16},{16,0},{32,48},{48,32},{64,80},{80,64},{96,112},{112,96},{1... | collective-permute-start | bytes 393224 | tf_op jit(solution)/shard_map/ppermute | solution.py:546
  1.9 6.4 %collective-permute-start = (f32[2,8,16,128]{3,2,1,0:T(8,128)S(1)}, f32[2,8,16,128]{3,2,1,0:T(8,128)S(1)}, u32[]{:S(2)}, u32[]{:S(2)}) collective-permute-start(f32[2,8,16,128]{3,2,1,0:T(8,128)S(1)} %get-tuple-element.23), channel_id=1, source_target_pairs={{16,32},{32,16},{48,64},{64,48},{80,96},{96,80},{17,33},{33,17},{4... | collective-permute-start | bytes 393224 | tf_op jit(solution)/shard_map/ppermute | solution.py:546
  3.3 30.2 %collective-permute-start.2 = (f32[2,48,8,128]{3,2,1,0:T(8,128)S(1)}, f32[2,48,8,128]{3,2,1,0:T(8,128)S(1)}, u32[]{:S(2)}, u32[]{:S(2)}) collective-permute-start(f32[2,48,8,128]{3,2,1,0:T(8,128)S(1)} %get-tuple-element.32), channel_id=1, source_target_pairs={{1,2},{2,1},{3,4},{4,3},{5,6},{6,5},{7,8},{8,7},{9,10},{10,9},{11,... | collective-permute-start | bytes 1179656 | tf_op jit(solution)/shard_map/ppermute | solution.py:546
  4.0 29.5 %collective-permute-start.3 = (f32[2,48,8,128]{3,2,1,0:T(8,128)S(1)}, f32[2,48,8,128]{3,2,1,0:T(8,128)S(1)}, u32[]{:S(2)}, u32[]{:S(2)}) collective-permute-start(f32[2,48,8,128]{3,2,1,0:T(8,128)S(1)} %get-tuple-element.33), channel_id=1, source_target_pairs={{0,1},{1,0},{2,3},{3,2},{4,5},{5,4},{6,7},{7,6},{8,9},{9,8},{10,11... | collective-permute-start | bytes 1179656 | tf_op jit(solution)/shard_map/ppermute | solution.py:546
  9.3 4.8 %copy-start.7 = (f32[2]{0:T(128)S(1)}, f32[2]{0:T(128)}, u32[]{:S(2)}) copy-start(f32[2]{0:T(128)} %param.6) | copy-start | bytes 28
  9.3 24.2 %collective-permute-start.4 = (f32[2,44,8,128]{3,2,1,0:T(8,128)}, f32[2,44,8,128]{3,2,1,0:T(8,128)S(1)}, u32[]{:S(2)}, u32[]{:S(2)}) collective-permute-start(f32[2,44,8,128]{3,2,1,0:T(8,128)} %get-tuple-element.26), channel_id=1, source_target_pairs={{1,2},{2,1},{3,4},{4,3},{5,6},{6,5},{7,8},{8,7},{9,10},{10,9},{11,... | collective-permute-start | bytes 1081352 | tf_op jit(solution)/shard_map/ppermute | solution.py:546
  10.1 23.4 %collective-permute-start.5 = (f32[2,44,8,128]{3,2,1,0:T(8,128)}, f32[2,44,8,128]{3,2,1,0:T(8,128)S(1)}, u32[]{:S(2)}, u32[]{:S(2)}) collective-permute-start(f32[2,44,8,128]{3,2,1,0:T(8,128)} %get-tuple-element.34), channel_id=1, source_target_pairs={{0,1},{1,0},{2,3},{3,2},{4,5},{5,4},{6,7},{7,6},{8,9},{9,8},{10,11... | collective-permute-start | bytes 1081352 | tf_op jit(solution)/shard_map/ppermute | solution.py:546
  16.1 29.6 %all-to-all-start = ((f32[256,1,128]{2,1,0:T(1,128)}), f32[256,1,128]{2,1,0:T(1,128)S(1)}, u32[]{:S(2)}, u32[]{:S(2)}) async-start(f32[256,1,128]{2,1,0:T(1,128)} %bitcast.3), calls=%async_computation | async-start | bytes 262144 | tf_op jit(solution)/shard_map/all_to_all | solution.py:586
  36.4 18.4 %collective-permute-start.6 = (f32[2,24,16,128]{3,2,1,0:T(8,128)}, f32[2,24,16,128]{3,2,1,0:T(8,128)S(1)}, u32[]{:S(2)}, u32[]{:S(2)}) collective-permute-start(f32[2,24,16,128]{3,2,1,0:T(8,128)} %get-tuple-element.36), channel_id=1, source_target_pairs={{0,128},{1,129},{2,130},{3,131},{4,132},{5,133},{6,134},{7,135},{8... | collective-permute-start | bytes 1179656 | tf_op jit(solution)/shard_map/ppermute | solution.py:603
  39.7 0.7 %copy-start.2 = (f32[2,24,16,128]{3,2,1,0:T(8,128)}, f32[2,24,16,128]{3,2,1,0:T(8,128)S(1)}, u32[]{:S(2)}) copy-start(f32[2,24,16,128]{3,2,1,0:T(8,128)S(1)} %get-tuple-element.38.refs_1_) | copy-start | bytes 1179652
  40.5 0.7 %copy-start.5 = (f32[2,24,16,128]{3,2,1,0:T(8,128)}, f32[2,24,16,128]{3,2,1,0:T(8,128)S(1)}, u32[]{:S(2)}) copy-start(f32[2,24,16,128]{3,2,1,0:T(8,128)S(1)} %get-tuple-element.42) | copy-start | bytes 1179652
  41.2 5.8 %copy-start.6 = (s32[2,48,16,1]{1,3,2,0:T(1,128)S(1)}, s32[2,48,16,1]{1,3,2,0:T(1,128)}, u32[]{:S(2)}) copy-start(s32[2,48,16,1]{1,3,2,0:T(1,128)} %param.5) | copy-start | bytes 18436
  45.7 13.3 %collective-permute-start.7 = (f32[2,24,16,128]{3,2,1,0:T(8,128)}, f32[2,24,16,128]{3,2,1,0:T(8,128)S(1)}, u32[]{:S(2)}, u32[]{:S(2)}) collective-permute-start(f32[2,24,16,128]{3,2,1,0:T(8,128)} %copy-done.5), channel_id=1, source_target_pairs={{0,128},{1,129},{2,130},{3,131},{4,132},{5,133},{6,134},{7,135},{8... | collective-permute-start | bytes 1179656 | tf_op jit(solution)/shard_map/ppermute | solution.py:603
  47.4 1.0 %copy-start.3 = (f32[2,24,16,128]{3,2,1,0:T(8,128)S(1)}, f32[2,24,16,128]{3,2,1,0:T(8,128)}, u32[]{:S(2)}) copy-start(f32[2,24,16,128]{3,2,1,0:T(8,128)} %copy-done.2) | copy-start | bytes 1179652
  48.4 1.0 %copy-start.4 = (f32[128,640]{1,0:T(8,128)S(1)}, f32[128,640]{1,0:T(8,128)}, u32[]{:S(2)}) copy-start(f32[128,640]{1,0:T(8,128)} %constant.25.clone.refs_5_) | copy-start | bytes 983044

commit v6 on v5

--- a/solution.py
+++ b/solution.py
@@ -16,7 +16,7 @@
 EXT = ROWS + 2 * HY
 RIM = 4
 HALF = EXT // 2 - RIM
-PARTS = 2
+PARTS = 3
 PART = ROWS // PARTS
 SIXTH = 1.0 / 6.0
 SHARE, PIECES = 0.34, 3
@@ -48,9 +48,11 @@
     return zp, zm
 
 
-def beside(c):
+def beside(c, share):
     n, z, _ = c.shape
-    k = int(n * SHARE)
+    k = int(n * share)
+    if k == 0:
+        return pltpu.roll(c, 1, 2) + pltpu.roll(c, LANES - 1, 2)
     row = lax.broadcasted_iota(jnp.int32, (LANES, LANES), 0)
     lane = lax.broadcasted_iota(jnp.int32, (LANES, LANES), 1)
     apart = (row - lane) & (LANES - 1)
@@ -70,7 +72,7 @@
     c = w[1:-1]
     zp, zm = zshift(c, closed)
     s = (w[:-2] + w[2:]) + (zp + zm)
-    return c, s + beside(c), zp - zm
+    return c, s + beside(c, 0.0 if closed else SHARE), zp - zm
 
 
 def zero_edges(edge, ref, at):
@@ -239,7 +241,7 @@
         zp, zm = zshift(T2[pl.ds(r, n)], closed)
         u = B[pl.ds(r, n)] + 0.5 * (zp - zm)
         give(r - HY, n, u[:, own], s[:, own] * SIXTH)
-    rows_loop(8, top - 8, stage_l, pieces)
+    rows_loop(8, top - 8, stage_l, 2)
 
 
 def load_extended(dst, f, part, own, yd, yu, below, above):
@@ -282,7 +284,7 @@
     far[...] = jnp.where(even, low, high)
 
 
-def pack_kernel(own, far, near, yd, yu, z_near, z_far):
+def pack_kernel(own, far, near, yd, yu, near_out, far_out, z_near, z_far, sems):
     even = is_even("gy")
     yd[...] = jnp.where(even, far[...], near[...])
     yu[...] = jnp.where(even, near[...], far[...])
@@ -296,15 +298,22 @@
         dst[:, at:at + HALF - edge, 4:8, :] = own[:, HALF - edge:, part:part + 4, :]
         dst[:, at + HALF - edge:, 4:8, :] = yu[:, 0:edge, part:part + 4, :]
 
-    @pl.when(is_even("gz"))
-    def _():
-        pack(z_near, 8, 4)
-        pack(z_far, 0, 8)
-
-    @pl.when(jnp.logical_not(is_even("gz")))
-    def _():
-        pack(z_near, 0, 8)
-        pack(z_far, 8, 4)
+    copies = [pltpu.make_async_copy(*pair, sems.at[i]) for i, pair in enumerate(((z_far, far_out), (z_near, near_out)))]
+    upward = is_even("gz")
+
+    def fill(dst, when, copy):
+        @pl.when(when)
+        def _():
+            pack(dst, 8, 4)
+
+        @pl.when(jnp.logical_not(when))
+        def _():
+            pack(dst, 0, 8)
+        copy.start()
+    fill(z_far, jnp.logical_not(upward), copies[0])
+    fill(z_near, upward, copies[1])
+    for copy in copies:
+        copy.wait()
 
 
 HIGHEST = lax.Precision.HIGHEST
@@ -389,9 +398,10 @@
     row[...] = jnp.broadcast_to(sums[...] + volts[...], row.shape)
 
 
-def bulk_kernel(part, own, yd, yu, z_far, z_near, far, near, main, send, *refs):
+def bulk_kernel(part, own, yd, yu, z_far, z_near, far, near, main_out, send_out, *refs):
     far, near = (z_far, far), (z_near, near)
     early, mid, late = split(refs)
+    main, send, sems = refs[21:]
     ylo, yhi, zlo, zhi = edges()
     edge = (ylo if part == 0 else None, yhi if part == PARTS - 1 else None, zlo, zhi)
     is_forward = lax.axis_index("grp") == 0
@@ -406,56 +416,77 @@
         for f in range(2):
             load_extended(early[f], f, part, own, yd, yu, near, far)
 
-    def into(ref):
+    def leave(ref, out, rows, copies):
+        copy = pltpu.make_async_copy(ref.at[:, rows], out.at[:, rows], sems.at[len(copies)])
+        copy.start()
+        copies.append(copy)
+
+    def into(ref, out, copies):
         def give(r, n, u, p):
             ref[0, pl.ds(r, n)] = u
             ref[1, pl.ds(r, n)] = p
+            leave(ref, out, pl.ds(r, n), copies)
         return give
 
     @pl.when(is_forward)
     def _():
+        copies = []
         forward(edge, None, BULK, 1, early, mid)
         at = (slice(HY, HY + PART), slice(BULK[1][0], BULK[1][0] + COLS))
         main[0] = mid[4][at]
         main[1] = mid[3][at]
-        adjoint(edge, BULK, 1, (mid[4], BULK[1]), None, (early[5], BULK[0]), mid, late, into(send))
+        leave(main, main_out, pl.ds(0, PART), copies)
+        adjoint(edge, BULK, 1, (mid[4], BULK[1]), None, (early[5], BULK[0]), mid, late, into(send, send_out, copies))
+        for copy in copies:
+            copy.wait()
 
     @pl.when(jnp.logical_not(is_forward))
     def _():
-        adjoint(edge, BULK, 1, (early[0], BULK[0]), (early[1], BULK[0]), None, mid, late, into(main))
+        copies = []
+        adjoint(edge, BULK, 1, (early[0], BULK[0]), (early[1], BULK[0]), None, mid, late, into(main, main_out, copies))
+        for copy in copies:
+            copy.wait()
 
 
 def volts_kernel(*refs):
     parts, refs = refs[:PARTS], refs[PARTS:]
-    rows, near, labels, response, out, grad = refs[:6]
+    rows, near, labels, far_response, out, grad = refs[:6]
     early, mid, late = split(refs[6:])
-    ghost = refs[27]
+    ghost, response, sems = refs[27:]
+    copies = [pltpu.make_async_copy(part, out.at[:, i * PART:(i + 1) * PART], sems.at[i]) for i, part in enumerate(parts)]
+    fetch = pltpu.make_async_copy(far_response, response, sems.at[PARTS])
+    for copy in copies:
+        copy.start()
+    fetch.start()
     ylo, yhi, zlo, zhi = edges()
     edge = (ylo, yhi, None, None)
+    at_wall = jnp.logical_or(zlo, zhi)
     is_forward = lax.axis_index("grp") == 0
     n = rows.shape[0]
     first = jnp.broadcast_to(rows[:, VOLT:VOLT + 1], (n, LANES))
     second = jnp.broadcast_to(rows[:, VOLT + 1:VOLT + 2], (n, LANES))
-    for i, part in enumerate(parts):
-        out[:, i * PART:(i + 1) * PART] = part[...]
-
-    @pl.when(jnp.logical_or(zlo, zhi))
+
+    @pl.when(at_wall)
     def _():
         fill_ghost(zhi, ghost, tile_volts(first, second, near[...]))
-        forward(edge, ghost, NEAR, 2, early, mid)
-
-        @pl.when(is_forward)
-        def _():
-            out[0] += mid[4][HY:HY + ROWS]
-            out[1] += mid[3][HY:HY + ROWS]
-
-        @pl.when(jnp.logical_not(is_forward))
-        def _():
-            def give(r, n, u, p):
-                out[0, pl.ds(r, n)] += u
-                out[1, pl.ds(r, n)] += p
-            adjoint(edge, NEAR, 2, (mid[4], NEAR[1]), None, (early[5], NEAR[0]), mid, late, give)
-
+        forward(edge, ghost, NEAR, 1, early, mid)
+
+    for copy in copies:
+        copy.wait()
+
+    @pl.when(jnp.logical_and(at_wall, is_forward))
+    def _():
+        out[0] += mid[4][HY:HY + ROWS]
+        out[1] += mid[3][HY:HY + ROWS]
+
+    @pl.when(jnp.logical_and(at_wall, jnp.logical_not(is_forward)))
+    def _():
+        def give(r, n, u, p):
+            out[0, pl.ds(r, n)] += u
+            out[1, pl.ds(r, n)] += p
+        adjoint(edge, NEAR, 1, (mid[4], NEAR[1]), None, (early[5], NEAR[0]), mid, late, give)
+
+    fetch.wait()
     gy, gz = lax.axis_size("gy"), lax.axis_size("gz")
     me = (lax.axis_index("grp") * gy + lax.axis_index("gy")) * gz + lax.axis_index("gz")
     pair = [jnp.zeros((gy, LANES), jnp.float32)] * 2
@@ -539,6 +570,10 @@
     return pltpu.VMEM(dims, jnp.float32)
 
 
+def in_hbm(array):
+    return pltpu.with_memory_space_constraint(array, pltpu.HBM)
+
+
 def swapped(array, axis, first):
     pairs = []
     for i in range(first, lax.axis_size(axis) - 1, 2):
@@ -551,9 +586,9 @@
     labels = tile_owner[..., 0]
     gy, gz = lax.axis_index("gy"), lax.axis_index("gz")
     devices = lax.axis_size(AXES)
-    half = kept(2, PART, COLS, LANES)
+    half = pltpu.HBM((2, PART, COLS, LANES), jnp.float32)
     strip, tiles = kept(2, HY, COLS, LANES), kept(2, ROWS, 8, LANES)
-    slab = kept(2, 2 * HY + HALF, 8, LANES)
+    slab = pltpu.HBM((2, 2 * HY + HALF, 8, LANES), jnp.float32)
 
     def limit(mib):
         return pltpu.CompilerParams(vmem_limit_bytes=mib * 1024 * 1024)
@@ -570,26 +605,29 @@
     z_far = swapped(z_far, "gz", 1)
     z_near = swapped(z_near, "gz", 0)
     yd, yu, near, far = pl.pallas_call(
-        pack_kernel, out_shape=(strip, strip, slab, slab), in_specs=vmem(3), out_specs=vmem(4), compiler_params=limit(8),
+        pack_kernel, out_shape=(strip, strip, slab, slab), in_specs=vmem(3),
+        out_specs=vmem(2) + [pl.BlockSpec(memory_space=pl.ANY)] * 2,
+        scratch_shapes=[pltpu.VMEM((2, 2 * HY + HALF, 8, LANES), jnp.float32)] * 2 + [pltpu.SemaphoreType.DMA((2,))],
+        compiler_params=limit(8),
     )(own, far, near)
-    mine, _ = lax.optimization_barrier((own, far))
+    volts = jnp.pad(electrode_volts, (VOLT, LANES - VOLT - 2))[None]
+    row = pl.pallas_call(
+        wall_kernel, out_shape=kept(devices, LANES), in_specs=vmem(4), out_specs=vmem(1)[0],
+        scratch_shapes=scratch(EXT, LOWER) + [pltpu.VMEM((8, LANES), jnp.float32), pltpu.VMEM((1, LANES), jnp.float32)],
+        compiler_params=limit(12),
+    )(own, yd, yu, volts)
+    far, near, row = lax.optimization_barrier((far, near, row))
     far = swapped(far, "gz", 1)
     near = swapped(near, "gz", 0)
-
-    volts = jnp.pad(electrode_volts, (VOLT, LANES - VOLT - 2))[None]
-    row = pl.pallas_call(
-        wall_kernel, out_shape=kept(devices, LANES),
-        in_specs=vmem(4), out_specs=vmem(1)[0],
-        scratch_shapes=scratch(EXT, LOWER) + [pltpu.VMEM((8, LANES), jnp.float32), pltpu.VMEM((1, LANES), jnp.float32)],
-        compiler_params=limit(12),
-    )(mine, yd, yu, volts)
     rows = lax.all_to_all(row, AXES, 0, 0, tiled=True)
 
     mine, _ = lax.optimization_barrier((own, row))
     def bulk(part, block, load):
         return pl.pallas_call(
-            functools.partial(bulk_kernel, part), out_shape=(half, half), in_specs=vmem(7), out_specs=vmem(2),
-            scratch_shapes=scratch(PART + 2 * HY, BULK), compiler_params=limit(20),
+            functools.partial(bulk_kernel, part), out_shape=(half, half), in_specs=vmem(7),
+            out_specs=[pl.BlockSpec(memory_space=pl.ANY)] * 2,
+            scratch_shapes=scratch(PART + 2 * HY, BULK) + [pltpu.VMEM((2, PART, COLS, LANES), jnp.float32)] * 2
+            + [pltpu.SemaphoreType.DMA((3,))], compiler_params=limit(20),
             cost_estimate=pl.CostEstimate(flops=10 ** 8, bytes_accessed=load * 10 ** 6, transcendentals=0),
         )(block, yd, yu, z_far, z_near, far, near)
 
@@ -607,9 +645,12 @@
     by_wall = lax.dynamic_slice(fenced, (side, gy * TY, 0), (1, 8, 16)).reshape(1, LANES)
     by_block = jnp.pad(labels.reshape(2, 8, TY * 16), ((0, 0), (0, 0), (0, LANES - TY * 16)), constant_values=-1)
     total, grad = pl.pallas_call(
-        volts_kernel, out_shape=(kept(2, ROWS, COLS, LANES), shape(1, 2)), in_specs=vmem(PARTS + 4), out_specs=vmem(2),
-        scratch_shapes=scratch(EXT, NEAR) + [pltpu.VMEM((EXT, COLS, LANES), jnp.float32)], compiler_params=limit(16),
-    )(*mains, rows, by_wall, by_block, response)
+        volts_kernel, out_shape=(kept(2, ROWS, COLS, LANES), shape(1, 2)),
+        in_specs=[pl.BlockSpec(memory_space=pl.ANY)] * PARTS + vmem(3) + [pl.BlockSpec(memory_space=pl.ANY)], out_specs=vmem(2),
+        scratch_shapes=scratch(EXT, NEAR) + [pltpu.VMEM((EXT, COLS, LANES), jnp.float32), pltpu.VMEM(response.shape, jnp.float32),
+                                             pltpu.SemaphoreType.DMA((PARTS + 1,))],
+        compiler_params=limit(16),
+    )(*[in_hbm(main) for main in mains], rows, by_wall, by_block, in_hbm(response))
     advanced = pl.pallas_call(
         sum_kernel, out_shape=shape(1, 2, ROWS, COLS, LANES), in_specs=vmem(PARTS + 1), out_specs=vmem(1)[0],
         compiler_params=limit(8),

time: 60.6 us -> 58.3 us (0.962)
  local copies, waits for them, and re-layouts: 5.05 us -> 1.61 us
  Pallas kernels: 14.4 us -> 16.8 us
  waiting for transfers between devices: 9.14 us -> 8.03 us
    unnamed x17 -> x9, local copies, waits for them, and re-layouts: 4.66 us -> 1.22 us
    pallas_call x2 -> x3, Pallas kernels: 4.93 us -> 7.13 us  [bulk(): pl.pallas_call(functools.partial(bulk_kernel, part), out_shape=(half, hal...]
    all_to_all x1, waiting for transfers between devices: 4.48 us -> 2.45 us  [per_device(): rows = lax.all_to_all(row, AXES, 0, 0, tiled=True)]
    ppermute x2 -> x3, starting transfers between devices: 2.56 us -> 3.86 us  [per_device(): extras.append(lax.ppermute(send, 'grp', [(0, 1)]))]
    ppermute x6, starting transfers between devices: 10.7 us -> 9.42 us  [swapped(): return lax.ppermute(array, axis, pairs)]
    ppermute x2 -> x3, waiting for transfers between devices: 4.12 us -> 5.04 us  [per_device(): extras.append(lax.ppermute(send, 'grp', [(0, 1)]))]
  transfers between devices with their start and end apart: 9 -> 10, of which waited for: 3 -> 3; matrix products, arithmetic and copies ran while one was open for 1% -> 1% of each run, Pallas kernels for 22% -> 27%
where the time goes in v6:
time: 58.3 us; the launch traced here: 57.8 us
  starting transfers between devices  30.4 us (52%)
  Pallas kernels  16.8 us (29%)
  waiting for transfers between devices  8.03 us (14%)
  local copies, waits for them, and re-layouts  1.61 us (3%)
  between operations  0.85 us (1%)
    all_to_all x1, starting transfers between devices, per_device(): rows = lax.all_to_all(row, AXES, 0, 0, tiled=True)  17.2 us
    ppermute x6, starting transfers between devices, swapped(): return lax.ppermute(array, axis, pairs)  9.42 us
    pallas_call x3, Pallas kernels, bulk(): pl.pallas_call(functools.partial(bulk_kernel, part), out_shape=(half, hal...  7.13 us
    pallas_call x1, Pallas kernels, per_device(): pl.pallas_call(volts_kernel, out_shape=(kept(2, ROWS, COLS, LANES), shape...  5.83 us
    ppermute x3, waiting for transfers between devices, per_device(): extras.append(lax.ppermute(send, 'grp', [(0, 1)]))  5.04 us
    ppermute x3, starting transfers between devices, per_device(): extras.append(lax.ppermute(send, 'grp', [(0, 1)]))  3.86 us
    all_to_all x1, waiting for transfers between devices, per_device(): rows = lax.all_to_all(row, AXES, 0, 0, tiled=True)  2.45 us
    pallas_call x1, Pallas kernels, per_device(): pl.pallas_call(wall_kernel, out_shape=kept(devices, LANES), in_specs=vmem...  1.81 us
  transfers between devices with their start and end apart: 10, of which 3 were waited for; matrix products, arithmetic and copies ran while one was open for 1% of the time, Pallas kernels for 27%

profile of v6, /device:TPU:32, one launch (start us, length us, event | category | flops | bytes accessed | tf_op | source)
XLA Modules:
  0.0 57.8 jit_solution(11845122454916433900)
XLA Ops:
  0.6 1.1 %copy-done = f32[1,2,48,16,128]{4,3,2,1,0:T(8,128)S(1)} copy-done((f32[1,2,48,16,128]{4,3,2,1,0:T(8,128)S(1)}, f32[1,2,48,16,128]{4,3,2,1,0:T(8,128)}, u32[]{:S(2)}) %copy-start) | copy-done | bytes 786456
  1.8 0.1 collective-permute-start.1
  1.9 0.8 %collective-permute-start = (f32[2,8,16,128]{3,2,1,0:T(8,128)S(1)}, f32[2,8,16,128]{3,2,1,0:T(8,128)S(1)}, u32[]{:S(2)}, u32[]{:S(2)}) collective-permute-start(f32[2,8,16,128]{3,2,1,0:T(8,128)S(1)} %get-tuple-element.28), channel_id=1, source_target_pairs={{16,32},{32,16},{48,64},{64,48},{80,96},{96,80},{17,33},{33,17},{4... | collective-permute-start | bytes 393224 | tf_op jit(solution)/shard_map/ppermute | solution.py:581
  2.7 0.5 collective-permute-done.1.near
  3.2 0.1 shard_map.62
  3.3 0.7 %collective-permute-start.2 = (f32[2,48,8,128]{3,2,1,0:T(8,128)S(1)}, f32[2,48,8,128]{3,2,1,0:T(8,128)S(1)}, u32[]{:S(2)}, u32[]{:S(2)}) collective-permute-start(f32[2,48,8,128]{3,2,1,0:T(8,128)S(1)} %get-tuple-element.38), channel_id=1, source_target_pairs={{1,2},{2,1},{3,4},{4,3},{5,6},{6,5},{7,8},{8,7},{9,10},{10,9},{11,... | collective-permute-start | bytes 1179656 | tf_op jit(solution)/shard_map/ppermute | solution.py:581
  4.0 4.3 %collective-permute-start.3 = (f32[2,48,8,128]{3,2,1,0:T(8,128)S(1)}, f32[2,48,8,128]{3,2,1,0:T(8,128)S(1)}, u32[]{:S(2)}, u32[]{:S(2)}) collective-permute-start(f32[2,48,8,128]{3,2,1,0:T(8,128)S(1)} %get-tuple-element.39), channel_id=1, source_target_pairs={{0,1},{1,0},{2,3},{3,2},{4,5},{5,4},{6,7},{7,6},{8,9},{9,8},{10,11... | collective-permute-start | bytes 1179656 | tf_op jit(solution)/shard_map/ppermute | solution.py:581
  8.4 0.9 %shard_map.60 = (f32[2,8,16,128]{3,2,1,0:T(8,128)S(1)}, f32[2,8,16,128]{3,2,1,0:T(8,128)S(1)}, f32[2,44,8,128]{3,2,1,0:T(8,128)}, f32[2,44,8,128]{3,2,1,0:T(8,128)}) custom-call(f32[2,48,16,128]{3,2,1,0:T(8,128)S(1)} %bitcast.15, f32[2,8,16,128]{3,2,1,0:T(8,128)S(1)} %collective-permute-done.far, f32[2,8,16,128]{3,2,1,0:T(8,128)S(1)} %collective-permute-done.1.near), custom_call_target="tpu_custom_call" | custom-call | tf_op jit(solution)/shard_map/pallas_call | solution.py:607
  9.4 1.8 %shard_map.61 = f32[256,128]{1,0:T(8,128)} custom-call(f32[2,48,16,128]{3,2,1,0:T(8,128)S(1)} %bitcast.16, f32[2,8,16,128]{3,2,1,0:T(8,128)S(1)} %get-tuple-element.33.yd, f32[2,8,16,128]{3,2,1,0:T(8,128)S(1)} %get-tuple-element.34.yu, f32[1,128]{1,0:T(1,128)S(1)} %pad_bitcast_fusion.volts), custom_call_target="tpu_custom_call" | custom-call | tf_op jit(solution)/shard_map/pallas_call | solution.py:614
  11.2 0.7 %collective-permute-start.4 = (f32[2,44,8,128]{3,2,1,0:T(8,128)}, f32[2,44,8,128]{3,2,1,0:T(8,128)S(1)}, u32[]{:S(2)}, u32[]{:S(2)}) collective-permute-start(f32[2,44,8,128]{3,2,1,0:T(8,128)} %get-tuple-element.40), channel_id=1, source_target_pairs={{1,2},{2,1},{3,4},{4,3},{5,6},{6,5},{7,8},{8,7},{9,10},{10,9},{11,... | collective-permute-start | bytes 1081352 | tf_op jit(solution)/shard_map/ppermute | solution.py:581
  11.8 2.9 %collective-permute-start.5 = (f32[2,44,8,128]{3,2,1,0:T(8,128)}, f32[2,44,8,128]{3,2,1,0:T(8,128)S(1)}, u32[]{:S(2)}, u32[]{:S(2)}) collective-permute-start(f32[2,44,8,128]{3,2,1,0:T(8,128)} %get-tuple-element.41), channel_id=1, source_target_pairs={{0,1},{1,0},{2,3},{3,2},{4,5},{5,4},{6,7},{7,6},{8,9},{9,8},{10,11... | collective-permute-start | bytes 1081352 | tf_op jit(solution)/shard_map/ppermute | solution.py:581
  14.7 17.2 %all-to-all-start = ((f32[256,1,128]{2,1,0:T(1,128)}), f32[256,1,128]{2,1,0:T(1,128)S(1)}, u32[]{:S(2)}, u32[]{:S(2)}) async-start(f32[256,1,128]{2,1,0:T(1,128)} %bitcast.3), calls=%async_computation | async-start | bytes 262144 | tf_op jit(solution)/shard_map/all_to_all | solution.py:622
  31.9 2.5 %shard_map.63 = (f32[2,16,16,128]{3,2,1,0:T(8,128)}, f32[2,16,16,128]{3,2,1,0:T(8,128)}) custom-call(f32[2,48,16,128]{3,2,1,0:T(8,128)S(1)} %bitcast.17, f32[2,8,16,128]{3,2,1,0:T(8,128)S(1)} %get-tuple-element.33.yd, f32[2,8,16,128]{3,2,1,0:T(8,128)S(1)} %get-tuple-element.34.yu, f32[2,48,8,128]{3,2,1,0:T(8,128)S(1)} %collective-permute-done.2.z_far, ...), custom_call_target="tpu_custom_call" | custom-call | flops 100000000 | bytes 36000000 | tf_op jit(solution)/shard_map/pallas_call | solution.py:626
  34.5 1.3 %collective-permute-start.6 = (f32[2,16,16,128]{3,2,1,0:T(8,128)}, f32[2,16,16,128]{3,2,1,0:T(8,128)S(1)}, u32[]{:S(2)}, u32[]{:S(2)}) collective-permute-start(f32[2,16,16,128]{3,2,1,0:T(8,128)} %get-tuple-element.43), channel_id=1, source_target_pairs={{0,128},{1,129},{2,130},{3,131},{4,132},{5,133},{6,134},{7,135},{8... | collective-permute-start | bytes 786440 | tf_op jit(solution)/shard_map/ppermute | solution.py:641
  35.8 2.3 %shard_map.64 = (f32[2,16,16,128]{3,2,1,0:T(8,128)}, f32[2,16,16,128]{3,2,1,0:T(8,128)}) custom-call(f32[2,48,16,128]{3,2,1,0:T(8,128)S(1)} %bitcast.18, f32[2,8,16,128]{3,2,1,0:T(8,128)S(1)} %get-tuple-element.33.yd, f32[2,8,16,128]{3,2,1,0:T(8,128)S(1)} %get-tuple-element.34.yu, f32[2,48,8,128]{3,2,1,0:T(8,128)S(1)} %collective-permute-done.2.z_far, ...), custom_call_target="tpu_custom_call" | custom-call | flops 100000000 | bytes 9000000 | tf_op jit(solution)/shard_map/pallas_call | solution.py:626
  38.1 1.3 %collective-permute-start.7 = (f32[2,16,16,128]{3,2,1,0:T(8,128)}, f32[2,16,16,128]{3,2,1,0:T(8,128)S(1)}, u32[]{:S(2)}, u32[]{:S(2)}) collective-permute-start(f32[2,16,16,128]{3,2,1,0:T(8,128)} %get-tuple-element.46), channel_id=1, source_target_pairs={{0,128},{1,129},{2,130},{3,131},{4,132},{5,133},{6,134},{7,135},{8... | collective-permute-start | bytes 786440 | tf_op jit(solution)/shard_map/ppermute | solution.py:641
  39.4 2.3 %shard_map.65 = (f32[2,16,16,128]{3,2,1,0:T(8,128)}, f32[2,16,16,128]{3,2,1,0:T(8,128)}) custom-call(f32[2,48,16,128]{3,2,1,0:T(8,128)S(1)} %bitcast.19, f32[2,8,16,128]{3,2,1,0:T(8,128)S(1)} %get-tuple-element.33.yd, f32[2,8,16,128]{3,2,1,0:T(8,128)S(1)} %get-tuple-element.34.yu, f32[2,48,8,128]{3,2,1,0:T(8,128)S(1)} %collective-permute-done.2.z_far, ...), custom_call_target="tpu_custom_call" | custom-call | flops 100000000 | bytes 9000000 | tf_op jit(solution)/shard_map/pallas_call | solution.py:626
  41.7 2.4 %all-to-all-done = f32[256,1,128]{2,1,0:T(1,128)S(1)} async-done(((f32[256,1,128]{2,1,0:T(1,128)}), f32[256,1,128]{2,1,0:T(1,128)S(1)}, u32[]{:S(2)}, u32[]{:S(2)}) %all-to-all-start) | async-done | bytes 131104 | tf_op jit(solution)/shard_map/all_to_all | solution.py:622
  44.2 1.3 %collective-permute-start.8 = (f32[2,16,16,128]{3,2,1,0:T(8,128)}, f32[2,16,16,128]{3,2,1,0:T(8,128)S(1)}, u32[]{:S(2)}, u32[]{:S(2)}) collective-permute-start(f32[2,16,16,128]{3,2,1,0:T(8,128)} %get-tuple-element.52), channel_id=1, source_target_pairs={{0,128},{1,129},{2,130},{3,131},{4,132},{5,133},{6,134},{7,135},{8... | collective-permute-start | bytes 786440 | tf_op jit(solution)/shard_map/ppermute | solution.py:641
  45.5 0.1 copy.12
  45.7 0.1 reshape.12.refs_4_
  45.9 5.8 %shard_map.66 = (f32[2,48,16,128]{3,2,1,0:T(8,128)S(1)}, f32[1,2]{1,0:T(1,128)}) custom-call(f32[2,16,16,128]{3,2,1,0:T(8,128)} %get-tuple-element.42.refs_0_, f32[2,16,16,128]{3,2,1,0:T(8,128)} %get-tuple-element.45.refs_1_, f32[2,16,16,128]{3,2,1,0:T(8,128)} %get-tuple-element.48.refs_2_, f32[256,128]{1,0:T(8,128)S(1)} %bitcast.20, ...), custom_call_target="tpu_custom_call" | custom-call | tf_op jit(solution)/shard_map/pallas_call | solution.py:647
  51.7 5.0 %collective-permute-done.8.refs_2_ = f32[2,16,16,128]{3,2,1,0:T(8,128)S(1)} collective-permute-done((f32[2,16,16,128]{3,2,1,0:T(8,128)}, f32[2,16,16,128]{3,2,1,0:T(8,128)S(1)}, u32[]{:S(2)}, u32[]{:S(2)}) %collective-permute-start.8) | collective-permute-done | bytes 262176 | tf_op jit(solution)/shard_map/ppermute | solution.py:641
  56.8 1.0 %shard_map.67 = f32[1,2,48,16,128]{4,3,2,1,0:T(8,128)} custom-call(f32[2,48,16,128]{3,2,1,0:T(8,128)S(1)} %get-tuple-element.51.main, f32[2,16,16,128]{3,2,1,0:T(8,128)S(1)} %collective-permute-done.6.refs_0_, f32[2,16,16,128]{3,2,1,0:T(8,128)S(1)} %collective-permute-done.7.refs_1_, f32[2,16,16,128]{3,2,1,0:T(8,128)S(1)} %collective-permute-done.8.refs_2_), custom_call_target="tpu_custom_call" | custom-call | tf_op jit(solution)/shard_map/pallas_call | solution.py:654
  (20 shorter events, 0.4 us)
Async XLA Ops:
  0.6 1.1 %copy-start = (f32[1,2,48,16,128]{4,3,2,1,0:T(8,128)S(1)}, f32[1,2,48,16,128]{4,3,2,1,0:T(8,128)}, u32[]{:S(2)}) copy-start(f32[1,2,48,16,128]{4,3,2,1,0:T(8,128)} %param.4) | copy-start | bytes 2359300
  1.8 1.5 %copy-start.1 = (f32[1,2,48,16,128]{4,3,2,1,0:T(8,128)S(1)}, f32[1,2,48,16,128]{4,3,2,1,0:T(8,128)}, u32[]{:S(2)}) copy-start(f32[1,2,48,16,128]{4,3,2,1,0:T(8,128)} %param.4) | copy-start | bytes 2359300
  1.8 1.4 %collective-permute-start.1 = (f32[2,8,16,128]{3,2,1,0:T(8,128)S(1)}, f32[2,8,16,128]{3,2,1,0:T(8,128)S(1)}, u32[]{:S(2)}, u32[]{:S(2)}) collective-permute-start(f32[2,8,16,128]{3,2,1,0:T(8,128)S(1)} %get-tuple-element.29), channel_id=1, source_target_pairs={{0,16},{16,0},{32,48},{48,32},{64,80},{80,64},{96,112},{112,96},{1... | collective-permute-start | bytes 393224 | tf_op jit(solution)/shard_map/ppermute | solution.py:581
  1.9 6.5 %collective-permute-start = (f32[2,8,16,128]{3,2,1,0:T(8,128)S(1)}, f32[2,8,16,128]{3,2,1,0:T(8,128)S(1)}, u32[]{:S(2)}, u32[]{:S(2)}) collective-permute-start(f32[2,8,16,128]{3,2,1,0:T(8,128)S(1)} %get-tuple-element.28), channel_id=1, source_target_pairs={{16,32},{32,16},{48,64},{64,48},{80,96},{96,80},{17,33},{33,17},{4... | collective-permute-start | bytes 393224 | tf_op jit(solution)/shard_map/ppermute | solution.py:581
  3.3 5.0 %copy-start.3 = (f32[2]{0:T(128)S(1)}, f32[2]{0:T(128)}, u32[]{:S(2)}) copy-start(f32[2]{0:T(128)} %param.6) | copy-start | bytes 28
  3.3 28.6 %collective-permute-start.2 = (f32[2,48,8,128]{3,2,1,0:T(8,128)S(1)}, f32[2,48,8,128]{3,2,1,0:T(8,128)S(1)}, u32[]{:S(2)}, u32[]{:S(2)}) collective-permute-start(f32[2,48,8,128]{3,2,1,0:T(8,128)S(1)} %get-tuple-element.38), channel_id=1, source_target_pairs={{1,2},{2,1},{3,4},{4,3},{5,6},{6,5},{7,8},{8,7},{9,10},{10,9},{11,... | collective-permute-start | bytes 1179656 | tf_op jit(solution)/shard_map/ppermute | solution.py:581
  4.0 27.9 %collective-permute-start.3 = (f32[2,48,8,128]{3,2,1,0:T(8,128)S(1)}, f32[2,48,8,128]{3,2,1,0:T(8,128)S(1)}, u32[]{:S(2)}, u32[]{:S(2)}) collective-permute-start(f32[2,48,8,128]{3,2,1,0:T(8,128)S(1)} %get-tuple-element.39), channel_id=1, source_target_pairs={{0,1},{1,0},{2,3},{3,2},{4,5},{5,4},{6,7},{7,6},{8,9},{9,8},{10,11... | collective-permute-start | bytes 1179656 | tf_op jit(solution)/shard_map/ppermute | solution.py:581
  11.2 20.7 %collective-permute-start.4 = (f32[2,44,8,128]{3,2,1,0:T(8,128)}, f32[2,44,8,128]{3,2,1,0:T(8,128)S(1)}, u32[]{:S(2)}, u32[]{:S(2)}) collective-permute-start(f32[2,44,8,128]{3,2,1,0:T(8,128)} %get-tuple-element.40), channel_id=1, source_target_pairs={{1,2},{2,1},{3,4},{4,3},{5,6},{6,5},{7,8},{8,7},{9,10},{10,9},{11,... | collective-permute-start | bytes 1081352 | tf_op jit(solution)/shard_map/ppermute | solution.py:581
  11.8 20.1 %collective-permute-start.5 = (f32[2,44,8,128]{3,2,1,0:T(8,128)}, f32[2,44,8,128]{3,2,1,0:T(8,128)S(1)}, u32[]{:S(2)}, u32[]{:S(2)}) collective-permute-start(f32[2,44,8,128]{3,2,1,0:T(8,128)} %get-tuple-element.41), channel_id=1, source_target_pairs={{0,1},{1,0},{2,3},{3,2},{4,5},{5,4},{6,7},{7,6},{8,9},{9,8},{10,11... | collective-permute-start | bytes 1081352 | tf_op jit(solution)/shard_map/ppermute | solution.py:581
  14.7 29.4 %all-to-all-start = ((f32[256,1,128]{2,1,0:T(1,128)}), f32[256,1,128]{2,1,0:T(1,128)S(1)}, u32[]{:S(2)}, u32[]{:S(2)}) async-start(f32[256,1,128]{2,1,0:T(1,128)} %bitcast.3), calls=%async_computation | async-start | bytes 262144 | tf_op jit(solution)/shard_map/all_to_all | solution.py:622
  34.5 17.2 %collective-permute-start.6 = (f32[2,16,16,128]{3,2,1,0:T(8,128)}, f32[2,16,16,128]{3,2,1,0:T(8,128)S(1)}, u32[]{:S(2)}, u32[]{:S(2)}) collective-permute-start(f32[2,16,16,128]{3,2,1,0:T(8,128)} %get-tuple-element.43), channel_id=1, source_target_pairs={{0,128},{1,129},{2,130},{3,131},{4,132},{5,133},{6,134},{7,135},{8... | collective-permute-start | bytes 786440 | tf_op jit(solution)/shard_map/ppermute | solution.py:641
  38.1 13.6 %collective-permute-start.7 = (f32[2,16,16,128]{3,2,1,0:T(8,128)}, f32[2,16,16,128]{3,2,1,0:T(8,128)S(1)}, u32[]{:S(2)}, u32[]{:S(2)}) collective-permute-start(f32[2,16,16,128]{3,2,1,0:T(8,128)} %get-tuple-element.46), channel_id=1, source_target_pairs={{0,128},{1,129},{2,130},{3,131},{4,132},{5,133},{6,134},{7,135},{8... | collective-permute-start | bytes 786440 | tf_op jit(solution)/shard_map/ppermute | solution.py:641
  41.7 3.8 %copy-start.2 = (s32[2,48,16,1]{1,3,2,0:T(1,128)S(1)}, s32[2,48,16,1]{1,3,2,0:T(1,128)}, u32[]{:S(2)}) copy-start(s32[2,48,16,1]{1,3,2,0:T(1,128)} %param.5) | copy-start | bytes 18436
  44.2 12.6 %collective-permute-start.8 = (f32[2,16,16,128]{3,2,1,0:T(8,128)}, f32[2,16,16,128]{3,2,1,0:T(8,128)S(1)}, u32[]{:S(2)}, u32[]{:S(2)}) collective-permute-start(f32[2,16,16,128]{3,2,1,0:T(8,128)} %get-tuple-element.52), channel_id=1, source_target_pairs={{0,128},{1,129},{2,130},{3,131},{4,132},{5,133},{6,134},{7,135},{8... | collective-permute-start | bytes 786440 | tf_op jit(solution)/shard_map/ppermute | solution.py:641

commit v7 on v6

--- a/solution.py
+++ b/solution.py
@@ -10,7 +10,7 @@
 
 AXES = ("grp", "gy", "gz")
 TY = 6
-VOLT = TY * 16
+VOLT = (TY + 1) * 16
 ROWS, COLS, LANES = 48, 16, 128
 HY, HZ = 8, 12
 EXT = ROWS + 2 * HY
@@ -38,14 +38,20 @@
         body(first + i * n, n)
 
 
-def zshift(v, closed):
+def zshift(v, ends):
     z = v.shape[1]
     zp, zm = pltpu.roll(v, z - 1, 1), pltpu.roll(v, 1, 1)
-    if closed:
+    if ends is None:
         layer = lax.broadcasted_iota(jnp.int32, v.shape, 1)
-        zp = jnp.where(layer == z - 1, 0.0, zp)
-        zm = jnp.where(layer == 0, 0.0, zm)
-    return zp, zm
+        return jnp.where(layer == z - 1, 0.0, zp), jnp.where(layer == 0, 0.0, zm)
+
+    def cut(shifted, at, when):
+        g = at // 8 * 8
+        hit = (lax.broadcasted_iota(jnp.int32, (1, 8, LANES), 1) == at - g) & when
+        tile = jnp.where(jnp.broadcast_to(hit, (v.shape[0], 8, LANES)), 0.0, shifted[:, g:g + 8])
+        return jnp.concatenate([part for part in (shifted[:, :g], tile, shifted[:, g + 8:]) if part.shape[1]], axis=1)
+    at, below, above = ends
+    return cut(zp, at + COLS - 1, above), cut(zm, at, below)
 
 
 def beside(c, share):
@@ -68,27 +74,17 @@
     return jnp.concatenate([total.reshape(k, z, LANES), rolled], axis=0)
 
 
-def around(w, closed):
+def around(w, ends):
     c = w[1:-1]
-    zp, zm = zshift(c, closed)
+    zp, zm = zshift(c, ends)
     s = (w[:-2] + w[2:]) + (zp + zm)
-    return c, s + beside(c, 0.0 if closed else SHARE), zp - zm
-
-
-def zero_edges(edge, ref, at):
-    ylo, yhi, zlo, zhi = edge
-    rows, layers, _ = ref.shape
-
-    def clear(when, index):
+    return c, s + beside(c, 0.0 if ends is None else SHARE), zp - zm
+
+
+def zero_edges(edge, ref):
+    for when, r in ((edge[0], HY - 1), (edge[1], ref.shape[0] - HY)):
         if when is not None:
-            @pl.when(when)
-            def _():
-                part = ref.at[index]
-                part[...] = jnp.zeros(part.shape, jnp.float32)
-    clear(ylo, pl.ds(HY - 1, 1))
-    clear(yhi, pl.ds(rows - HY, 1))
-    clear(zlo, (slice(None), pl.ds(at - 1, 1)))
-    clear(zhi, (slice(None), pl.ds(at + COLS, 1)))
+            ref[r] = jnp.where(when, 0.0, ref[r])
 
 
 def early_scratch(rows, window):
@@ -107,76 +103,86 @@
     return early_scratch(rows, window) + mid_scratch(rows, window) + late_scratch(rows, window)
 
 
-def forward(edge, ghost, window, pieces, early, mid):
+def forward(edge, ghost, window, pieces, early, mid, spread=False):
     U, V, SRC, B, Q, U1 = early
     SRC2, B2, Q2, P2, A = mid[:5]
     top = U1.shape[0] - 1
     closed = window[0][0] == 0
+    ends = [None if closed else (part[0],) + edge[2:] for part in window]
+
+    def span(k):
+        return (1, top - 1) if spread else (k, top - k)
+
     m = piece(window[0], window[1])
-    first, second = window[0][0], window[1][0]
-
-    def finish(ref, at):
+
+    def finish(ref):
         if ghost is not None:
             ref[...] += ghost[...]
-        zero_edges(edge, ref, at)
+        zero_edges(edge, ref)
 
     def stage_a(r, n):
-        c, s, d = around(U[pl.ds(r - 1, n + 2)], closed)
+        c, s, d = around(U[pl.ds(r - 1, n + 2)], ends[0])
         src = (0.5 / 6.0) * d
         SRC[pl.ds(r, n)] = src
         B[pl.ds(r, n)] = 0.35 * c + 0.1 * s
-        _, s, _ = around(V[pl.ds(r - 1, n + 2)], closed)
+        _, s, _ = around(V[pl.ds(r - 1, n + 2)], ends[0])
         Q[pl.ds(r, n)] = s * SIXTH - src
     if ghost is not None:
         Q[...] = ghost[...]
-        zero_edges(edge, Q, first)
+        zero_edges(edge, Q)
     else:
-        rows_loop(1, top - 1, stage_a, pieces)
-        finish(Q, first)
+        rows_loop(*span(1), stage_a, pieces)
+        finish(Q)
 
     def stage_b(r, n):
-        _, s, _ = around(Q[pl.ds(r - 1, n + 2)], closed)
+        _, s, _ = around(Q[pl.ds(r - 1, n + 2)], ends[0])
         s = s * SIXTH
         V[pl.ds(r, n)] = s if ghost is not None else s - SRC[pl.ds(r, n)]
-    rows_loop(2, top - 2, stage_b, pieces)
-    finish(V, first)
+    rows_loop(*span(2), stage_b, pieces)
+    finish(V)
 
     def stage_c(r, n):
-        zp, zm = zshift(V[pl.ds(r, n)], closed)
+        zp, zm = zshift(V[pl.ds(r, n)], ends[0])
         u = 0.5 * (zp - zm)
         U1[pl.ds(r, n)] = u if ghost is not None else u + B[pl.ds(r, n)]
-    rows_loop(3, top - 3, stage_c, pieces)
-    zero_edges(edge, U1, first)
+    rows_loop(*span(3), stage_c, pieces)
+    zero_edges(edge, U1)
 
     def stage_d(r, n):
-        c, s, d = around(U1[pl.ds(r - 1, n + 2)], closed)
+        c, s, d = around(U1[pl.ds(r - 1, n + 2)], ends[0])
         src = (0.5 / 6.0) * d[:, m]
         SRC2[pl.ds(r, n)] = src
         B2[pl.ds(r, n)] = 0.35 * c[:, m] + 0.1 * s[:, m]
-        _, s, _ = around(V[pl.ds(r - 1, n + 2)], closed)
+        _, s, _ = around(V[pl.ds(r - 1, n + 2)], ends[0])
         Q2[pl.ds(r, n)] = s[:, m] * SIXTH - src
-    rows_loop(3, top - 3, stage_d, pieces)
-    finish(Q2, second)
+    rows_loop(*span(3), stage_d, pieces)
+    finish(Q2)
 
     def stage_e(r, n):
-        _, s, _ = around(Q2[pl.ds(r - 1, n + 2)], closed)
+        _, s, _ = around(Q2[pl.ds(r - 1, n + 2)], ends[1])
         P2[pl.ds(r, n)] = s * SIXTH - SRC2[pl.ds(r, n)]
-    rows_loop(4, top - 4, stage_e, pieces)
-    finish(P2, second)
+    rows_loop(*span(4), stage_e, pieces)
+    if ghost is not None:
+        P2[...] += ghost[...]
 
     def stage_f(r, n):
-        zp, zm = zshift(P2[pl.ds(r, n)], closed)
+        zp, zm = zshift(P2[pl.ds(r, n)], ends[1])
         A[pl.ds(r, n)] = B2[pl.ds(r, n)] + 0.5 * (zp - zm)
-    rows_loop(4, top - 4, stage_f, pieces)
-    zero_edges(edge, A, second)
-
-
-def adjoint(edge, window, pieces, a2, pot, u1, mid, late, give):
+    rows_loop(*span(4), stage_f, pieces)
+    zero_edges(edge, A)
+
+
+def adjoint(edge, window, pieces, a2, pot, u1, mid, late, give, spread=False):
     BM, SP = mid[5:7]
     S2, T, B, A1, S3, SP2, S4, T2 = late
     top = SP.shape[0] - 1
     closed = window[0][0] == 0
-    second, third = window[1][0], window[2][0]
+    ends = [None if closed else (part[0],) + edge[2:] for part in window]
+
+    def span(k):
+        return (1, top - 1) if spread else (k, top - k)
+
+    third = window[2][0]
     m = piece(window[1], window[2])
 
     def take(source, inner, r, n):
@@ -184,64 +190,62 @@
         return ref[pl.ds(r, n), piece(place, inner), :]
 
     def stage_g(r, n):
-        c, s, d = around(take(a2, window[1], r - 1, n + 2), closed)
+        c, s, d = around(take(a2, window[1], r - 1, n + 2), ends[1])
         BM[pl.ds(r, n)] = 0.35 * c + 0.1 * s
         sp = -0.5 * d
         if pot is not None:
             sp = sp + take(pot, window[1], r, n)
         SP[pl.ds(r, n)] = sp
-    rows_loop(4, top - 4, stage_g, pieces)
-    zero_edges(edge, SP, second)
+    rows_loop(*span(4), stage_g, pieces)
+    zero_edges(edge, SP)
 
     def stage_h(r, n):
-        c, s, _ = around(SP[pl.ds(r - 1, n + 2)], closed)
+        c, s, _ = around(SP[pl.ds(r - 1, n + 2)], ends[1])
         c, s = c[:, m], s[:, m] * SIXTH
         S2[pl.ds(r, n)] = s
         T[pl.ds(r, n)] = (c + s) * SIXTH
-    rows_loop(5, top - 5, stage_h, pieces)
-    zero_edges(edge, S2, third)
-    zero_edges(edge, T, third)
+    rows_loop(*span(5), stage_h, pieces)
+    zero_edges(edge, S2)
 
     def stage_i(r, n):
-        _, s, _ = around(S2[pl.ds(r - 1, n + 2)], closed)
+        _, s, _ = around(S2[pl.ds(r - 1, n + 2)], ends[2])
         S3[pl.ds(r, n)] = s * SIXTH
-        zp, zm = zshift(T[pl.ds(r, n)], closed)
+        zp, zm = zshift(T[pl.ds(r, n)], ends[2])
         a = BM[pl.ds(r, n), m, :] + 0.5 * (zp - zm)
         if u1 is not None:
             a = a + take(u1, window[2], r, n)
         A1[pl.ds(r, n)] = a
-    rows_loop(6, top - 6, stage_i, pieces)
-    zero_edges(edge, A1, third)
+    rows_loop(*span(6), stage_i, pieces)
+    zero_edges(edge, A1)
 
     def stage_j(r, n):
         if give is None:
-            zp, zm = zshift(A1[pl.ds(r, n)], closed)
+            zp, zm = zshift(A1[pl.ds(r, n)], ends[2])
             d = zp - zm
         else:
-            c, s, d = around(A1[pl.ds(r - 1, n + 2)], closed)
+            c, s, d = around(A1[pl.ds(r - 1, n + 2)], ends[2])
             B[pl.ds(r, n)] = 0.35 * c + 0.1 * s
         SP2[pl.ds(r, n)] = S3[pl.ds(r, n)] - 0.5 * d
-    rows_loop(6, top - 6, stage_j, pieces)
-    zero_edges(edge, SP2, third)
+    rows_loop(*span(6), stage_j, pieces)
+    zero_edges(edge, SP2)
 
     def stage_k(r, n):
-        c, s, _ = around(SP2[pl.ds(r - 1, n + 2)], closed)
+        c, s, _ = around(SP2[pl.ds(r - 1, n + 2)], ends[2])
         s = s * SIXTH
         S4[pl.ds(r, n)] = s
         T2[pl.ds(r, n)] = (c + s) * SIXTH
-    rows_loop(7, top - 7, stage_k, pieces)
-    zero_edges(edge, S4, third)
-    zero_edges(edge, T2, third)
+    rows_loop(*span(7), stage_k, pieces)
+    zero_edges(edge, S4)
     if give is None:
         return
     own = slice(third, third + COLS)
 
     def stage_l(r, n):
-        _, s, _ = around(S4[pl.ds(r - 1, n + 2)], closed)
-        zp, zm = zshift(T2[pl.ds(r, n)], closed)
+        _, s, _ = around(S4[pl.ds(r - 1, n + 2)], ends[2])
+        zp, zm = zshift(T2[pl.ds(r, n)], ends[2])
         u = B[pl.ds(r, n)] + 0.5 * (zp - zm)
         give(r - HY, n, u[:, own], s[:, own] * SIXTH)
-    rows_loop(8, top - 8, stage_l, 2)
+    rows_loop(*span(8), stage_l, 2)
 
 
 def load_extended(dst, f, part, own, yd, yu, below, above):
@@ -345,14 +349,13 @@
         ghost[8 * ty:8 * ty + 8] = jnp.broadcast_to(tile[None], (8, COLS, LANES))
 
 
-def wall_tiles(layer, T, T2, held):
-    at = slice(HY, HY + ROWS)
-    w = T[at, layer, :] + T2[at, layer, :]
-    held[...] = jnp.zeros((8, LANES), jnp.float32)
-    held[0:TY] = jnp.sum(w.reshape(TY, 8, LANES), axis=1)
+def wall_tiles(layer, T, T2):
+    w = jnp.sum((T[:, layer, :] + T2[:, layer, :]).reshape(8, 8, LANES), axis=1)
     gather = ((iota((LANES, LANES), 0) >> 3) == (iota((LANES, LANES), 1) & 15)).astype(jnp.float32)
-    sums = jnp.dot(held[...], gather, precision=HIGHEST, preferred_element_type=jnp.float32)
-    keep = (iota((8, LANES), 1) >> 4) == iota((8, LANES), 0)
+    sums = jnp.dot(w, gather, precision=HIGHEST, preferred_element_type=jnp.float32)
+    first = lax.rem(lax.axis_index("gy"), 2)
+    lane = iota((8, LANES), 1)
+    keep = ((lane >> 4) + first == iota((8, LANES), 0)) & (lane < VOLT)
     return jnp.sum(jnp.where(keep, sums, 0.0), axis=0, keepdims=True)
 
 
@@ -360,9 +363,9 @@
     return refs[:6], refs[6:13], refs[13:21]
 
 
-def wall_kernel(own, yd, yu, volts, row, *refs):
+def wall_kernel(own, near, volts, row, *refs):
     early, mid, late = split(refs)
-    held, sums = refs[21:]
+    sums = refs[21]
     ylo, yhi, zlo, zhi = edges()
     edge = (ylo, yhi, None, None)
     is_forward = lax.axis_index("grp") == 0
@@ -370,22 +373,25 @@
 
     @pl.when(jnp.logical_or(zlo, zhi))
     def _():
+        for ref in early + mid + late:
+            for r in (0, EXT - 1):
+                ref[r] = jnp.zeros(ref.shape[1:], jnp.float32)
         for f in range(2):
-            early[f][0:HY] = yd[f]
+            early[f][0:HY] = jnp.where(is_even("gy"), 0.0, near[f])
             early[f][HY:HY + ROWS] = own[f]
-            early[f][HY + ROWS:] = yu[f]
+            early[f][HY + ROWS:] = jnp.where(is_even("gy"), near[f], 0.0)
 
     def side(window, layer):
         @pl.when(is_forward)
         def _():
-            forward(edge, None, window, 1, early, mid)
-            adjoint(edge, window, 1, (mid[4], window[1]), None, (early[5], window[0]), mid, late, None)
+            forward(edge, None, window, 1, early, mid, True)
+            adjoint(edge, window, 1, (mid[4], window[1]), None, (early[5], window[0]), mid, late, None, True)
 
         @pl.when(jnp.logical_not(is_forward))
         def _():
-            adjoint(edge, window, 1, (early[0], window[0]), (early[1], window[0]), None, mid, late, None)
-
-        sums[...] = wall_tiles(layer, late[1], late[7], held)
+            adjoint(edge, window, 1, (early[0], window[0]), (early[1], window[0]), None, mid, late, None, True)
+
+        sums[...] = wall_tiles(layer, late[1], late[7])
 
     @pl.when(zlo)
     def _():
@@ -490,7 +496,7 @@
     gy, gz = lax.axis_size("gy"), lax.axis_size("gz")
     me = (lax.axis_index("grp") * gy + lax.axis_index("gy")) * gz + lax.axis_index("gz")
     pair = [jnp.zeros((gy, LANES), jnp.float32)] * 2
-    block = iota((gy, LANES), 0)
+    block, lane = iota((gy, LANES), 0), iota((gy, LANES), 1)
     for s in range(2):
         v = jnp.concatenate([tile_volts(first, second, labels[s, g:g + 1]) for g in range(gy)], axis=0)
         r = jnp.dot(v, response[...], precision=HIGHEST, preferred_element_type=jnp.float32)
@@ -498,8 +504,13 @@
         w = jnp.where(block == 0, r[3], jnp.where(block == gy - 1, r[4], r[0]))
         w = w + jnp.where(block == 0, 0.0, pltpu.roll(r[1], 1, 0))
         w = w + jnp.where(block == gy - 1, 0.0, pltpu.roll(r[2], gy - 1, 0))
-        for g in range(2):
-            w = w + rows[pl.ds(g * gy * gz + s * (gz - 1), gy, stride=gz), :]
+        got = sum(rows[pl.ds(g * gy * gz + s * (gz - 1), gy, stride=gz), :] for g in range(2))
+        odd = (block & 1) == 1
+        w = w + jnp.where(odd, got, pltpu.roll(got, LANES - 16, 1))
+        below = pltpu.roll(pltpu.roll(got, 32, 1), 1, 0)
+        above = pltpu.roll(pltpu.roll(got, 80, 1), gy - 1, 0)
+        w = w + jnp.where((block > 0) & jnp.logical_not(odd) & (lane < 16), below, 0.0)
+        w = w + jnp.where((block < gy - 1) & odd & (lane >= 80), above, 0.0)
         for j in range(2):
             pair[j] = pair[j] + jnp.where(labels[s] == 2 * me + j, w, 0.0)
     total = [jnp.sum(p) for p in pair]
@@ -599,6 +610,11 @@
     far = swapped(far, "gy", 1)
     near = swapped(near, "gy", 0)
     mine, near = lax.optimization_barrier((own, near))
+    row = pl.pallas_call(
+        wall_kernel, out_shape=kept(devices, LANES), in_specs=vmem(3), out_specs=vmem(1)[0],
+        scratch_shapes=scratch(EXT, LOWER) + [pltpu.VMEM((1, LANES), jnp.float32)], compiler_params=limit(12),
+    )(mine, near, jnp.pad(electrode_volts, (VOLT, LANES - VOLT - 2))[None])
+    mine, row = lax.optimization_barrier((mine, row))
     z_near, z_far = pl.pallas_call(
         tiles_kernel, out_shape=(tiles, tiles), in_specs=vmem(1), out_specs=vmem(2), compiler_params=limit(8),
     )(mine)
@@ -610,12 +626,6 @@
         scratch_shapes=[pltpu.VMEM((2, 2 * HY + HALF, 8, LANES), jnp.float32)] * 2 + [pltpu.SemaphoreType.DMA((2,))],
         compiler_params=limit(8),
     )(own, far, near)
-    volts = jnp.pad(electrode_volts, (VOLT, LANES - VOLT - 2))[None]
-    row = pl.pallas_call(
-        wall_kernel, out_shape=kept(devices, LANES), in_specs=vmem(4), out_specs=vmem(1)[0],
-        scratch_shapes=scratch(EXT, LOWER) + [pltpu.VMEM((8, LANES), jnp.float32), pltpu.VMEM((1, LANES), jnp.float32)],
-        compiler_params=limit(12),
-    )(own, yd, yu, volts)
     far, near, row = lax.optimization_barrier((far, near, row))
     far = swapped(far, "gz", 1)
     near = swapped(near, "gz", 0)

time: 58.3 us -> 56.4 us (0.967)
  Pallas kernels: 16.8 us -> 15.2 us
    pallas_call x1, Pallas kernels: 5.83 us -> 5.06 us  [per_device(): pl.pallas_call(volts_kernel, out_shape=(kept(2, ROWS, COLS, LANES), shape...]
    pallas_call x3, Pallas kernels: 7.13 us -> 6.4 us  [bulk(): pl.pallas_call(functools.partial(bulk_kernel, part), out_shape=(half, hal...]
    all_to_all x1, waiting for transfers between devices: 2.45 us -> 3.18 us  [per_device(): rows = lax.all_to_all(row, AXES, 0, 0, tiled=True)]
    all_to_all x1, starting transfers between devices: 17.2 us -> 16.5 us  [per_device(): rows = lax.all_to_all(row, AXES, 0, 0, tiled=True)]
  transfers between devices with their start and end apart: 10 -> 10, of which waited for: 3 -> 3; matrix products, arithmetic and copies ran while one was open for 1% -> 1% of each run, Pallas kernels for 27% -> 25%
where the time goes in v7:
time: 56.4 us; the launch traced here: 56.1 us
  starting transfers between devices  29.9 us (53%)
  Pallas kernels  15.2 us (27%)
  waiting for transfers between devices  8.52 us (15%)
  local copies, waits for them, and re-layouts  1.61 us (3%)
  between operations  0.85 us (2%)
    all_to_all x1, starting transfers between devices, per_device(): rows = lax.all_to_all(row, AXES, 0, 0, tiled=True)  16.5 us
    ppermute x6, starting transfers between devices, swapped(): return lax.ppermute(array, axis, pairs)  9.57 us
    pallas_call x3, Pallas kernels, bulk(): pl.pallas_call(functools.partial(bulk_kernel, part), out_shape=(half, hal...  6.4 us
    pallas_call x1, Pallas kernels, per_device(): pl.pallas_call(volts_kernel, out_shape=(kept(2, ROWS, COLS, LANES), shape...  5.06 us
    ppermute x3, waiting for transfers between devices, per_device(): extras.append(lax.ppermute(send, 'grp', [(0, 1)]))  4.89 us
    ppermute x3, starting transfers between devices, per_device(): extras.append(lax.ppermute(send, 'grp', [(0, 1)]))  3.86 us
    all_to_all x1, waiting for transfers between devices, per_device(): rows = lax.all_to_all(row, AXES, 0, 0, tiled=True)  3.18 us
    pallas_call x1, Pallas kernels, per_device(): pl.pallas_call(wall_kernel, out_shape=kept(devices, LANES), in_specs=vmem...  1.65 us
  transfers between devices with their start and end apart: 10, of which 3 were waited for; matrix products, arithmetic and copies ran while one was open for 1% of the time, Pallas kernels for 25%

profile of v7, /device:TPU:32, one launch (start us, length us, event | category | flops | bytes accessed | tf_op | source)
XLA Modules:
  0.0 56.1 jit_solution(15817687107905684462)
XLA Ops:
  0.6 1.1 %copy-done = f32[1,2,48,16,128]{4,3,2,1,0:T(8,128)S(1)} copy-done((f32[1,2,48,16,128]{4,3,2,1,0:T(8,128)S(1)}, f32[1,2,48,16,128]{4,3,2,1,0:T(8,128)}, u32[]{:S(2)}) %copy-start) | copy-done | bytes 786456
  1.8 0.1 collective-permute-start.1
  1.9 0.8 %collective-permute-start = (f32[2,8,16,128]{3,2,1,0:T(8,128)S(1)}, f32[2,8,16,128]{3,2,1,0:T(8,128)S(1)}, u32[]{:S(2)}, u32[]{:S(2)}) collective-permute-start(f32[2,8,16,128]{3,2,1,0:T(8,128)S(1)} %get-tuple-element.30), channel_id=1, source_target_pairs={{16,32},{32,16},{48,64},{64,48},{80,96},{96,80},{17,33},{33,17},{4... | collective-permute-start | bytes 393224 | tf_op jit(solution)/shard_map/ppermute | solution.py:592
  2.8 0.4 collective-permute-done.1.near
  3.3 1.6 %shard_map.61 = f32[256,128]{1,0:T(8,128)} custom-call(f32[2,48,16,128]{3,2,1,0:T(8,128)S(1)} %bitcast.14, f32[2,8,16,128]{3,2,1,0:T(8,128)S(1)} %collective-permute-done.1.near, f32[1,128]{1,0:T(1,128)S(1)} %pad_bitcast_fusion.volts), custom_call_target="tpu_custom_call" | custom-call | tf_op jit(solution)/shard_map/pallas_call | solution.py:613
  4.9 0.1 shard_map.62
  5.0 0.7 %collective-permute-start.2 = (f32[2,48,8,128]{3,2,1,0:T(8,128)S(1)}, f32[2,48,8,128]{3,2,1,0:T(8,128)S(1)}, u32[]{:S(2)}, u32[]{:S(2)}) collective-permute-start(f32[2,48,8,128]{3,2,1,0:T(8,128)S(1)} %get-tuple-element.42), channel_id=1, source_target_pairs={{1,2},{2,1},{3,4},{4,3},{5,6},{6,5},{7,8},{8,7},{9,10},{10,9},{11,... | collective-permute-start | bytes 1179656 | tf_op jit(solution)/shard_map/ppermute | solution.py:592
  5.7 3.3 %collective-permute-start.3 = (f32[2,48,8,128]{3,2,1,0:T(8,128)S(1)}, f32[2,48,8,128]{3,2,1,0:T(8,128)S(1)}, u32[]{:S(2)}, u32[]{:S(2)}) collective-permute-start(f32[2,48,8,128]{3,2,1,0:T(8,128)S(1)} %get-tuple-element.43), channel_id=1, source_target_pairs={{0,1},{1,0},{2,3},{3,2},{4,5},{5,4},{6,7},{7,6},{8,9},{9,8},{10,11... | collective-permute-start | bytes 1179656 | tf_op jit(solution)/shard_map/ppermute | solution.py:592
  9.0 0.9 %shard_map.60 = (f32[2,8,16,128]{3,2,1,0:T(8,128)S(1)}, f32[2,8,16,128]{3,2,1,0:T(8,128)S(1)}, f32[2,44,8,128]{3,2,1,0:T(8,128)}, f32[2,44,8,128]{3,2,1,0:T(8,128)}) custom-call(f32[2,48,16,128]{3,2,1,0:T(8,128)S(1)} %bitcast.16, f32[2,8,16,128]{3,2,1,0:T(8,128)S(1)} %collective-permute-done.far, f32[2,8,16,128]{3,2,1,0:T(8,128)S(1)} %collective-permute-done.1.near), custom_call_target="tpu_custom_call" | custom-call | tf_op jit(solution)/shard_map/pallas_call | solution.py:623
  9.9 0.7 %collective-permute-start.4 = (f32[2,44,8,128]{3,2,1,0:T(8,128)}, f32[2,44,8,128]{3,2,1,0:T(8,128)S(1)}, u32[]{:S(2)}, u32[]{:S(2)}) collective-permute-start(f32[2,44,8,128]{3,2,1,0:T(8,128)} %get-tuple-element.44), channel_id=1, source_target_pairs={{1,2},{2,1},{3,4},{4,3},{5,6},{6,5},{7,8},{8,7},{9,10},{10,9},{11,... | collective-permute-start | bytes 1081352 | tf_op jit(solution)/shard_map/ppermute | solution.py:592
  10.6 4.0 %collective-permute-start.5 = (f32[2,44,8,128]{3,2,1,0:T(8,128)}, f32[2,44,8,128]{3,2,1,0:T(8,128)S(1)}, u32[]{:S(2)}, u32[]{:S(2)}) collective-permute-start(f32[2,44,8,128]{3,2,1,0:T(8,128)} %get-tuple-element.45), channel_id=1, source_target_pairs={{0,1},{1,0},{2,3},{3,2},{4,5},{5,4},{6,7},{7,6},{8,9},{9,8},{10,11... | collective-permute-start | bytes 1081352 | tf_op jit(solution)/shard_map/ppermute | solution.py:592
  14.6 16.5 %all-to-all-start = ((f32[256,1,128]{2,1,0:T(1,128)}), f32[256,1,128]{2,1,0:T(1,128)S(1)}, u32[]{:S(2)}, u32[]{:S(2)}) async-start(f32[256,1,128]{2,1,0:T(1,128)} %bitcast.3), calls=%async_computation | async-start | bytes 262144 | tf_op jit(solution)/shard_map/all_to_all | solution.py:632
  31.2 2.2 %shard_map.63 = (f32[2,16,16,128]{3,2,1,0:T(8,128)}, f32[2,16,16,128]{3,2,1,0:T(8,128)}) custom-call(f32[2,48,16,128]{3,2,1,0:T(8,128)S(1)} %bitcast.17, f32[2,8,16,128]{3,2,1,0:T(8,128)S(1)} %get-tuple-element.39.yd, f32[2,8,16,128]{3,2,1,0:T(8,128)S(1)} %get-tuple-element.40.yu, f32[2,48,8,128]{3,2,1,0:T(8,128)S(1)} %collective-permute-done.2.z_far, ...), custom_call_target="tpu_custom_call" | custom-call | flops 100000000 | bytes 36000000 | tf_op jit(solution)/shard_map/pallas_call | solution.py:636
  33.4 1.3 %collective-permute-start.6 = (f32[2,16,16,128]{3,2,1,0:T(8,128)}, f32[2,16,16,128]{3,2,1,0:T(8,128)S(1)}, u32[]{:S(2)}, u32[]{:S(2)}) collective-permute-start(f32[2,16,16,128]{3,2,1,0:T(8,128)} %get-tuple-element.47), channel_id=1, source_target_pairs={{0,128},{1,129},{2,130},{3,131},{4,132},{5,133},{6,134},{7,135},{8... | collective-permute-start | bytes 786440 | tf_op jit(solution)/shard_map/ppermute | solution.py:651
  34.7 2.0 %shard_map.64 = (f32[2,16,16,128]{3,2,1,0:T(8,128)}, f32[2,16,16,128]{3,2,1,0:T(8,128)}) custom-call(f32[2,48,16,128]{3,2,1,0:T(8,128)S(1)} %bitcast.18, f32[2,8,16,128]{3,2,1,0:T(8,128)S(1)} %get-tuple-element.39.yd, f32[2,8,16,128]{3,2,1,0:T(8,128)S(1)} %get-tuple-element.40.yu, f32[2,48,8,128]{3,2,1,0:T(8,128)S(1)} %collective-permute-done.2.z_far, ...), custom_call_target="tpu_custom_call" | custom-call | flops 100000000 | bytes 9000000 | tf_op jit(solution)/shard_map/pallas_call | solution.py:636
  36.7 1.3 %collective-permute-start.7 = (f32[2,16,16,128]{3,2,1,0:T(8,128)}, f32[2,16,16,128]{3,2,1,0:T(8,128)S(1)}, u32[]{:S(2)}, u32[]{:S(2)}) collective-permute-start(f32[2,16,16,128]{3,2,1,0:T(8,128)} %get-tuple-element.50), channel_id=1, source_target_pairs={{0,128},{1,129},{2,130},{3,131},{4,132},{5,133},{6,134},{7,135},{8... | collective-permute-start | bytes 786440 | tf_op jit(solution)/shard_map/ppermute | solution.py:651
  38.0 2.2 %shard_map.65 = (f32[2,16,16,128]{3,2,1,0:T(8,128)}, f32[2,16,16,128]{3,2,1,0:T(8,128)}) custom-call(f32[2,48,16,128]{3,2,1,0:T(8,128)S(1)} %bitcast.19, f32[2,8,16,128]{3,2,1,0:T(8,128)S(1)} %get-tuple-element.39.yd, f32[2,8,16,128]{3,2,1,0:T(8,128)S(1)} %get-tuple-element.40.yu, f32[2,48,8,128]{3,2,1,0:T(8,128)S(1)} %collective-permute-done.2.z_far, ...), custom_call_target="tpu_custom_call" | custom-call | flops 100000000 | bytes 9000000 | tf_op jit(solution)/shard_map/pallas_call | solution.py:636
  40.2 3.2 %all-to-all-done = f32[256,1,128]{2,1,0:T(1,128)S(1)} async-done(((f32[256,1,128]{2,1,0:T(1,128)}), f32[256,1,128]{2,1,0:T(1,128)S(1)}, u32[]{:S(2)}, u32[]{:S(2)}) %all-to-all-start) | async-done | bytes 131104 | tf_op jit(solution)/shard_map/all_to_all | solution.py:632
  43.4 1.3 %collective-permute-start.8 = (f32[2,16,16,128]{3,2,1,0:T(8,128)}, f32[2,16,16,128]{3,2,1,0:T(8,128)S(1)}, u32[]{:S(2)}, u32[]{:S(2)}) collective-permute-start(f32[2,16,16,128]{3,2,1,0:T(8,128)} %get-tuple-element.56), channel_id=1, source_target_pairs={{0,128},{1,129},{2,130},{3,131},{4,132},{5,133},{6,134},{7,135},{8... | collective-permute-start | bytes 786440 | tf_op jit(solution)/shard_map/ppermute | solution.py:651
  44.7 0.1 copy.12
  44.9 0.1 reshape.12.refs_4_
  45.1 5.1 %shard_map.66 = (f32[2,48,16,128]{3,2,1,0:T(8,128)S(1)}, f32[1,2]{1,0:T(1,128)}) custom-call(f32[2,16,16,128]{3,2,1,0:T(8,128)} %get-tuple-element.46.refs_0_, f32[2,16,16,128]{3,2,1,0:T(8,128)} %get-tuple-element.49.refs_1_, f32[2,16,16,128]{3,2,1,0:T(8,128)} %get-tuple-element.52.refs_2_, f32[256,128]{1,0:T(8,128)S(1)} %bitcast.20, ...), custom_call_target="tpu_custom_call" | custom-call | tf_op jit(solution)/shard_map/pallas_call | solution.py:657
  50.2 4.9 %collective-permute-done.8.refs_2_ = f32[2,16,16,128]{3,2,1,0:T(8,128)S(1)} collective-permute-done((f32[2,16,16,128]{3,2,1,0:T(8,128)}, f32[2,16,16,128]{3,2,1,0:T(8,128)S(1)}, u32[]{:S(2)}, u32[]{:S(2)}) %collective-permute-start.8) | collective-permute-done | bytes 262176 | tf_op jit(solution)/shard_map/ppermute | solution.py:651
  55.1 1.0 %shard_map.67 = f32[1,2,48,16,128]{4,3,2,1,0:T(8,128)} custom-call(f32[2,48,16,128]{3,2,1,0:T(8,128)S(1)} %get-tuple-element.55.main, f32[2,16,16,128]{3,2,1,0:T(8,128)S(1)} %collective-permute-done.6.refs_0_, f32[2,16,16,128]{3,2,1,0:T(8,128)S(1)} %collective-permute-done.7.refs_1_, f32[2,16,16,128]{3,2,1,0:T(8,128)S(1)} %collective-permute-done.8.refs_2_), custom_call_target="tpu_custom_call" | custom-call | tf_op jit(solution)/shard_map/pallas_call | solution.py:664
  (20 shorter events, 0.4 us)
Async XLA Ops:
  0.6 1.1 %copy-start = (f32[1,2,48,16,128]{4,3,2,1,0:T(8,128)S(1)}, f32[1,2,48,16,128]{4,3,2,1,0:T(8,128)}, u32[]{:S(2)}) copy-start(f32[1,2,48,16,128]{4,3,2,1,0:T(8,128)} %param.4) | copy-start | bytes 2359300
  1.8 1.5 %copy-start.1 = (f32[1,2,48,16,128]{4,3,2,1,0:T(8,128)S(1)}, f32[1,2,48,16,128]{4,3,2,1,0:T(8,128)}, u32[]{:S(2)}) copy-start(f32[1,2,48,16,128]{4,3,2,1,0:T(8,128)} %param.4) | copy-start | bytes 2359300
  1.8 0.9 %copy-start.3 = (f32[2]{0:T(128)S(1)}, f32[2]{0:T(128)}, u32[]{:S(2)}) copy-start(f32[2]{0:T(128)} %param.6) | copy-start | bytes 28
  1.8 1.4 %collective-permute-start.1 = (f32[2,8,16,128]{3,2,1,0:T(8,128)S(1)}, f32[2,8,16,128]{3,2,1,0:T(8,128)S(1)}, u32[]{:S(2)}, u32[]{:S(2)}) collective-permute-start(f32[2,8,16,128]{3,2,1,0:T(8,128)S(1)} %get-tuple-element.31), channel_id=1, source_target_pairs={{0,16},{16,0},{32,48},{48,32},{64,80},{80,64},{96,112},{112,96},{1... | collective-permute-start | bytes 393224 | tf_op jit(solution)/shard_map/ppermute | solution.py:592
  1.9 7.1 %collective-permute-start = (f32[2,8,16,128]{3,2,1,0:T(8,128)S(1)}, f32[2,8,16,128]{3,2,1,0:T(8,128)S(1)}, u32[]{:S(2)}, u32[]{:S(2)}) collective-permute-start(f32[2,8,16,128]{3,2,1,0:T(8,128)S(1)} %get-tuple-element.30), channel_id=1, source_target_pairs={{16,32},{32,16},{48,64},{64,48},{80,96},{96,80},{17,33},{33,17},{4... | collective-permute-start | bytes 393224 | tf_op jit(solution)/shard_map/ppermute | solution.py:592
  5.0 26.2 %collective-permute-start.2 = (f32[2,48,8,128]{3,2,1,0:T(8,128)S(1)}, f32[2,48,8,128]{3,2,1,0:T(8,128)S(1)}, u32[]{:S(2)}, u32[]{:S(2)}) collective-permute-start(f32[2,48,8,128]{3,2,1,0:T(8,128)S(1)} %get-tuple-element.42), channel_id=1, source_target_pairs={{1,2},{2,1},{3,4},{4,3},{5,6},{6,5},{7,8},{8,7},{9,10},{10,9},{11,... | collective-permute-start | bytes 1179656 | tf_op jit(solution)/shard_map/ppermute | solution.py:592
  5.7 25.5 %collective-permute-start.3 = (f32[2,48,8,128]{3,2,1,0:T(8,128)S(1)}, f32[2,48,8,128]{3,2,1,0:T(8,128)S(1)}, u32[]{:S(2)}, u32[]{:S(2)}) collective-permute-start(f32[2,48,8,128]{3,2,1,0:T(8,128)S(1)} %get-tuple-element.43), channel_id=1, source_target_pairs={{0,1},{1,0},{2,3},{3,2},{4,5},{5,4},{6,7},{7,6},{8,9},{9,8},{10,11... | collective-permute-start | bytes 1179656 | tf_op jit(solution)/shard_map/ppermute | solution.py:592
  9.9 21.2 %collective-permute-start.4 = (f32[2,44,8,128]{3,2,1,0:T(8,128)}, f32[2,44,8,128]{3,2,1,0:T(8,128)S(1)}, u32[]{:S(2)}, u32[]{:S(2)}) collective-permute-start(f32[2,44,8,128]{3,2,1,0:T(8,128)} %get-tuple-element.44), channel_id=1, source_target_pairs={{1,2},{2,1},{3,4},{4,3},{5,6},{6,5},{7,8},{8,7},{9,10},{10,9},{11,... | collective-permute-start | bytes 1081352 | tf_op jit(solution)/shard_map/ppermute | solution.py:592
  10.6 20.5 %collective-permute-start.5 = (f32[2,44,8,128]{3,2,1,0:T(8,128)}, f32[2,44,8,128]{3,2,1,0:T(8,128)S(1)}, u32[]{:S(2)}, u32[]{:S(2)}) collective-permute-start(f32[2,44,8,128]{3,2,1,0:T(8,128)} %get-tuple-element.45), channel_id=1, source_target_pairs={{0,1},{1,0},{2,3},{3,2},{4,5},{5,4},{6,7},{7,6},{8,9},{9,8},{10,11... | collective-permute-start | bytes 1081352 | tf_op jit(solution)/shard_map/ppermute | solution.py:592
  14.6 28.8 %all-to-all-start = ((f32[256,1,128]{2,1,0:T(1,128)}), f32[256,1,128]{2,1,0:T(1,128)S(1)}, u32[]{:S(2)}, u32[]{:S(2)}) async-start(f32[256,1,128]{2,1,0:T(1,128)} %bitcast.3), calls=%async_computation | async-start | bytes 262144 | tf_op jit(solution)/shard_map/all_to_all | solution.py:632
  33.4 16.8 %collective-permute-start.6 = (f32[2,16,16,128]{3,2,1,0:T(8,128)}, f32[2,16,16,128]{3,2,1,0:T(8,128)S(1)}, u32[]{:S(2)}, u32[]{:S(2)}) collective-permute-start(f32[2,16,16,128]{3,2,1,0:T(8,128)} %get-tuple-element.47), channel_id=1, source_target_pairs={{0,128},{1,129},{2,130},{3,131},{4,132},{5,133},{6,134},{7,135},{8... | collective-permute-start | bytes 786440 | tf_op jit(solution)/shard_map/ppermute | solution.py:651
  36.7 13.5 %collective-permute-start.7 = (f32[2,16,16,128]{3,2,1,0:T(8,128)}, f32[2,16,16,128]{3,2,1,0:T(8,128)S(1)}, u32[]{:S(2)}, u32[]{:S(2)}) collective-permute-start(f32[2,16,16,128]{3,2,1,0:T(8,128)} %get-tuple-element.50), channel_id=1, source_target_pairs={{0,128},{1,129},{2,130},{3,131},{4,132},{5,133},{6,134},{7,135},{8... | collective-permute-start | bytes 786440 | tf_op jit(solution)/shard_map/ppermute | solution.py:651
  40.2 4.5 %copy-start.2 = (s32[2,48,16,1]{1,3,2,0:T(1,128)S(1)}, s32[2,48,16,1]{1,3,2,0:T(1,128)}, u32[]{:S(2)}) copy-start(s32[2,48,16,1]{1,3,2,0:T(1,128)} %param.5) | copy-start | bytes 18436
  43.4 11.7 %collective-permute-start.8 = (f32[2,16,16,128]{3,2,1,0:T(8,128)}, f32[2,16,16,128]{3,2,1,0:T(8,128)S(1)}, u32[]{:S(2)}, u32[]{:S(2)}) collective-permute-start(f32[2,16,16,128]{3,2,1,0:T(8,128)} %get-tuple-element.56), channel_id=1, source_target_pairs={{0,128},{1,129},{2,130},{3,131},{4,132},{5,133},{6,134},{7,135},{8... | collective-permute-start | bytes 786440 | tf_op jit(solution)/shard_map/ppermute | solution.py:651

commit v8 on v7

--- a/solution.py
+++ b/solution.py
@@ -517,11 +517,20 @@
     grad[...] = jnp.where(iota((1, 2), 1) == 0, total[0], total[1])
 
 
-def sum_kernel(main, *refs):
-    out = refs[PARTS]
-    for i in range(PARTS):
+def sum_kernel(which, main, *refs):
+    extras, (out, total, sems) = refs[:len(which)], refs[-3:]
+    copies = []
+    for n, i in enumerate(which):
         at = slice(i * PART, (i + 1) * PART)
-        out[0, :, at] = main[:, at] + refs[i][...]
+        total[:, n * PART:(n + 1) * PART] = main[:, at] + extras[n][...]
+        copies.append(pltpu.make_async_copy(total.at[:, n * PART:(n + 1) * PART], out.at[0, :, at], sems.at[n]))
+        copies[-1].start()
+    for copy in copies:
+        copy.wait()
+
+
+def last_sum_kernel(which, main, extra, before, out, total, sems):
+    sum_kernel(which, main, extra, out, total, sems)
 
 
 def wall_response():
@@ -661,10 +670,18 @@
                                              pltpu.SemaphoreType.DMA((PARTS + 1,))],
         compiler_params=limit(16),
     )(*[in_hbm(main) for main in mains], rows, by_wall, by_block, in_hbm(response))
-    advanced = pl.pallas_call(
-        sum_kernel, out_shape=shape(1, 2, ROWS, COLS, LANES), in_specs=vmem(PARTS + 1), out_specs=vmem(1)[0],
-        compiler_params=limit(8),
-    )(total, *extras)
+    def sums(kernel, which, operands, specs, aliases):
+        return pl.pallas_call(
+            functools.partial(kernel, which), out_shape=pltpu.HBM((1, 2, ROWS, COLS, LANES), jnp.float32), in_specs=specs,
+            out_specs=pl.BlockSpec(memory_space=pl.ANY), input_output_aliases=aliases,
+            scratch_shapes=[pltpu.VMEM((2, len(which) * PART, COLS, LANES), jnp.float32), pltpu.SemaphoreType.DMA((len(which),))],
+            compiler_params=limit(8),
+        )(*operands)
+
+    early = tuple(range(PARTS - 1))
+    advanced = sums(sum_kernel, early, (total, *extras[:-1]), vmem(PARTS), {})
+    advanced = sums(last_sum_kernel, (PARTS - 1,), (total, extras[-1], advanced),
+                    vmem(2) + [pl.BlockSpec(memory_space=pl.ANY)], {2: 0})
     return (advanced, grad.reshape(2))
 
 

time: 56.4 us -> 56.4 us (level)
  waiting for transfers between devices: 8.52 us -> 7.67 us
  Pallas kernels: 15.2 us -> 15.8 us
    ppermute x3, waiting for transfers between devices: 4.89 us -> 4.03 us  [per_device(): extras.append(lax.ppermute(send, 'grp', [(0, 1)]))]
    pallas_call x1 -> x2, Pallas kernels: 0.99 us -> 1.59 us  [sums(): pl.pallas_call(functools.partial(kernel, which), out_shape=pltpu.HBM((1,...]
  transfers between devices with their start and end apart: 10 -> 10, of which waited for: 3 -> 3; matrix products, arithmetic and copies ran while one was open for 1% -> 1% of each run, Pallas kernels for 25% -> 27%
where the time goes in v8:
time: 56.4 us; the launch traced here: 56 us
  starting transfers between devices  29.9 us (53%)
  Pallas kernels  15.8 us (28%)
  waiting for transfers between devices  7.67 us (14%)
  local copies, waits for them, and re-layouts  1.61 us (3%)
  between operations  1.04 us (2%)
    all_to_all x1, starting transfers between devices, per_device(): rows = lax.all_to_all(row, AXES, 0, 0, tiled=True)  16.5 us
    ppermute x6, starting transfers between devices, swapped(): return lax.ppermute(array, axis, pairs)  9.57 us
    pallas_call x3, Pallas kernels, bulk(): pl.pallas_call(functools.partial(bulk_kernel, part), out_shape=(half, hal...  6.4 us
    pallas_call x1, Pallas kernels, per_device(): pl.pallas_call(volts_kernel, out_shape=(kept(2, ROWS, COLS, LANES), shape...  5.06 us
    ppermute x3, waiting for transfers between devices, per_device(): extras.append(lax.ppermute(send, 'grp', [(0, 1)]))  4.03 us
    ppermute x3, starting transfers between devices, per_device(): extras.append(lax.ppermute(send, 'grp', [(0, 1)]))  3.86 us
    all_to_all x1, waiting for transfers between devices, per_device(): rows = lax.all_to_all(row, AXES, 0, 0, tiled=True)  3.18 us
    pallas_call x1, Pallas kernels, per_device(): pl.pallas_call(wall_kernel, out_shape=kept(devices, LANES), in_specs=vmem...  1.65 us
  transfers between devices with their start and end apart: 10, of which 3 were waited for; matrix products, arithmetic and copies ran while one was open for 1% of the time, Pallas kernels for 27%

profile of v8, /device:TPU:32, one launch (start us, length us, event | category | flops | bytes accessed | tf_op | source)
XLA Modules:
  0.0 56.0 jit_solution(6660972321087798153)
XLA Ops:
  0.6 1.1 %copy-done = f32[1,2,48,16,128]{4,3,2,1,0:T(8,128)S(1)} copy-done((f32[1,2,48,16,128]{4,3,2,1,0:T(8,128)S(1)}, f32[1,2,48,16,128]{4,3,2,1,0:T(8,128)}, u32[]{:S(2)}) %copy-start) | copy-done | bytes 786456
  1.8 0.1 collective-permute-start.1
  1.9 0.8 %collective-permute-start = (f32[2,8,16,128]{3,2,1,0:T(8,128)S(1)}, f32[2,8,16,128]{3,2,1,0:T(8,128)S(1)}, u32[]{:S(2)}, u32[]{:S(2)}) collective-permute-start(f32[2,8,16,128]{3,2,1,0:T(8,128)S(1)} %get-tuple-element.30), channel_id=1, source_target_pairs={{16,32},{32,16},{48,64},{64,48},{80,96},{96,80},{17,33},{33,17},{4... | collective-permute-start | bytes 393224 | tf_op jit(solution)/shard_map/ppermute | solution.py:601
  2.8 0.4 collective-permute-done.1.near
  3.3 1.6 %shard_map.61 = f32[256,128]{1,0:T(8,128)} custom-call(f32[2,48,16,128]{3,2,1,0:T(8,128)S(1)} %bitcast.14, f32[2,8,16,128]{3,2,1,0:T(8,128)S(1)} %collective-permute-done.1.near, f32[1,128]{1,0:T(1,128)S(1)} %pad_bitcast_fusion.volts), custom_call_target="tpu_custom_call" | custom-call | tf_op jit(solution)/shard_map/pallas_call | solution.py:622
  4.9 0.1 shard_map.62
  5.0 0.7 %collective-permute-start.2 = (f32[2,48,8,128]{3,2,1,0:T(8,128)S(1)}, f32[2,48,8,128]{3,2,1,0:T(8,128)S(1)}, u32[]{:S(2)}, u32[]{:S(2)}) collective-permute-start(f32[2,48,8,128]{3,2,1,0:T(8,128)S(1)} %get-tuple-element.42), channel_id=1, source_target_pairs={{1,2},{2,1},{3,4},{4,3},{5,6},{6,5},{7,8},{8,7},{9,10},{10,9},{11,... | collective-permute-start | bytes 1179656 | tf_op jit(solution)/shard_map/ppermute | solution.py:601
  5.7 3.3 %collective-permute-start.3 = (f32[2,48,8,128]{3,2,1,0:T(8,128)S(1)}, f32[2,48,8,128]{3,2,1,0:T(8,128)S(1)}, u32[]{:S(2)}, u32[]{:S(2)}) collective-permute-start(f32[2,48,8,128]{3,2,1,0:T(8,128)S(1)} %get-tuple-element.43), channel_id=1, source_target_pairs={{0,1},{1,0},{2,3},{3,2},{4,5},{5,4},{6,7},{7,6},{8,9},{9,8},{10,11... | collective-permute-start | bytes 1179656 | tf_op jit(solution)/shard_map/ppermute | solution.py:601
  9.0 0.9 %shard_map.60 = (f32[2,8,16,128]{3,2,1,0:T(8,128)S(1)}, f32[2,8,16,128]{3,2,1,0:T(8,128)S(1)}, f32[2,44,8,128]{3,2,1,0:T(8,128)}, f32[2,44,8,128]{3,2,1,0:T(8,128)}) custom-call(f32[2,48,16,128]{3,2,1,0:T(8,128)S(1)} %bitcast.16, f32[2,8,16,128]{3,2,1,0:T(8,128)S(1)} %collective-permute-done.far, f32[2,8,16,128]{3,2,1,0:T(8,128)S(1)} %collective-permute-done.1.near), custom_call_target="tpu_custom_call" | custom-call | tf_op jit(solution)/shard_map/pallas_call | solution.py:632
  9.9 0.7 %collective-permute-start.4 = (f32[2,44,8,128]{3,2,1,0:T(8,128)}, f32[2,44,8,128]{3,2,1,0:T(8,128)S(1)}, u32[]{:S(2)}, u32[]{:S(2)}) collective-permute-start(f32[2,44,8,128]{3,2,1,0:T(8,128)} %get-tuple-element.44), channel_id=1, source_target_pairs={{1,2},{2,1},{3,4},{4,3},{5,6},{6,5},{7,8},{8,7},{9,10},{10,9},{11,... | collective-permute-start | bytes 1081352 | tf_op jit(solution)/shard_map/ppermute | solution.py:601
  10.6 4.0 %collective-permute-start.5 = (f32[2,44,8,128]{3,2,1,0:T(8,128)}, f32[2,44,8,128]{3,2,1,0:T(8,128)S(1)}, u32[]{:S(2)}, u32[]{:S(2)}) collective-permute-start(f32[2,44,8,128]{3,2,1,0:T(8,128)} %get-tuple-element.45), channel_id=1, source_target_pairs={{0,1},{1,0},{2,3},{3,2},{4,5},{5,4},{6,7},{7,6},{8,9},{9,8},{10,11... | collective-permute-start | bytes 1081352 | tf_op jit(solution)/shard_map/ppermute | solution.py:601
  14.6 16.5 %all-to-all-start = ((f32[256,1,128]{2,1,0:T(1,128)}), f32[256,1,128]{2,1,0:T(1,128)S(1)}, u32[]{:S(2)}, u32[]{:S(2)}) async-start(f32[256,1,128]{2,1,0:T(1,128)} %bitcast.3), calls=%async_computation | async-start | bytes 262144 | tf_op jit(solution)/shard_map/all_to_all | solution.py:641
  31.2 2.2 %shard_map.63 = (f32[2,16,16,128]{3,2,1,0:T(8,128)}, f32[2,16,16,128]{3,2,1,0:T(8,128)}) custom-call(f32[2,48,16,128]{3,2,1,0:T(8,128)S(1)} %bitcast.17, f32[2,8,16,128]{3,2,1,0:T(8,128)S(1)} %get-tuple-element.39.yd, f32[2,8,16,128]{3,2,1,0:T(8,128)S(1)} %get-tuple-element.40.yu, f32[2,48,8,128]{3,2,1,0:T(8,128)S(1)} %collective-permute-done.2.z_far, ...), custom_call_target="tpu_custom_call" | custom-call | flops 100000000 | bytes 36000000 | tf_op jit(solution)/shard_map/pallas_call | solution.py:645
  33.4 1.3 %collective-permute-start.7 = (f32[2,16,16,128]{3,2,1,0:T(8,128)}, f32[2,16,16,128]{3,2,1,0:T(8,128)S(1)}, u32[]{:S(2)}, u32[]{:S(2)}) collective-permute-start(f32[2,16,16,128]{3,2,1,0:T(8,128)} %get-tuple-element.47), channel_id=1, source_target_pairs={{0,128},{1,129},{2,130},{3,131},{4,132},{5,133},{6,134},{7,135},{8... | collective-permute-start | bytes 786440 | tf_op jit(solution)/shard_map/ppermute | solution.py:660
  34.7 2.0 %shard_map.64 = (f32[2,16,16,128]{3,2,1,0:T(8,128)}, f32[2,16,16,128]{3,2,1,0:T(8,128)}) custom-call(f32[2,48,16,128]{3,2,1,0:T(8,128)S(1)} %bitcast.18, f32[2,8,16,128]{3,2,1,0:T(8,128)S(1)} %get-tuple-element.39.yd, f32[2,8,16,128]{3,2,1,0:T(8,128)S(1)} %get-tuple-element.40.yu, f32[2,48,8,128]{3,2,1,0:T(8,128)S(1)} %collective-permute-done.2.z_far, ...), custom_call_target="tpu_custom_call" | custom-call | flops 100000000 | bytes 9000000 | tf_op jit(solution)/shard_map/pallas_call | solution.py:645
  36.7 1.3 %collective-permute-start.8 = (f32[2,16,16,128]{3,2,1,0:T(8,128)}, f32[2,16,16,128]{3,2,1,0:T(8,128)S(1)}, u32[]{:S(2)}, u32[]{:S(2)}) collective-permute-start(f32[2,16,16,128]{3,2,1,0:T(8,128)} %get-tuple-element.50), channel_id=1, source_target_pairs={{0,128},{1,129},{2,130},{3,131},{4,132},{5,133},{6,134},{7,135},{8... | collective-permute-start | bytes 786440 | tf_op jit(solution)/shard_map/ppermute | solution.py:660
  38.0 2.2 %shard_map.65 = (f32[2,16,16,128]{3,2,1,0:T(8,128)}, f32[2,16,16,128]{3,2,1,0:T(8,128)}) custom-call(f32[2,48,16,128]{3,2,1,0:T(8,128)S(1)} %bitcast.19, f32[2,8,16,128]{3,2,1,0:T(8,128)S(1)} %get-tuple-element.39.yd, f32[2,8,16,128]{3,2,1,0:T(8,128)S(1)} %get-tuple-element.40.yu, f32[2,48,8,128]{3,2,1,0:T(8,128)S(1)} %collective-permute-done.2.z_far, ...), custom_call_target="tpu_custom_call" | custom-call | flops 100000000 | bytes 9000000 | tf_op jit(solution)/shard_map/pallas_call | solution.py:645
  40.2 3.2 %all-to-all-done = f32[256,1,128]{2,1,0:T(1,128)S(1)} async-done(((f32[256,1,128]{2,1,0:T(1,128)}), f32[256,1,128]{2,1,0:T(1,128)S(1)}, u32[]{:S(2)}, u32[]{:S(2)}) %all-to-all-start) | async-done | bytes 131104 | tf_op jit(solution)/shard_map/all_to_all | solution.py:641
  43.4 1.3 %collective-permute-start.6 = (f32[2,16,16,128]{3,2,1,0:T(8,128)}, f32[2,16,16,128]{3,2,1,0:T(8,128)S(1)}, u32[]{:S(2)}, u32[]{:S(2)}) collective-permute-start(f32[2,16,16,128]{3,2,1,0:T(8,128)} %get-tuple-element.56), channel_id=1, source_target_pairs={{0,128},{1,129},{2,130},{3,131},{4,132},{5,133},{6,134},{7,135},{8... | collective-permute-start | bytes 786440 | tf_op jit(solution)/shard_map/ppermute | solution.py:660
  44.9 0.1 reshape.12.refs_4_
  45.1 5.1 %shard_map.66 = (f32[2,48,16,128]{3,2,1,0:T(8,128)S(1)}, f32[1,2]{1,0:T(1,128)}) custom-call(f32[2,16,16,128]{3,2,1,0:T(8,128)} %get-tuple-element.46.refs_0_, f32[2,16,16,128]{3,2,1,0:T(8,128)} %get-tuple-element.49.refs_1_, f32[2,16,16,128]{3,2,1,0:T(8,128)} %get-tuple-element.52.refs_2_, f32[256,128]{1,0:T(8,128)S(1)} %bitcast.20, ...), custom_call_target="tpu_custom_call" | custom-call | tf_op jit(solution)/shard_map/pallas_call | solution.py:666
  50.2 0.8 %shard_map.67.before = f32[1,2,48,16,128]{4,3,2,1,0:T(8,128)} custom-call(f32[2,48,16,128]{3,2,1,0:T(8,128)S(1)} %get-tuple-element.55.main, f32[2,16,16,128]{3,2,1,0:T(8,128)S(1)} %collective-permute-done.7.refs_0_, f32[2,16,16,128]{3,2,1,0:T(8,128)S(1)} %collective-permute-done.8.refs_1_), custom_call_target="tpu_custom_call" | custom-call | tf_op jit(solution)/shard_map/pallas_call | solution.py:674
  51.1 4.0 %collective-permute-done.6.extra = f32[2,16,16,128]{3,2,1,0:T(8,128)S(1)} collective-permute-done((f32[2,16,16,128]{3,2,1,0:T(8,128)}, f32[2,16,16,128]{3,2,1,0:T(8,128)S(1)}, u32[]{:S(2)}, u32[]{:S(2)}) %collective-permute-start.6) | collective-permute-done | bytes 262176 | tf_op jit(solution)/shard_map/ppermute | solution.py:660
  55.1 0.7 %shard_map.68 = f32[1,2,48,16,128]{4,3,2,1,0:T(8,128)} custom-call(f32[2,48,16,128]{3,2,1,0:T(8,128)S(1)} %get-tuple-element.55.main, f32[2,16,16,128]{3,2,1,0:T(8,128)S(1)} %collective-permute-done.6.extra, f32[1,2,48,16,128]{4,3,2,1,0:T(8,128)} %shard_map.67.before), custom_call_target="tpu_custom_call", output_to_operand_aliasing={{}: (2, {})} | custom-call | tf_op jit(solution)/shard_map/pallas_call | solution.py:674
  (21 shorter events, 0.4 us)
Async XLA Ops:
  0.6 1.1 %copy-start = (f32[1,2,48,16,128]{4,3,2,1,0:T(8,128)S(1)}, f32[1,2,48,16,128]{4,3,2,1,0:T(8,128)}, u32[]{:S(2)}) copy-start(f32[1,2,48,16,128]{4,3,2,1,0:T(8,128)} %param.4) | copy-start | bytes 2359300
  1.8 1.5 %copy-start.1 = (f32[1,2,48,16,128]{4,3,2,1,0:T(8,128)S(1)}, f32[1,2,48,16,128]{4,3,2,1,0:T(8,128)}, u32[]{:S(2)}) copy-start(f32[1,2,48,16,128]{4,3,2,1,0:T(8,128)} %param.4) | copy-start | bytes 2359300
  1.8 0.9 %copy-start.3 = (f32[2]{0:T(128)S(1)}, f32[2]{0:T(128)}, u32[]{:S(2)}) copy-start(f32[2]{0:T(128)} %param.6) | copy-start | bytes 28
  1.8 1.4 %collective-permute-start.1 = (f32[2,8,16,128]{3,2,1,0:T(8,128)S(1)}, f32[2,8,16,128]{3,2,1,0:T(8,128)S(1)}, u32[]{:S(2)}, u32[]{:S(2)}) collective-permute-start(f32[2,8,16,128]{3,2,1,0:T(8,128)S(1)} %get-tuple-element.31), channel_id=1, source_target_pairs={{0,16},{16,0},{32,48},{48,32},{64,80},{80,64},{96,112},{112,96},{1... | collective-permute-start | bytes 393224 | tf_op jit(solution)/shard_map/ppermute | solution.py:601
  1.9 7.1 %collective-permute-start = (f32[2,8,16,128]{3,2,1,0:T(8,128)S(1)}, f32[2,8,16,128]{3,2,1,0:T(8,128)S(1)}, u32[]{:S(2)}, u32[]{:S(2)}) collective-permute-start(f32[2,8,16,128]{3,2,1,0:T(8,128)S(1)} %get-tuple-element.30), channel_id=1, source_target_pairs={{16,32},{32,16},{48,64},{64,48},{80,96},{96,80},{17,33},{33,17},{4... | collective-permute-start | bytes 393224 | tf_op jit(solution)/shard_map/ppermute | solution.py:601
  5.0 26.2 %collective-permute-start.2 = (f32[2,48,8,128]{3,2,1,0:T(8,128)S(1)}, f32[2,48,8,128]{3,2,1,0:T(8,128)S(1)}, u32[]{:S(2)}, u32[]{:S(2)}) collective-permute-start(f32[2,48,8,128]{3,2,1,0:T(8,128)S(1)} %get-tuple-element.42), channel_id=1, source_target_pairs={{1,2},{2,1},{3,4},{4,3},{5,6},{6,5},{7,8},{8,7},{9,10},{10,9},{11,... | collective-permute-start | bytes 1179656 | tf_op jit(solution)/shard_map/ppermute | solution.py:601
  5.7 25.5 %collective-permute-start.3 = (f32[2,48,8,128]{3,2,1,0:T(8,128)S(1)}, f32[2,48,8,128]{3,2,1,0:T(8,128)S(1)}, u32[]{:S(2)}, u32[]{:S(2)}) collective-permute-start(f32[2,48,8,128]{3,2,1,0:T(8,128)S(1)} %get-tuple-element.43), channel_id=1, source_target_pairs={{0,1},{1,0},{2,3},{3,2},{4,5},{5,4},{6,7},{7,6},{8,9},{9,8},{10,11... | collective-permute-start | bytes 1179656 | tf_op jit(solution)/shard_map/ppermute | solution.py:601
  9.9 21.2 %collective-permute-start.4 = (f32[2,44,8,128]{3,2,1,0:T(8,128)}, f32[2,44,8,128]{3,2,1,0:T(8,128)S(1)}, u32[]{:S(2)}, u32[]{:S(2)}) collective-permute-start(f32[2,44,8,128]{3,2,1,0:T(8,128)} %get-tuple-element.44), channel_id=1, source_target_pairs={{1,2},{2,1},{3,4},{4,3},{5,6},{6,5},{7,8},{8,7},{9,10},{10,9},{11,... | collective-permute-start | bytes 1081352 | tf_op jit(solution)/shard_map/ppermute | solution.py:601
  10.6 20.5 %collective-permute-start.5 = (f32[2,44,8,128]{3,2,1,0:T(8,128)}, f32[2,44,8,128]{3,2,1,0:T(8,128)S(1)}, u32[]{:S(2)}, u32[]{:S(2)}) collective-permute-start(f32[2,44,8,128]{3,2,1,0:T(8,128)} %get-tuple-element.45), channel_id=1, source_target_pairs={{0,1},{1,0},{2,3},{3,2},{4,5},{5,4},{6,7},{7,6},{8,9},{9,8},{10,11... | collective-permute-start | bytes 1081352 | tf_op jit(solution)/shard_map/ppermute | solution.py:601
  14.6 28.8 %all-to-all-start = ((f32[256,1,128]{2,1,0:T(1,128)}), f32[256,1,128]{2,1,0:T(1,128)S(1)}, u32[]{:S(2)}, u32[]{:S(2)}) async-start(f32[256,1,128]{2,1,0:T(1,128)} %bitcast.3), calls=%async_computation | async-start | bytes 262144 | tf_op jit(solution)/shard_map/all_to_all | solution.py:641
  33.4 16.8 %collective-permute-start.7 = (f32[2,16,16,128]{3,2,1,0:T(8,128)}, f32[2,16,16,128]{3,2,1,0:T(8,128)S(1)}, u32[]{:S(2)}, u32[]{:S(2)}) collective-permute-start(f32[2,16,16,128]{3,2,1,0:T(8,128)} %get-tuple-element.47), channel_id=1, source_target_pairs={{0,128},{1,129},{2,130},{3,131},{4,132},{5,133},{6,134},{7,135},{8... | collective-permute-start | bytes 786440 | tf_op jit(solution)/shard_map/ppermute | solution.py:660
  36.7 13.5 %collective-permute-start.8 = (f32[2,16,16,128]{3,2,1,0:T(8,128)}, f32[2,16,16,128]{3,2,1,0:T(8,128)S(1)}, u32[]{:S(2)}, u32[]{:S(2)}) collective-permute-start(f32[2,16,16,128]{3,2,1,0:T(8,128)} %get-tuple-element.50), channel_id=1, source_target_pairs={{0,128},{1,129},{2,130},{3,131},{4,132},{5,133},{6,134},{7,135},{8... | collective-permute-start | bytes 786440 | tf_op jit(solution)/shard_map/ppermute | solution.py:660
  40.2 4.5 %copy-start.2 = (s32[2,48,16,1]{1,3,2,0:T(1,128)S(1)}, s32[2,48,16,1]{1,3,2,0:T(1,128)}, u32[]{:S(2)}) copy-start(s32[2,48,16,1]{1,3,2,0:T(1,128)} %param.5) | copy-start | bytes 18436
  43.4 11.7 %collective-permute-start.6 = (f32[2,16,16,128]{3,2,1,0:T(8,128)}, f32[2,16,16,128]{3,2,1,0:T(8,128)S(1)}, u32[]{:S(2)}, u32[]{:S(2)}) collective-permute-start(f32[2,16,16,128]{3,2,1,0:T(8,128)} %get-tuple-element.56), channel_id=1, source_target_pairs={{0,128},{1,129},{2,130},{3,131},{4,132},{5,133},{6,134},{7,135},{8... | collective-permute-start | bytes 786440 | tf_op jit(solution)/shard_map/ppermute | solution.py:660

commit v9 on v8

--- a/solution.py
+++ b/solution.py
@@ -19,7 +19,7 @@
 PARTS = 3
 PART = ROWS // PARTS
 SIXTH = 1.0 / 6.0
-SHARE, PIECES = 0.34, 3
+SHARE, PIECES = 0.2, 3
 
 BULK = ((12, 40), (8, 32), (4, 24))
 NEAR = ((0, COLS),) * 3

time: 56.4 us -> 56.3 us (level)
  transfers between devices with their start and end apart: 10 -> 10, of which waited for: 3 -> 3; matrix products, arithmetic and copies ran while one was open for 1% -> 1% of each run, Pallas kernels for 27% -> 26%
where the time goes in v9:
time: 56.3 us; the launch traced here: 56 us
  starting transfers between devices  29.9 us (53%)
  Pallas kernels  15.6 us (28%)
  waiting for transfers between devices  7.82 us (14%)
  local copies, waits for them, and re-layouts  1.61 us (3%)
  between operations  1.03 us (2%)
    all_to_all x1, starting transfers between devices, per_device(): rows = lax.all_to_all(row, AXES, 0, 0, tiled=True)  16.5 us
    ppermute x6, starting transfers between devices, swapped(): return lax.ppermute(array, axis, pairs)  9.57 us
    pallas_call x3, Pallas kernels, bulk(): pl.pallas_call(functools.partial(bulk_kernel, part), out_shape=(half, hal...  6.2 us
    pallas_call x1, Pallas kernels, per_device(): pl.pallas_call(volts_kernel, out_shape=(kept(2, ROWS, COLS, LANES), shape...  5.06 us
    ppermute x3, waiting for transfers between devices, per_device(): extras.append(lax.ppermute(send, 'grp', [(0, 1)]))  3.98 us
    ppermute x3, starting transfers between devices, per_device(): extras.append(lax.ppermute(send, 'grp', [(0, 1)]))  3.86 us
    all_to_all x1, waiting for transfers between devices, per_device(): rows = lax.all_to_all(row, AXES, 0, 0, tiled=True)  3.38 us
    pallas_call x1, Pallas kernels, per_device(): pl.pallas_call(wall_kernel, out_shape=kept(devices, LANES), in_specs=vmem...  1.65 us
  transfers between devices with their start and end apart: 10, of which 3 were waited for; matrix products, arithmetic and copies ran while one was open for 1% of the time, Pallas kernels for 26%

profile of v9, /device:TPU:32, one launch (start us, length us, event | category | flops | bytes accessed | tf_op | source)
XLA Modules:
  0.0 56.0 jit_solution(7467510660610917782)
XLA Ops:
  0.6 1.1 %copy-done = f32[1,2,48,16,128]{4,3,2,1,0:T(8,128)S(1)} copy-done((f32[1,2,48,16,128]{4,3,2,1,0:T(8,128)S(1)}, f32[1,2,48,16,128]{4,3,2,1,0:T(8,128)}, u32[]{:S(2)}) %copy-start) | copy-done | bytes 786456
  1.8 0.1 collective-permute-start.1
  1.9 0.8 %collective-permute-start = (f32[2,8,16,128]{3,2,1,0:T(8,128)S(1)}, f32[2,8,16,128]{3,2,1,0:T(8,128)S(1)}, u32[]{:S(2)}, u32[]{:S(2)}) collective-permute-start(f32[2,8,16,128]{3,2,1,0:T(8,128)S(1)} %get-tuple-element.30), channel_id=1, source_target_pairs={{16,32},{32,16},{48,64},{64,48},{80,96},{96,80},{17,33},{33,17},{4... | collective-permute-start | bytes 393224 | tf_op jit(solution)/shard_map/ppermute | solution.py:601
  2.8 0.4 collective-permute-done.1.near
  3.3 1.6 %shard_map.61 = f32[256,128]{1,0:T(8,128)} custom-call(f32[2,48,16,128]{3,2,1,0:T(8,128)S(1)} %bitcast.14, f32[2,8,16,128]{3,2,1,0:T(8,128)S(1)} %collective-permute-done.1.near, f32[1,128]{1,0:T(1,128)S(1)} %pad_bitcast_fusion.volts), custom_call_target="tpu_custom_call" | custom-call | tf_op jit(solution)/shard_map/pallas_call | solution.py:622
  4.9 0.1 shard_map.62
  5.0 0.7 %collective-permute-start.2 = (f32[2,48,8,128]{3,2,1,0:T(8,128)S(1)}, f32[2,48,8,128]{3,2,1,0:T(8,128)S(1)}, u32[]{:S(2)}, u32[]{:S(2)}) collective-permute-start(f32[2,48,8,128]{3,2,1,0:T(8,128)S(1)} %get-tuple-element.42), channel_id=1, source_target_pairs={{1,2},{2,1},{3,4},{4,3},{5,6},{6,5},{7,8},{8,7},{9,10},{10,9},{11,... | collective-permute-start | bytes 1179656 | tf_op jit(solution)/shard_map/ppermute | solution.py:601
  5.7 3.3 %collective-permute-start.3 = (f32[2,48,8,128]{3,2,1,0:T(8,128)S(1)}, f32[2,48,8,128]{3,2,1,0:T(8,128)S(1)}, u32[]{:S(2)}, u32[]{:S(2)}) collective-permute-start(f32[2,48,8,128]{3,2,1,0:T(8,128)S(1)} %get-tuple-element.43), channel_id=1, source_target_pairs={{0,1},{1,0},{2,3},{3,2},{4,5},{5,4},{6,7},{7,6},{8,9},{9,8},{10,11... | collective-permute-start | bytes 1179656 | tf_op jit(solution)/shard_map/ppermute | solution.py:601
  9.0 0.9 %shard_map.60 = (f32[2,8,16,128]{3,2,1,0:T(8,128)S(1)}, f32[2,8,16,128]{3,2,1,0:T(8,128)S(1)}, f32[2,44,8,128]{3,2,1,0:T(8,128)}, f32[2,44,8,128]{3,2,1,0:T(8,128)}) custom-call(f32[2,48,16,128]{3,2,1,0:T(8,128)S(1)} %bitcast.16, f32[2,8,16,128]{3,2,1,0:T(8,128)S(1)} %collective-permute-done.far, f32[2,8,16,128]{3,2,1,0:T(8,128)S(1)} %collective-permute-done.1.near), custom_call_target="tpu_custom_call" | custom-call | tf_op jit(solution)/shard_map/pallas_call | solution.py:632
  9.9 0.7 %collective-permute-start.4 = (f32[2,44,8,128]{3,2,1,0:T(8,128)}, f32[2,44,8,128]{3,2,1,0:T(8,128)S(1)}, u32[]{:S(2)}, u32[]{:S(2)}) collective-permute-start(f32[2,44,8,128]{3,2,1,0:T(8,128)} %get-tuple-element.44), channel_id=1, source_target_pairs={{1,2},{2,1},{3,4},{4,3},{5,6},{6,5},{7,8},{8,7},{9,10},{10,9},{11,... | collective-permute-start | bytes 1081352 | tf_op jit(solution)/shard_map/ppermute | solution.py:601
  10.6 4.0 %collective-permute-start.5 = (f32[2,44,8,128]{3,2,1,0:T(8,128)}, f32[2,44,8,128]{3,2,1,0:T(8,128)S(1)}, u32[]{:S(2)}, u32[]{:S(2)}) collective-permute-start(f32[2,44,8,128]{3,2,1,0:T(8,128)} %get-tuple-element.45), channel_id=1, source_target_pairs={{0,1},{1,0},{2,3},{3,2},{4,5},{5,4},{6,7},{7,6},{8,9},{9,8},{10,11... | collective-permute-start | bytes 1081352 | tf_op jit(solution)/shard_map/ppermute | solution.py:601
  14.6 16.5 %all-to-all-start = ((f32[256,1,128]{2,1,0:T(1,128)}), f32[256,1,128]{2,1,0:T(1,128)S(1)}, u32[]{:S(2)}, u32[]{:S(2)}) async-start(f32[256,1,128]{2,1,0:T(1,128)} %bitcast.3), calls=%async_computation | async-start | bytes 262144 | tf_op jit(solution)/shard_map/all_to_all | solution.py:641
  31.2 2.1 %shard_map.63 = (f32[2,16,16,128]{3,2,1,0:T(8,128)}, f32[2,16,16,128]{3,2,1,0:T(8,128)}) custom-call(f32[2,48,16,128]{3,2,1,0:T(8,128)S(1)} %bitcast.17, f32[2,8,16,128]{3,2,1,0:T(8,128)S(1)} %get-tuple-element.39.yd, f32[2,8,16,128]{3,2,1,0:T(8,128)S(1)} %get-tuple-element.40.yu, f32[2,48,8,128]{3,2,1,0:T(8,128)S(1)} %collective-permute-done.2.z_far, ...), custom_call_target="tpu_custom_call" | custom-call | flops 100000000 | bytes 36000000 | tf_op jit(solution)/shard_map/pallas_call | solution.py:645
  33.3 1.3 %collective-permute-start.7 = (f32[2,16,16,128]{3,2,1,0:T(8,128)}, f32[2,16,16,128]{3,2,1,0:T(8,128)S(1)}, u32[]{:S(2)}, u32[]{:S(2)}) collective-permute-start(f32[2,16,16,128]{3,2,1,0:T(8,128)} %get-tuple-element.47), channel_id=1, source_target_pairs={{0,128},{1,129},{2,130},{3,131},{4,132},{5,133},{6,134},{7,135},{8... | collective-permute-start | bytes 786440 | tf_op jit(solution)/shard_map/ppermute | solution.py:660
  34.6 1.9 %shard_map.64 = (f32[2,16,16,128]{3,2,1,0:T(8,128)}, f32[2,16,16,128]{3,2,1,0:T(8,128)}) custom-call(f32[2,48,16,128]{3,2,1,0:T(8,128)S(1)} %bitcast.18, f32[2,8,16,128]{3,2,1,0:T(8,128)S(1)} %get-tuple-element.39.yd, f32[2,8,16,128]{3,2,1,0:T(8,128)S(1)} %get-tuple-element.40.yu, f32[2,48,8,128]{3,2,1,0:T(8,128)S(1)} %collective-permute-done.2.z_far, ...), custom_call_target="tpu_custom_call" | custom-call | flops 100000000 | bytes 9000000 | tf_op jit(solution)/shard_map/pallas_call | solution.py:645
  36.6 1.3 %collective-permute-start.8 = (f32[2,16,16,128]{3,2,1,0:T(8,128)}, f32[2,16,16,128]{3,2,1,0:T(8,128)S(1)}, u32[]{:S(2)}, u32[]{:S(2)}) collective-permute-start(f32[2,16,16,128]{3,2,1,0:T(8,128)} %get-tuple-element.50), channel_id=1, source_target_pairs={{0,128},{1,129},{2,130},{3,131},{4,132},{5,133},{6,134},{7,135},{8... | collective-permute-start | bytes 786440 | tf_op jit(solution)/shard_map/ppermute | solution.py:660
  37.9 2.2 %shard_map.65 = (f32[2,16,16,128]{3,2,1,0:T(8,128)}, f32[2,16,16,128]{3,2,1,0:T(8,128)}) custom-call(f32[2,48,16,128]{3,2,1,0:T(8,128)S(1)} %bitcast.19, f32[2,8,16,128]{3,2,1,0:T(8,128)S(1)} %get-tuple-element.39.yd, f32[2,8,16,128]{3,2,1,0:T(8,128)S(1)} %get-tuple-element.40.yu, f32[2,48,8,128]{3,2,1,0:T(8,128)S(1)} %collective-permute-done.2.z_far, ...), custom_call_target="tpu_custom_call" | custom-call | flops 100000000 | bytes 9000000 | tf_op jit(solution)/shard_map/pallas_call | solution.py:645
  40.0 3.4 %all-to-all-done = f32[256,1,128]{2,1,0:T(1,128)S(1)} async-done(((f32[256,1,128]{2,1,0:T(1,128)}), f32[256,1,128]{2,1,0:T(1,128)S(1)}, u32[]{:S(2)}, u32[]{:S(2)}) %all-to-all-start) | async-done | bytes 131104 | tf_op jit(solution)/shard_map/all_to_all | solution.py:641
  43.4 1.3 %collective-permute-start.6 = (f32[2,16,16,128]{3,2,1,0:T(8,128)}, f32[2,16,16,128]{3,2,1,0:T(8,128)S(1)}, u32[]{:S(2)}, u32[]{:S(2)}) collective-permute-start(f32[2,16,16,128]{3,2,1,0:T(8,128)} %get-tuple-element.56), channel_id=1, source_target_pairs={{0,128},{1,129},{2,130},{3,131},{4,132},{5,133},{6,134},{7,135},{8... | collective-permute-start | bytes 786440 | tf_op jit(solution)/shard_map/ppermute | solution.py:660
  44.9 0.1 reshape.12.refs_4_
  45.1 5.1 %shard_map.66 = (f32[2,48,16,128]{3,2,1,0:T(8,128)S(1)}, f32[1,2]{1,0:T(1,128)}) custom-call(f32[2,16,16,128]{3,2,1,0:T(8,128)} %get-tuple-element.46.refs_0_, f32[2,16,16,128]{3,2,1,0:T(8,128)} %get-tuple-element.49.refs_1_, f32[2,16,16,128]{3,2,1,0:T(8,128)} %get-tuple-element.52.refs_2_, f32[256,128]{1,0:T(8,128)S(1)} %bitcast.20, ...), custom_call_target="tpu_custom_call" | custom-call | tf_op jit(solution)/shard_map/pallas_call | solution.py:666
  50.2 0.8 %shard_map.67.before = f32[1,2,48,16,128]{4,3,2,1,0:T(8,128)} custom-call(f32[2,48,16,128]{3,2,1,0:T(8,128)S(1)} %get-tuple-element.55.main, f32[2,16,16,128]{3,2,1,0:T(8,128)S(1)} %collective-permute-done.7.refs_0_, f32[2,16,16,128]{3,2,1,0:T(8,128)S(1)} %collective-permute-done.8.refs_1_), custom_call_target="tpu_custom_call" | custom-call | tf_op jit(solution)/shard_map/pallas_call | solution.py:674
  51.1 4.0 %collective-permute-done.6.extra = f32[2,16,16,128]{3,2,1,0:T(8,128)S(1)} collective-permute-done((f32[2,16,16,128]{3,2,1,0:T(8,128)}, f32[2,16,16,128]{3,2,1,0:T(8,128)S(1)}, u32[]{:S(2)}, u32[]{:S(2)}) %collective-permute-start.6) | collective-permute-done | bytes 262176 | tf_op jit(solution)/shard_map/ppermute | solution.py:660
  55.0 0.7 %shard_map.68 = f32[1,2,48,16,128]{4,3,2,1,0:T(8,128)} custom-call(f32[2,48,16,128]{3,2,1,0:T(8,128)S(1)} %get-tuple-element.55.main, f32[2,16,16,128]{3,2,1,0:T(8,128)S(1)} %collective-permute-done.6.extra, f32[1,2,48,16,128]{4,3,2,1,0:T(8,128)} %shard_map.67.before), custom_call_target="tpu_custom_call", output_to_operand_aliasing={{}: (2, {})} | custom-call | tf_op jit(solution)/shard_map/pallas_call | solution.py:674
  (21 shorter events, 0.5 us)
Async XLA Ops:
  0.6 1.1 %copy-start = (f32[1,2,48,16,128]{4,3,2,1,0:T(8,128)S(1)}, f32[1,2,48,16,128]{4,3,2,1,0:T(8,128)}, u32[]{:S(2)}) copy-start(f32[1,2,48,16,128]{4,3,2,1,0:T(8,128)} %param.4) | copy-start | bytes 2359300
  1.8 1.5 %copy-start.1 = (f32[1,2,48,16,128]{4,3,2,1,0:T(8,128)S(1)}, f32[1,2,48,16,128]{4,3,2,1,0:T(8,128)}, u32[]{:S(2)}) copy-start(f32[1,2,48,16,128]{4,3,2,1,0:T(8,128)} %param.4) | copy-start | bytes 2359300
  1.8 0.9 %copy-start.3 = (f32[2]{0:T(128)S(1)}, f32[2]{0:T(128)}, u32[]{:S(2)}) copy-start(f32[2]{0:T(128)} %param.6) | copy-start | bytes 28
  1.8 1.4 %collective-permute-start.1 = (f32[2,8,16,128]{3,2,1,0:T(8,128)S(1)}, f32[2,8,16,128]{3,2,1,0:T(8,128)S(1)}, u32[]{:S(2)}, u32[]{:S(2)}) collective-permute-start(f32[2,8,16,128]{3,2,1,0:T(8,128)S(1)} %get-tuple-element.31), channel_id=1, source_target_pairs={{0,16},{16,0},{32,48},{48,32},{64,80},{80,64},{96,112},{112,96},{1... | collective-permute-start | bytes 393224 | tf_op jit(solution)/shard_map/ppermute | solution.py:601
  1.9 7.1 %collective-permute-start = (f32[2,8,16,128]{3,2,1,0:T(8,128)S(1)}, f32[2,8,16,128]{3,2,1,0:T(8,128)S(1)}, u32[]{:S(2)}, u32[]{:S(2)}) collective-permute-start(f32[2,8,16,128]{3,2,1,0:T(8,128)S(1)} %get-tuple-element.30), channel_id=1, source_target_pairs={{16,32},{32,16},{48,64},{64,48},{80,96},{96,80},{17,33},{33,17},{4... | collective-permute-start | bytes 393224 | tf_op jit(solution)/shard_map/ppermute | solution.py:601
  5.0 26.2 %collective-permute-start.2 = (f32[2,48,8,128]{3,2,1,0:T(8,128)S(1)}, f32[2,48,8,128]{3,2,1,0:T(8,128)S(1)}, u32[]{:S(2)}, u32[]{:S(2)}) collective-permute-start(f32[2,48,8,128]{3,2,1,0:T(8,128)S(1)} %get-tuple-element.42), channel_id=1, source_target_pairs={{1,2},{2,1},{3,4},{4,3},{5,6},{6,5},{7,8},{8,7},{9,10},{10,9},{11,... | collective-permute-start | bytes 1179656 | tf_op jit(solution)/shard_map/ppermute | solution.py:601
  5.7 25.5 %collective-permute-start.3 = (f32[2,48,8,128]{3,2,1,0:T(8,128)S(1)}, f32[2,48,8,128]{3,2,1,0:T(8,128)S(1)}, u32[]{:S(2)}, u32[]{:S(2)}) collective-permute-start(f32[2,48,8,128]{3,2,1,0:T(8,128)S(1)} %get-tuple-element.43), channel_id=1, source_target_pairs={{0,1},{1,0},{2,3},{3,2},{4,5},{5,4},{6,7},{7,6},{8,9},{9,8},{10,11... | collective-permute-start | bytes 1179656 | tf_op jit(solution)/shard_map/ppermute | solution.py:601
  9.9 21.2 %collective-permute-start.4 = (f32[2,44,8,128]{3,2,1,0:T(8,128)}, f32[2,44,8,128]{3,2,1,0:T(8,128)S(1)}, u32[]{:S(2)}, u32[]{:S(2)}) collective-permute-start(f32[2,44,8,128]{3,2,1,0:T(8,128)} %get-tuple-element.44), channel_id=1, source_target_pairs={{1,2},{2,1},{3,4},{4,3},{5,6},{6,5},{7,8},{8,7},{9,10},{10,9},{11,... | collective-permute-start | bytes 1081352 | tf_op jit(solution)/shard_map/ppermute | solution.py:601
  10.6 20.5 %collective-permute-start.5 = (f32[2,44,8,128]{3,2,1,0:T(8,128)}, f32[2,44,8,128]{3,2,1,0:T(8,128)S(1)}, u32[]{:S(2)}, u32[]{:S(2)}) collective-permute-start(f32[2,44,8,128]{3,2,1,0:T(8,128)} %get-tuple-element.45), channel_id=1, source_target_pairs={{0,1},{1,0},{2,3},{3,2},{4,5},{5,4},{6,7},{7,6},{8,9},{9,8},{10,11... | collective-permute-start | bytes 1081352 | tf_op jit(solution)/shard_map/ppermute | solution.py:601
  14.6 28.8 %all-to-all-start = ((f32[256,1,128]{2,1,0:T(1,128)}), f32[256,1,128]{2,1,0:T(1,128)S(1)}, u32[]{:S(2)}, u32[]{:S(2)}) async-start(f32[256,1,128]{2,1,0:T(1,128)} %bitcast.3), calls=%async_computation | async-start | bytes 262144 | tf_op jit(solution)/shard_map/all_to_all | solution.py:641
  33.3 16.9 %collective-permute-start.7 = (f32[2,16,16,128]{3,2,1,0:T(8,128)}, f32[2,16,16,128]{3,2,1,0:T(8,128)S(1)}, u32[]{:S(2)}, u32[]{:S(2)}) collective-permute-start(f32[2,16,16,128]{3,2,1,0:T(8,128)} %get-tuple-element.47), channel_id=1, source_target_pairs={{0,128},{1,129},{2,130},{3,131},{4,132},{5,133},{6,134},{7,135},{8... | collective-permute-start | bytes 786440 | tf_op jit(solution)/shard_map/ppermute | solution.py:660
  36.6 13.7 %collective-permute-start.8 = (f32[2,16,16,128]{3,2,1,0:T(8,128)}, f32[2,16,16,128]{3,2,1,0:T(8,128)S(1)}, u32[]{:S(2)}, u32[]{:S(2)}) collective-permute-start(f32[2,16,16,128]{3,2,1,0:T(8,128)} %get-tuple-element.50), channel_id=1, source_target_pairs={{0,128},{1,129},{2,130},{3,131},{4,132},{5,133},{6,134},{7,135},{8... | collective-permute-start | bytes 786440 | tf_op jit(solution)/shard_map/ppermute | solution.py:660
  40.0 4.7 %copy-start.2 = (s32[2,48,16,1]{1,3,2,0:T(1,128)S(1)}, s32[2,48,16,1]{1,3,2,0:T(1,128)}, u32[]{:S(2)}) copy-start(s32[2,48,16,1]{1,3,2,0:T(1,128)} %param.5) | copy-start | bytes 18436
  43.4 11.6 %collective-permute-start.6 = (f32[2,16,16,128]{3,2,1,0:T(8,128)}, f32[2,16,16,128]{3,2,1,0:T(8,128)S(1)}, u32[]{:S(2)}, u32[]{:S(2)}) collective-permute-start(f32[2,16,16,128]{3,2,1,0:T(8,128)} %get-tuple-element.56), channel_id=1, source_target_pairs={{0,128},{1,129},{2,130},{3,131},{4,132},{5,133},{6,134},{7,135},{8... | collective-permute-start | bytes 786440 | tf_op jit(solution)/shard_map/ppermute | solution.py:660
